TPU v7x, 32 devices: a whole 2x2x4 slice. The times are simulated.
32 devices in a mesh: chan: 4 (over y, x), patch: 8 (over z, core).
Axes of the slice: x: 2, y: 2, z: 4, core: 2. Of those that a mesh axis runs over, the one named last changes fastest.
Arguments:
- sky_maps: float32 [64, 24576], P('chan', 'patch')
- mode_vectors: float32 [64, 8], replicated
- pixel_weight: float32 [24576], P('patch'), may hold values from 0.3 to 3
- neighbours: int32 [12, 16, 9], P('chan', 'patch'), may hold values from 0 to 8, as said below
- tile_counts: int32 [12, 16], P('chan', 'patch'), may hold values from 0 to 9, as said below
- pair_bins: int32 [9, 128, 128], replicated, may hold values from 0 to 8, as said below
Outputs:
- correlation: float32 [4, 8, 8, 64, 64], P('chan', 'patch')
- covariance: float32 [64, 64], replicated
Inputs may be any that keep to these rules, and one draw needn't show every extreme that they name: `neighbours`: for tile (A, B) the first tile_counts[A, B] entries are distinct offset codes o in ascending order, each naming the tile (A + o // 3 - 1, B + o % 3 - 1), which lies inside the grid and is observed; later entries mean nothing. An observed tile lists code 4 (itself); if a tile lists another, that one lists it back. `tile_counts`: 0 exactly for tiles that are not observed; some tile has 9. `pair_bins`: one table for each offset code, the same for every tile pair with that offset; the value 8 marks a pair beyond the last bin.
All inputs are finite; a program needn't handle non-finite values.
Results may differ from a plain program's by a relative error of at most 0.00075.
Values may be sent and summed in bfloat16 or wider, within the bound.
No kernel may reach another device: no remote copies, remote signals or barrier semaphores. Data moves between devices by JAX's collectives and lax.ppermute only.
A program may use at most 64 MiB of HBM per device.

v0:
```python
import math

import jax
import jax.numpy as jnp
from jax import lax
from jax.sharding import PartitionSpec as P

NCH = 64
MODES = 8
TILE = 128
NBIN = 8
NBR = 9
TA = 3
TB = 2


def padded(cells, sides, width):
    for axis, dim in sides:
        count = lax.axis_size(axis)
        ends = count - 1
        head = lax.slice_in_dim(cells, 0, width, axis=dim)
        tail = lax.slice_in_dim(cells, cells.shape[dim] - width, cells.shape[dim], axis=dim)
        cells = jnp.concatenate(
            [
                lax.ppermute(tail, axis, [(i, (i + 1) % count) for i in range(ends)]),
                cells,
                lax.ppermute(head, axis, [((i + 1) % count, i) for i in range(ends)]),
            ],
            axis=dim,
        )
    return cells


def orthonormal_basis(mode_vectors):
    columns = []
    for number in range(MODES):
        vector = mode_vectors[:, number]
        for earlier in columns:
            vector = vector - jnp.sum(earlier * vector) * earlier
        columns.append(vector / jnp.sqrt(jnp.sum(vector * vector) + 1e-06))
    return jnp.stack(columns, axis=1)


def projector(mode_vectors):
    basis = orthonormal_basis(mode_vectors)
    outer = jnp.dot(
        basis, basis.T, precision=lax.Precision.HIGHEST, preferred_element_type=jnp.float32
    )
    return jnp.eye(NCH, dtype=jnp.float32) - outer


def bin_masks(pair_bins):
    levels = jnp.arange(NBIN, dtype=jnp.int32)
    table = pair_bins[:, :, None, :] == levels[None, None, :, None]
    return table.astype(jnp.bfloat16).reshape(NBR, TILE, NBIN * TILE)


def taper_table():
    return 0.75 + 0.25 * jnp.cos(math.pi * jnp.arange(NBIN, dtype=jnp.float32) / NBIN)


def clean_block(project, gathered, weight_part):
    cleaned = jnp.dot(
        project, gathered, precision=lax.Precision.HIGHEST, preferred_element_type=jnp.float32
    )
    weighted = (cleaned * weight_part[None, :]).astype(jnp.bfloat16)
    return jnp.concatenate([weighted, weight_part.astype(jnp.bfloat16)[None, :]], axis=0)


def per_device(sky_maps, mode_vectors, pixel_weight, neighbours, tile_counts, pair_bins):
    chan_count = lax.axis_size("chan")
    chan_index = lax.axis_index("chan")
    local_channels = sky_maps.shape[0]
    project = projector(mode_vectors)
    block_pixels = TA * TB * TILE
    blocks = sky_maps.reshape(local_channels, chan_count, block_pixels)
    regrouped = lax.all_to_all(blocks, "chan", split_axis=1, concat_axis=0, tiled=True)
    gathered = regrouped.reshape(NCH, block_pixels)
    weight_part = lax.dynamic_slice_in_dim(pixel_weight, chan_index * block_pixels, block_pixels)
    own_tiles = clean_block(project, gathered, weight_part).reshape(NCH + 1, TA, TB, TILE)
    extended = padded(own_tiles, (("chan", 1), ("patch", 2)), 1)
    core_maps = own_tiles[:NCH]
    observed = tile_counts > 0
    masked = jnp.where(observed[None, :, :, None], core_maps, jnp.zeros((), jnp.bfloat16))
    partial_cov = jnp.einsum("cabq,dabq->cd", masked, core_maps, preferred_element_type=jnp.float32)
    pixel_total = jnp.sum(observed.astype(jnp.float32)) * TILE
    cov_sum, pixel_sum = lax.psum((partial_cov, pixel_total), ("chan", "patch"))
    covariance = cov_sum / pixel_sum
    mask_table = bin_masks(pair_bins)
    start_sums = jnp.zeros((NBIN, NCH + 1, NCH + 1), jnp.float32)
    centres = extended[:, 1 : TA + 1, 1 : TB + 1].reshape(NCH + 1, TA * TB, TILE)
    slot_live = jnp.arange(NBR, dtype=jnp.int32)[None, None, :] < tile_counts[:, :, None]
    pair_sums = start_sums
    for offset_code in range(NBR):
        row_shift = offset_code // 3
        col_shift = offset_code % 3
        partners = extended[:, row_shift : row_shift + TA, col_shift : col_shift + TB].reshape(
            NCH + 1, TA * TB, TILE
        )
        present = jnp.any((neighbours == offset_code) & slot_live, axis=-1)
        present = present.reshape(1, TA * TB, 1).astype(jnp.bfloat16)
        binned = jnp.einsum(
            "ctq,qk->ctk", centres, mask_table[offset_code], preferred_element_type=jnp.float32
        )
        binned = binned.astype(jnp.bfloat16) * present
        binned = binned.reshape(NCH + 1, TA * TB, NBIN, TILE)
        pair_sums = pair_sums + jnp.einsum(
            "ctbr,dtr->bcd", binned, partners, preferred_element_type=jnp.float32
        )
    spread = jnp.sqrt(jnp.diagonal(covariance) + 1e-06)
    norm_scale = spread[:, None] * spread[None, :]
    pair_weight = jnp.maximum(pair_sums[:, NCH, NCH], 1.0)
    correlation = taper_table()[:, None, None] * pair_sums[:, :NCH, :NCH]
    correlation = correlation / (pair_weight[:, None, None] * norm_scale[None])
    return (correlation[None, None], covariance)


def solution(mesh):
    return jax.shard_map(
        per_device,
        mesh=mesh,
        in_specs=(
            P("chan", "patch"),
            P(),
            P("patch"),
            P("chan", "patch", None),
            P("chan", "patch"),
            P(),
        ),
        out_specs=(P("chan", "patch", None, None, None), P()),
        check_vma=False,
    )
```

profile of v0, /device:TPU:1, one launch (start us, length us, event | category | flops | bytes accessed | tf_op | source)
XLA Modules:
  0.0 169.4 jit_solution(6443171478240522248)
XLA Ops:
  0.6 1.7 copy.129
  2.3 4.3 %all-to-all-start = ((f32[16,4,768]{2,0,1:T(8,128)}), f32[16,4,768]{2,0,1:T(8,128)S(1)}, u32[]{:S(2)}, u32[]{:S(2)}) async-start(f32[16,4,768]{2,0,1:T(8,128)} %bitcast.245), calls=%async_computation | async-start | bytes 393216 | tf_op jit(solution)/shard_map/all_to_all | solution.py:77
  6.6 0.8 copy.78
  7.3 1.4 convert_reduce_fusion
  8.7 1.3 multiply_reduce_fusion.28
  10.7 1.4 fusion.42
  12.1 2.3 %fusion.36 = (f32[]{:T(128)}, f32[]{:T(128)}, f32[]{:T(128)}, f32[]{:T(128)}, f32[]{:T(128)}, /*index=5*/f32[]{:T(128)}, f32[]{:T(128)}) fusion(f32[64,1]{0,1:T(1,128)S(1)} %get-tuple-element.86, f32[64,8]{0,1:T(8,128)} %param.7, f32[]{:T(128)} %get-tuple-element.85), kind=kLoop, calls=%fused_computation.94 | loop fusion | flops 1017 | bytes 2080 | tf_op jit(solution)/shard_map/reduce_sum | solution.py:39
  15.1 2.7 %multiply_reduce_fusion.26 = (f32[]{:T(128)}, f32[64]{0:T(128)S(1)}, f32[64]{0:T(128)S(1)}) fusion(f32[64,1]{0,1:T(1,128)S(1)} %get-tuple-element.86, f32[]{:T(128)} %get-tuple-element.21, f32[64,8]{0,1:T(8,128)} %param.7, f32[]{:T(128)S(6)} %sqrt.36, f32[]{:T(128)} %get-tuple-element.85), kind=kLoop, calls=%fused_computation.175 | loop fusion | flops 447 | bytes 1296 | tf_op jit(solution)/shard_map/reduce_sum | solution.py:39
  17.8 5.2 %multiply_reduce_fusion.6 = (f32[]{:T(128)}, f32[]{:T(128)}, f32[]{:T(128)}, f32[]{:T(128)}, f32[]{:T(128)}, /*index=5*/f32[]{:T(128)}, f32[64]{0:T(128)S(1)}, f...) fusion(f32[64]{0:T(128)S(1)} %get-tuple-element.84, f32[64]{0:T(128)S(1)} %get-tuple-element.83, ...), kind=kLoop, calls=%fused_computation.135 | loop fusion | flops 1530 | bytes 3376 | tf_op jit(solution)/shard_map/reduce_sum | solution.py:39
  23.7 4.5 %multiply_reduce_fusion.5 = (f32[]{:T(128)}, f32[]{:T(128)}, f32[]{:T(128)}, f32[]{:T(128)}, f32[]{:T(128)}, /*index=5*/f32[64]{0:T(128)S(1)}) fusion(f32[64]{0:T(128)S(1)} %get-tuple-element.81, f32[64]{0:T(128)S(1)} %get-tuple-element.84, f32[]{:T(128)} %get-tuple-element.40, f32[64]{0:T(128)S(1)} %get-tuple-element.80, f32[]{:T(128)} %get-tuple-element.41, ...), kind=kLoop, calls=%fused_computation.133 | loop fusion | flops 1467 | bytes 2096 | tf_op jit(solution)/shard_map/reduce_sum | solution.py:39
  28.2 1.8 %multiply_reduce_fusion.22 = (f32[]{:T(128)}, f32[64]{0:T(128)S(1)}) fusion(f32[64]{0:T(128)S(1)} %get-tuple-element.76, f32[]{:T(128)} %get-tuple-element.33, f32[64]{0:T(128)S(1)} %get-tuple-element.77, f32[64]{0:T(128)S(1)} %get-tuple-element.84, f32[]{:T(128)} %get-tuple-element.44), kind=kLoop, calls=%fused_computation.166 | loop fusion | flops 383 | bytes 1036 | tf_op jit(solution)/shard_map/reduce_sum | solution.py:40
  30.6 1.8 %multiply_reduce_fusion.19 = (f32[]{:T(128)}, f32[64]{0:T(128)S(1)}, f32[64]{0:T(128)S(1)}) fusion(f32[64]{0:T(128)S(1)} %get-tuple-element.76, f32[]{:T(128)} %get-tuple-element.32, f32[64]{0:T(128)S(1)} %get-tuple-element.78, f32[64]{0:T(128)S(1)} %get-tuple-element.84, f32[]{:T(128)} %get-tuple-element.43, f32[64]{0:T(128)S(1)} %get-tuple-element.75, ...), kind=kLoop, calls=%fused_computation.161 | loop fusion | flops 447 | bytes 1552 | tf_op jit(solution)/shard_map/reduce_sum | solution.py:39
  32.5 4.9 %multiply_reduce_fusion.4 = (f32[]{:T(128)}, f32[]{:T(128)}, f32[]{:T(128)}, f32[]{:T(128)}, f32[64]{0:T(128)S(1)}, /*index=5*/f32[64]{0:T(128)S(1)}, f32[64]{0:T(128)S(1)}) fusion(f32[64]{0:T(128)S(1)} %get-tuple-element.73, f32[64]{0:T(128)S(1)} %get-tuple-element.72, f32[]{:T(128)} %get-tuple-element.71, f32[64]{0:T(128)S(1)} %get-tuple-element.76, ...), kind=kLoop, calls=%fused_computation.131 | loop fusion | flops 1404 | bytes 2604 | tf_op jit(solution)/shard_map/reduce_sum | solution.py:39
  38.0 3.2 %multiply_reduce_fusion.3 = (f32[]{:T(128)}, f32[]{:T(128)}, f32[]{:T(128)}, f32[64]{0:T(128)S(1)}) fusion(f32[64]{0:T(128)S(1)} %get-tuple-element.70, f32[64]{0:T(128)S(1)} %get-tuple-element.73, f32[]{:T(128)} %get-tuple-element.36, f32[64]{0:T(128)S(1)} %get-tuple-element.69, f32[]{:T(128)} %get-tuple-element.37, f32[64]{0:T(128)S(1)} %get-tuple-element.68, ...), kind=kLoop, calls=%fused_computation.129 | loop fusion | flops 957 | bytes 1568 | tf_op jit(solution)/shard_map/reduce_sum | solution.py:39
  41.2 1.8 %multiply_reduce_fusion.13 = (f32[]{:T(128)}, f32[64]{0:T(128)S(1)}) fusion(f32[64]{0:T(128)S(1)} %get-tuple-element.67, f32[]{:T(128)} %get-tuple-element.28, f32[64]{0:T(128)S(1)} %get-tuple-element.68, f32[64]{0:T(128)S(1)} %get-tuple-element.73, f32[]{:T(128)} %get-tuple-element.38), kind=kLoop, calls=%fused_computation.148 | loop fusion | flops 383 | bytes 1036 | tf_op jit(solution)/shard_map/reduce_sum | solution.py:40
  43.7 1.9 %multiply_reduce_fusion.8 = (f32[]{:T(128)}, f32[64]{0:T(128)S(1)}, f32[64]{0:T(128)S(1)}) fusion(f32[64]{0:T(128)S(1)} %get-tuple-element.67, f32[]{:T(128)} %get-tuple-element.27, f32[64]{0:T(128)S(1)} %get-tuple-element.69, f32[64]{0:T(128)S(1)} %get-tuple-element.73, f32[]{:T(128)} %get-tuple-element.37, f32[64]{0:T(128)S(1)} %get-tuple-element.66, ...), kind=kLoop, calls=%fused_computation.139 | loop fusion | flops 447 | bytes 1552 | tf_op jit(solution)/shard_map/reduce_sum | solution.py:39
  45.6 2.6 %multiply_reduce_fusion.2 = (f32[]{:T(128)}, f32[]{:T(128)}, f32[64]{0:T(128)S(1)}) fusion(f32[64]{0:T(128)S(1)} %get-tuple-element.64, f32[64]{0:T(128)S(1)} %get-tuple-element.63, f32[]{:T(128)} %get-tuple-element.62, f32[64]{0:T(128)S(1)} %get-tuple-element.67, f32[]{:T(128)} %get-tuple-element.26, f32[64]{0:T(128)S(1)} %get-tuple-element.70, ...), kind=kLoop, calls=%fused_computation.127 | loop fusion | flops 638 | bytes 1556 | tf_op jit(solution)/shard_map/reduce_sum | solution.py:39
  48.8 1.9 %multiply_reduce_fusion.1 = (f32[]{:T(128)}, f32[64]{0:T(128)S(1)}) fusion(f32[64]{0:T(128)S(1)} %get-tuple-element.61, f32[64]{0:T(128)S(1)} %get-tuple-element.64, f32[]{:T(128)} %get-tuple-element.34, f32[]{:T(128)S(6)} %sqrt.41, f32[64]{0:T(128)S(1)} %get-tuple-element.63, f32[]{:T(128)} %get-tuple-element.62), kind=kLoop, calls=%fused_computation.125 | loop fusion | flops 447 | bytes 1040 | tf_op jit(solution)/shard_map/reduce_sum | solution.py:39
  50.7 1.9 %multiply_reduce_fusion = f32[]{:T(128)} fusion(f32[64]{0:T(128)S(1)} %get-tuple-element.60, f32[]{:T(128)} %get-tuple-element.59, f32[64]{0:T(128)S(1)} %get-tuple-element.61, f32[64]{0:T(128)S(1)} %get-tuple-element.64, f32[]{:T(128)} %get-tuple-element.34), kind=kLoop, calls=%fused_computation.123 | loop fusion | flops 383 | bytes 780 | tf_op jit(solution)/shard_map/reduce_sum | solution.py:40
  53.4 18.4 %subtract_divide_fusion = (f32[64,1]{0,1:T(1,128)S(1)}, f32[64,1]{0,1:T(1,128)S(1)}, f32[64,1]{0,1:T(1,128)S(1)}, f32[64,1]{0,1:T(1,128)S(1)}, f32[64,1]{0,1:T(1...) fusion(f32[64,1]{0,1:T(1,128)S(1)} %get-tuple-element.86, f32[]{:T(128)S(6)} %sqrt.42, f32[]{:T(128)} %get-tuple-element.59, ...), kind=kLoop, calls=%fused_computation.124 | loop fusion | flops 4032 | bytes 3980 | tf_op jit(solution)/shard_map/div | solution.py:40
  72.0 0.7 iota_compare_fusion
  72.8 0.8 fusion.44
  73.6 0.6 and_reduce_fusion.8
  77.9 3.4 %collective-permute-start = (bf16[65,1,2,128]{3,2,1,0:T(2,128)(2,1)S(1)}, bf16[65,1,2,128]{3,2,1,0:T(2,128)(2,1)S(1)}, u32[]{:S(2)}, u32[]{:S(2)}) collective-permute-start(bf16[65,1,2,128]{3,2,1,0:T(2,128)(2,1)S(1)} %get-tuple-element.106), channel_id=1, source_target_pairs={{0,8},{8,16},{16,24},{1,9},{9,17},{17,25},{2,10},{10,18},{18,26},{... | collective-permute-start | bytes 99848 | tf_op jit(solution)/shard_map/ppermute | solution.py:25
  81.3 1.3 collective-permute-start.1
  82.8 42.1 %all-reduce = (f32[64,64]{1,0:T(8,128)S(1)}, f32[]{:T(128)}) all-reduce(f32[64,64]{1,0:T(8,128)S(1)} %fusion.30, f32[]{:T(128)S(6)} %mul.782), channel_id=1, replica_groups=mesh['chan'=4,'patch'=8] {'chan','patch'}, use_global_device_ids=true, to_apply=%region_45.46 | all-reduce | flops 4097 | bytes 32776 | tf_op jit(solution)/shard_map/psum | solution.py:87
  124.9 0.7 broadcast_divide_fusion
  125.5 0.8 gather_fusion
  126.4 0.4 fusion.6
  126.8 0.4 fusion.3
  127.2 1.3 fusion.1
  128.5 1.3 fusion.7
  129.8 1.4 fusion.5
  131.2 1.3 fusion.2
  132.6 1.3 fusion.8
  133.9 1.3 fusion.4
  135.2 1.3 fusion
  136.5 0.7 broadcast_multiply_fusion
  137.2 1.5 reshape.240
  138.8 1.0 fusion.46
  139.8 4.7 %collective-permute-start.2 = (bf16[65,5,1,128]{3,2,1,0:T(2,128)(2,1)}, bf16[65,5,1,128]{3,2,1,0:T(2,128)(2,1)S(1)}, u32[]{:S(2)}, u32[]{:S(2)}) collective-permute-start(bf16[65,5,1,128]{3,2,1,0:T(2,128)(2,1)} %get-tuple-element.102), channel_id=1, source_target_pairs={{0,1},{1,2},{2,3},{3,4},{4,5},{5,6},{6,7},{8,9},{9,10},{10,11},{11... | collective-permute-start | bytes 249608 | tf_op jit(solution)/shard_map/ppermute | solution.py:25
  144.5 1.2 convolution_bitcast_fusion.4
  145.7 1.3 reshape.244
  147.0 1.3 reshape.239
  148.3 1.2 reshape.235
  149.5 1.3 reshape.246
  150.8 0.4 reshape.242
  151.1 1.5 reshape.237
  152.6 1.5 reshape.248
  154.1 1.5 reshape.233
  155.6 1.9 %collective-permute-start.3 = (bf16[65,5,1,128]{3,2,1,0:T(2,128)(2,1)}, bf16[65,5,1,128]{3,2,1,0:T(2,128)(2,1)S(1)}, u32[]{:S(2)}, u32[]{:S(2)}) collective-permute-start(bf16[65,5,1,128]{3,2,1,0:T(2,128)(2,1)} %get-tuple-element.103), channel_id=1, source_target_pairs={{1,0},{2,1},{3,2},{4,3},{5,4},{6,5},{7,6},{9,8},{10,9},{11,10},{12... | collective-permute-start | bytes 249608 | tf_op jit(solution)/shard_map/ppermute | solution.py:27
  157.5 0.8 pad_maximum_fusion.12
  158.4 4.1 %collective-permute-done.3 = bf16[65,5,1,128]{3,2,1,0:T(2,128)(2,1)S(1)} collective-permute-done((bf16[65,5,1,128]{3,2,1,0:T(2,128)(2,1)}, bf16[65,5,1,128]{3,2,1,0:T(2,128)(2,1)S(1)}, u32[]{:S(2)}, u32[]{:S(2)}) %collective-permute-start.3) | collective-permute-done | bytes 83232 | tf_op jit(solution)/shard_map/ppermute | solution.py:27
  162.5 0.8 pad_maximum_fusion.10
  163.4 0.5 convolution_bitcast_fusion.2
  163.9 0.5 copy-done.3
  164.4 0.5 convolution_bitcast_fusion.5
  164.9 0.5 convolution_bitcast_fusion.7
  165.6 0.5 convolution_bitcast_fusion.1
  166.1 0.5 convolution_bitcast_fusion.3
  166.6 0.5 convolution_bitcast_fusion.6
  167.1 0.5 convolution_bitcast_fusion
  167.7 0.6 fusion.17
  168.6 0.8 copy.96
  (83 shorter events, 4.2 us)
Async XLA Ops:
  0.6 71.4 %copy-start.9 = (s32[9,128,128]{2,1,0:T(8,128)S(1)}, s32[9,128,128]{2,1,0:T(8,128)}, u32[]{:S(2)}) copy-start(s32[9,128,128]{2,1,0:T(8,128)} %param.11) | copy-start | bytes 1769476
  2.3 75.1 %all-to-all-start = ((f32[16,4,768]{2,0,1:T(8,128)}), f32[16,4,768]{2,0,1:T(8,128)S(1)}, u32[]{:S(2)}, u32[]{:S(2)}) async-start(f32[16,4,768]{2,0,1:T(8,128)} %bitcast.245), calls=%async_computation | async-start | bytes 393216 | tf_op jit(solution)/shard_map/all_to_all | solution.py:77
  72.7 0.9 copy-start.11
  77.9 60.7 %collective-permute-start = (bf16[65,1,2,128]{3,2,1,0:T(2,128)(2,1)S(1)}, bf16[65,1,2,128]{3,2,1,0:T(2,128)(2,1)S(1)}, u32[]{:S(2)}, u32[]{:S(2)}) collective-permute-start(bf16[65,1,2,128]{3,2,1,0:T(2,128)(2,1)S(1)} %get-tuple-element.106), channel_id=1, source_target_pairs={{0,8},{8,16},{16,24},{1,9},{9,17},{17,25},{2,10},{10,18},{18,26},{... | collective-permute-start | bytes 99848 | tf_op jit(solution)/shard_map/ppermute | solution.py:25
  81.3 57.4 %collective-permute-start.1 = (bf16[65,1,2,128]{3,2,1,0:T(2,128)(2,1)S(1)}, bf16[65,1,2,128]{3,2,1,0:T(2,128)(2,1)S(1)}, u32[]{:S(2)}, u32[]{:S(2)}) collective-permute-start(bf16[65,1,2,128]{3,2,1,0:T(2,128)(2,1)S(1)} %get-tuple-element.107), channel_id=1, source_target_pairs={{8,0},{16,8},{24,16},{9,1},{17,9},{25,17},{10,2},{18,10},{26,18},{... | collective-permute-start | bytes 99848 | tf_op jit(solution)/shard_map/ppermute | solution.py:27
  125.5 1.7 copy-start
  139.8 17.7 %collective-permute-start.2 = (bf16[65,5,1,128]{3,2,1,0:T(2,128)(2,1)}, bf16[65,5,1,128]{3,2,1,0:T(2,128)(2,1)S(1)}, u32[]{:S(2)}, u32[]{:S(2)}) collective-permute-start(bf16[65,5,1,128]{3,2,1,0:T(2,128)(2,1)} %get-tuple-element.102), channel_id=1, source_target_pairs={{0,1},{1,2},{2,3},{3,4},{4,5},{5,6},{6,7},{8,9},{9,10},{10,11},{11... | collective-permute-start | bytes 249608 | tf_op jit(solution)/shard_map/ppermute | solution.py:25
  147.0 1.3 copy-start.5
  148.2 1.3 copy-start.6
  149.5 1.3 copy-start.7
  155.6 6.9 %collective-permute-start.3 = (bf16[65,5,1,128]{3,2,1,0:T(2,128)(2,1)}, bf16[65,5,1,128]{3,2,1,0:T(2,128)(2,1)S(1)}, u32[]{:S(2)}, u32[]{:S(2)}) collective-permute-start(bf16[65,5,1,128]{3,2,1,0:T(2,128)(2,1)} %get-tuple-element.103), channel_id=1, source_target_pairs={{1,0},{2,1},{3,2},{4,3},{5,4},{6,5},{7,6},{9,8},{10,9},{11,10},{12... | collective-permute-start | bytes 249608 | tf_op jit(solution)/shard_map/ppermute | solution.py:27
  158.3 5.1 %copy-start.4 = (bf16[65,6,8,128]{3,2,0,1:T(8,128)(2,1)S(1)}, bf16[65,6,8,128]{3,2,0,1:T(8,128)(2,1)}, u32[]{:S(2)}) copy-start(bf16[65,6,8,128]{3,2,0,1:T(8,128)(2,1)} %reshape.244) | copy-start | bytes 2396164
  163.2 1.1 copy-start.3
  163.4 1.5 copy-start.2
  164.4 1.2 copy-start.1
  166.6 1.0 copy-start.8
  167.7 0.8 copy-start.10
where the time goes:
time: 171 us; the launch traced here: 169 us
  other arithmetic  64.5 us (38%)
  blocking collectives  42.1 us (25%)
  local copies, waits for them, and re-layouts  19.7 us (12%)
  matrix products  16.2 us (9%)
  starting transfers between devices  15.5 us (9%)
  between operations  7.3 us (4%)
  waiting for transfers between devices  4.07 us (2%)
    psum x1, blocking collectives, per_device(): cov_sum, pixel_sum = lax.psum((partial_cov, pixel_total), ('chan', 'patch'))  42.1 us
    reduce_sum x11, other arithmetic, orthonormal_basis(): vector = vector - jnp.sum(earlier * vector) * earlier  32.4 us
    div x1, other arithmetic, orthonormal_basis(): columns.append(vector / jnp.sqrt(jnp.sum(vector * vector) + 1e-06))  18.4 us
    reshape x9, local copies, waits for them, and re-layouts, per_device(): binned = binned.reshape(NCH + 1, TA * TB, NBIN, TILE)  11.3 us
    dot_general x9, matrix products, per_device(): jnp.einsum('ctq,qk->ctk', centres, mask_table[offset_code], preferred_ele...  10.1 us
    ppermute x2, starting transfers between devices, padded(): lax.ppermute(tail, axis, [(i, (i + 1) % count) for i in range(ends)])  8.05 us
    reduce_sum x4, other arithmetic, orthonormal_basis(): columns.append(vector / jnp.sqrt(jnp.sum(vector * vector) + 1e-06))  6.83 us
    dot_general x9, matrix products, per_device(): jnp.einsum('ctbr,dtr->bcd', binned, partners, preferred_element_type=jnp....  5.33 us
  transfers between devices with their start and end apart: 5, of which 1 were waited for; matrix products, arithmetic and copies ran while one was open for 53% of the time, Pallas kernels for 0%

commit v1 on v0

v1 whole, which is shorter than its diff:
```python
import math

import jax
import jax.numpy as jnp
from jax import lax
from jax.experimental import pallas as pl
from jax.experimental.pallas import tpu as pltpu
from jax.sharding import PartitionSpec as P

NCH = 64
MODES = 8
TILE = 128
NBIN = 8
NBR = 9
TA = 3
TB = 2
EXT = TA + 2
WROW = EXT * NCH
COLH = WROW + 16
CHUNK = 512

F32 = jnp.float32
BF16 = jnp.bfloat16
ROWS_BY_ROWS = (((1,), (1,)), ((), ()))
VMEM = pl.BlockSpec(memory_space=pltpu.VMEM)
SMEM = pl.BlockSpec(memory_space=pltpu.SMEM)


def pieces(x):
    high = x.astype(BF16)
    rest = x - high.astype(F32)
    middle = rest.astype(BF16)
    low = (rest - middle.astype(F32)).astype(BF16)
    return high, middle, low


def projector_kernel(local_channels, modes_ref, project_ref):
    vectors = modes_ref[...].T
    lane = lax.broadcasted_iota(jnp.int32, (NCH, MODES), 1)
    for number in range(MODES):
        column = jnp.sum(jnp.where(lane == number, vectors, 0.0), axis=1, keepdims=True)
        inner = jnp.sum(column * vectors, axis=0, keepdims=True)
        square = jnp.sum(column * column, axis=0, keepdims=True)
        scale = 1.0 / jnp.sqrt(square + 1e-06)
        unit = column * scale
        reduced = vectors - unit * (inner * scale)
        vectors = jnp.where(lane == number, unit, jnp.where(lane > number, reduced, vectors))
    channel = lax.broadcasted_iota(jnp.int32, (NCH, NCH), 0)
    row = lax.broadcasted_iota(jnp.int32, (NCH, NCH), 1)
    holder = lax.axis_index("chan") ^ (row // local_channels)
    source = holder * local_channels + row % local_channels
    order = jnp.where(channel == source, 1.0, 0.0)
    ordered = lax.dot_general(
        order,
        vectors,
        (((0,), (0,)), ((), ())),
        precision=lax.Precision.HIGHEST,
        preferred_element_type=F32,
    )
    outer = lax.dot_general(
        vectors,
        ordered,
        ROWS_BY_ROWS,
        precision=lax.Precision.HIGHEST,
        preferred_element_type=F32,
    )
    high, middle, low = pieces(order - outer)
    none = jnp.zeros((NCH, NCH), BF16)
    project_ref[0:NCH, :] = jnp.concatenate([high, high, high], axis=1)
    project_ref[NCH : 2 * NCH, :] = jnp.concatenate([middle, middle, none], axis=1)
    project_ref[2 * NCH : 3 * NCH, :] = jnp.concatenate([low, none, none], axis=1)


def mask_kernel(bins_ref, mask_ref):
    for code in range(NBR):
        table = bins_ref[code]
        for level in range(NBIN):
            mask_ref[code, :, level * TILE : (level + 1) * TILE] = jnp.where(
                table == level, 1.0, 0.0
            ).astype(BF16)


def clean_kernel(block_count, *refs):
    counts_ref, project_ref, weight_ref = refs[:3]
    block_refs = refs[3 : 3 + block_count]
    cols_ref, near_ref, far_ref, cov_ref = refs[3 + block_count : 7 + block_count]
    padded_ref, masked_ref, weights_ref = refs[7 + block_count :]
    pixels = weight_ref.shape[1]
    row_pixels = TB * TILE
    region_pixels = TA * row_pixels
    chan_index = lax.axis_index("chan")
    side = lax.axis_index("patch") % 2

    for edge in (0, row_pixels + pixels):
        padded_ref[:, edge : edge + row_pixels] = jnp.zeros((NCH, row_pixels), BF16)
        weights_ref[:, edge : edge + row_pixels] = jnp.zeros((1, row_pixels), F32)
    weights_ref[:, row_pixels : row_pixels + pixels] = weight_ref[...]

    project = project_ref[...]
    observed_tiles = jnp.zeros((), jnp.int32)
    for begin in range(0, pixels, CHUNK):
        maps = jnp.concatenate([ref[:, begin : begin + CHUNK] for ref in block_refs], axis=0)
        split = jnp.concatenate(pieces(maps), axis=0)
        product = jnp.dot(project, split, preferred_element_type=F32)
        cleaned = (product[2 * NCH :] + product[NCH : 2 * NCH]) + product[:NCH]
        weighted = (cleaned * weight_ref[:, begin : begin + CHUNK]).astype(BF16)
        padded_ref[:, row_pixels + begin : row_pixels + begin + CHUNK] = weighted
        for place in range(begin, begin + CHUNK, TILE):
            tile = place // TILE
            holder = (tile // (TA * TB)) ^ chan_index
            observed = counts_ref[holder * (TA * TB) + tile % (TA * TB)] > 0
            observed_tiles = observed_tiles + observed.astype(jnp.int32)
            part = weighted[:, place - begin : place - begin + TILE]
            masked_ref[:, place : place + TILE] = jnp.where(observed, part, jnp.zeros_like(part))
    covariance = lax.dot_general(
        masked_ref[...],
        padded_ref[:, row_pixels : row_pixels + pixels],
        ROWS_BY_ROWS,
        preferred_element_type=F32,
    )
    total = jnp.full((NCH, NCH), (observed_tiles * TILE).astype(F32))
    cov_ref[...] = jnp.concatenate([covariance, total], axis=1)

    rows = lax.broadcasted_iota(jnp.int32, (16, TILE), 0)
    for col in range(TB):
        weight_rows = jnp.zeros((16, TILE), F32)
        for row in range(EXT):
            start = chan_index * region_pixels + row * row_pixels + col * TILE
            at = pl.ds(pl.multiple_of(start, TILE), TILE)
            cols_ref[col, row * NCH : (row + 1) * NCH, :] = padded_ref[:, at]
            weight_rows = jnp.where(rows == row, weights_ref[:, at], weight_rows)
        cols_ref[col, WROW:COLH, :] = weight_rows.astype(BF16)
    near_ref[...] = cols_ref[1 - side]
    far_ref[...] = cols_ref[side]


def add_pairs(code, live, centres, partners, mask_ref):
    row_shift = code // 3
    own = slice(NCH, (TA + 1) * NCH)
    left = jnp.concatenate(
        [column[own] for column in centres] + [column[WROW:] for column in centres], axis=0
    )
    binned = jnp.dot(left, mask_ref[code], preferred_element_type=F32).astype(BF16)
    rows = lax.broadcasted_iota(jnp.int32, (16, TILE), 0)
    right = []
    weight_sums = [jnp.zeros((16, TILE), F32) for _ in range(NBIN)]
    for col in range(TB):
        partner_weights = partners[col][WROW:].astype(F32)
        shifted = jnp.zeros((16, TILE), F32)
        for row in range(TA):
            present = live(row, col, code)
            place = row + row_shift
            tile = partners[col][place * NCH : (place + 1) * NCH]
            right.append(jnp.where(present, tile, jnp.zeros_like(tile)))
            weight = jnp.where(present, partner_weights[place : place + 1], 0.0)
            shifted = jnp.where(rows == row + 1, weight, shifted)
        first = TA * TB * NCH + col * 16
        for level in range(NBIN):
            lanes = slice(level * TILE, (level + 1) * TILE)
            weight_sums[level] += binned[first : first + 16, lanes].astype(F32) * shifted
    right = jnp.concatenate(right, axis=1)
    left = jnp.concatenate(
        [
            jnp.concatenate(
                [
                    binned[at * NCH : (at + 1) * NCH, level * TILE : (level + 1) * TILE]
                    for at in range(TA * TB)
                ],
                axis=1,
            )
            for level in range(NBIN)
        ],
        axis=0,
    )
    sums = lax.dot_general(left, right, ROWS_BY_ROWS, preferred_element_type=F32)
    return sums, weight_sums


def liveness(present_ref):
    return lambda row, col, code: present_ref[(row * TB + col) * NBR + code] > 0


def inner_kernel(present_ref, cols_ref, mask_ref, sums_ref, weight_sums_ref):
    live = liveness(present_ref)
    columns = [cols_ref[col] for col in range(TB)]
    for number, code in enumerate((1, 4, 7)):
        sums, weight_sums = add_pairs(code, live, columns, columns, mask_ref)
        if number:
            sums_ref[...] += sums
        else:
            sums_ref[...] = sums
        for level in range(NBIN):
            if number:
                weight_sums_ref[level] += weight_sums[level]
            else:
                weight_sums_ref[level] = weight_sums[level]


def outer_kernel(piece_count, *refs):
    present_ref, cols_ref, near_ref, far_ref, mask_ref, sums_in_ref, weight_in_ref = refs[:7]
    piece_refs = refs[7 : 7 + piece_count]
    corr_ref, cov_ref, sums_ref, weight_sums_ref = refs[7 + piece_count :]
    live = liveness(present_ref)
    even = lax.axis_index("patch") % 2 == 0
    columns = [cols_ref[col] for col in range(TB)]
    near, far = near_ref[...], far_ref[...]
    before = jnp.where(even, far, near)
    after = jnp.where(even, near, far)
    sums_ref[...] = sums_in_ref[...]
    weight_sums_ref[...] = weight_in_ref[...]
    for code in (0, 3, 6, 2, 5, 8):
        partners = [before, columns[0]] if code % 3 == 0 else [columns[1], after]
        sums, weight_sums = add_pairs(code, live, columns, partners, mask_ref)
        sums_ref[...] += sums
        for level in range(NBIN):
            weight_sums_ref[level] += weight_sums[level]

    whole = piece_refs[0][...]
    for ref in piece_refs[1:]:
        whole = whole + ref[...]
    covariance = whole[:, :NCH] / whole[:, NCH:]
    cov_ref[...] = covariance
    channel = lax.broadcasted_iota(jnp.int32, (NCH, NCH), 0)
    other = lax.broadcasted_iota(jnp.int32, (NCH, NCH), 1)
    diagonal = jnp.where(channel == other, covariance, 0.0)
    spread_down = jnp.sqrt(jnp.sum(diagonal, axis=1, keepdims=True) + 1e-06)
    spread_across = jnp.sqrt(jnp.sum(diagonal, axis=0, keepdims=True) + 1e-06)
    norm_scale = spread_down * spread_across
    for level in range(NBIN):
        taper = 0.75 + 0.25 * math.cos(math.pi * level / NBIN)
        total = jnp.sum(
            jnp.sum(weight_sums_ref[level], axis=1, keepdims=True), axis=0, keepdims=True
        )
        pair_weight = jnp.maximum(total, 1.0)
        sums = sums_ref[level * NCH : (level + 1) * NCH]
        corr_ref[level] = (taper * sums) / (pair_weight * norm_scale)


def run(kernel, outs, smem, args, scratch=()):
    return pl.pallas_call(
        kernel,
        out_shape=outs,
        in_specs=[SMEM] * smem + [VMEM] * (len(args) - smem),
        out_specs=jax.tree.map(lambda _: VMEM, outs),
        scratch_shapes=list(scratch),
        compiler_params=pltpu.CompilerParams(vmem_limit_bytes=24 * 2**20),
    )(*args)


def exchange(x, axis, step):
    count = lax.axis_size(axis)
    return lax.ppermute(x, axis, [(i, i ^ step) for i in range(count)])


def per_device(sky_maps, mode_vectors, pixel_weight, neighbours, tile_counts, pair_bins):
    shape = jax.ShapeDtypeStruct
    chan_count = lax.axis_size("chan")
    patch_count = lax.axis_size("patch")
    local_channels, pixels = sky_maps.shape

    blocks = [sky_maps] + [exchange(sky_maps, "chan", step) for step in range(1, chan_count)]
    counts = [tile_counts] + [exchange(tile_counts, "chan", step) for step in range(1, chan_count)]
    counts = jnp.concatenate([part.reshape(TA * TB) for part in counts])
    if local_channels % 16:
        blocks = [jnp.concatenate(blocks, axis=0)]

    project = run(
        lambda *refs: projector_kernel(local_channels, *refs),
        shape((3 * NCH, 3 * NCH), BF16),
        0,
        [mode_vectors.T],
    )
    mask = run(mask_kernel, shape((NBR, TILE, NBIN * TILE), BF16), 0, [pair_bins])
    codes = jnp.arange(NBR, dtype=jnp.int32)
    slot_live = codes[None, None, :] < tile_counts[:, :, None]
    matches = (neighbours[:, :, :, None] == codes) & slot_live[:, :, :, None]
    present = jnp.any(matches, axis=2).astype(jnp.int32).reshape(TA * TB * NBR)

    column = shape((COLH, TILE), BF16)
    cols, near, far, piece = run(
        lambda *refs: clean_kernel(len(blocks), *refs),
        (shape((TB, COLH, TILE), BF16), column, column, shape((NCH, 2 * NCH), F32)),
        1,
        [counts, project, pixel_weight.reshape(1, pixels)] + blocks,
        scratch=[
            pltpu.VMEM((NCH, pixels + 2 * TB * TILE), BF16),
            pltpu.VMEM((NCH, pixels), BF16),
            pltpu.VMEM((1, pixels + 2 * TB * TILE), F32),
        ],
    )

    near = exchange(near, "patch", 1)
    far_pairs = [(i, i + 1) for i in range(1, patch_count - 1, 2)]
    far = lax.ppermute(far, "patch", far_pairs + [(j, i) for i, j in far_pairs])

    piece = piece + exchange(piece, "patch", 1)
    stride = 2
    while True:
        group = min(4, patch_count // stride)
        parts = [piece] + [exchange(piece, "patch", stride * k) for k in range(1, group)]
        stride *= group
        if stride >= patch_count:
            break
        piece = sum(parts[1:], parts[0])

    sums_shape = shape((NBIN * NCH, NCH), F32)
    weight_shape = shape((NBIN, 16, TILE), F32)
    sums, weight_sums = run(inner_kernel, (sums_shape, weight_shape), 1, [present, cols, mask])
    correlation, covariance = run(
        lambda *refs: outer_kernel(len(parts), *refs),
        (shape((NBIN, NCH, NCH), F32), shape((NCH, NCH), F32)),
        1,
        [present, cols, near, far, mask, sums, weight_sums] + parts,
        scratch=[pltpu.VMEM((NBIN * NCH, NCH), F32), pltpu.VMEM((NBIN, 16, TILE), F32)],
    )
    return (correlation[None, None], covariance)


def solution(mesh):
    return jax.shard_map(
        per_device,
        mesh=mesh,
        in_specs=(
            P("chan", "patch"),
            P(),
            P("patch"),
            P("chan", "patch", None),
            P("chan", "patch"),
            P(),
        ),
        out_specs=(P("chan", "patch", None, None, None), P()),
        check_vma=False,
    )
```

time: 171 us -> 38.7 us (0.23)
  the two profiles are of different devices: /device:TPU:1 before, /device:TPU:0 now
where the time goes in v1:
time: 38.7 us; the launch traced here: 38.1 us
  starting transfers between devices  15.2 us (39%)
  Pallas kernels  9.48 us (24%)
  waiting for transfers between devices  6.17 us (16%)
  local copies, waits for them, and re-layouts  5.66 us (15%)
  other arithmetic  0.89 us (2%)
  between operations  0.74 us (2%)
    ppermute x11, starting transfers between devices, exchange(): return lax.ppermute(x, axis, [(i, i ^ step) for i in range(count)])  14.5 us
    pallas_call x5, Pallas kernels, run(): pl.pallas_call(kernel, out_shape=outs, in_specs=[SMEM] * smem + [VMEM] *...  9.48 us
    ppermute x11, waiting for transfers between devices, exchange(): return lax.ppermute(x, axis, [(i, i ^ step) for i in range(count)])  6.16 us
    unnamed x10, local copies, waits for them, and re-layouts  4.96 us
  transfers between devices with their start and end apart: 12, of which 3 were waited for; matrix products, arithmetic and copies ran while one was open for 8% of the time, Pallas kernels for 11%

profile of v1, /device:TPU:0, one launch (start us, length us, event | category | flops | bytes accessed | tf_op | source)
XLA Modules:
  0.0 38.1 jit_solution(200180538938321706)
XLA Ops:
  0.6 3.0 %collective-permute-start.4 = (f32[16,3072]{1,0:T(8,128)}, f32[16,3072]{1,0:T(8,128)S(1)}, u32[]{:S(2)}, u32[]{:S(2)}) collective-permute-start(f32[16,3072]{1,0:T(8,128)} %refs_3_.1), channel_id=1, source_target_pairs={{0,16},{8,24},{16,0},{24,8},{1,17},{9,25},{17,1},{25,9},{2,18},{10... | collective-permute-start | bytes 589832 | tf_op jit(solution)/shard_map/ppermute | solution.py:252
  3.7 1.5 %collective-permute-start.3 = (f32[16,3072]{1,0:T(8,128)}, f32[16,3072]{1,0:T(8,128)S(1)}, u32[]{:S(2)}, u32[]{:S(2)}) collective-permute-start(f32[16,3072]{1,0:T(8,128)} %refs_3_.1), channel_id=1, source_target_pairs={{0,8},{8,0},{16,24},{24,16},{1,9},{9,1},{17,25},{25,17},{2,10},{10... | collective-permute-start | bytes 589832 | tf_op jit(solution)/shard_map/ppermute | solution.py:252
  5.2 0.1 collective-permute-start.5
  5.2 1.9 %collective-permute-start = (s32[3,2]{0,1:T(2,128)}, s32[3,2]{0,1:T(2,128)S(1)}, u32[]{:S(2)}, u32[]{:S(2)}) collective-permute-start(s32[3,2]{0,1:T(2,128)} %param.10), channel_id=1, source_target_pairs={{0,8},{8,0},{16,24},{24,16},{1,9},{9,1},{17,25},{25,17},{2,10},{10... | collective-permute-start | bytes 80 | tf_op jit(solution)/shard_map/ppermute | solution.py:252
  7.1 1.5 %collective-permute-start.2 = (s32[3,2]{0,1:T(2,128)}, s32[3,2]{0,1:T(2,128)S(1)}, u32[]{:S(2)}, u32[]{:S(2)}) collective-permute-start(s32[3,2]{0,1:T(2,128)} %param.10), channel_id=1, source_target_pairs={{0,24},{8,16},{16,8},{24,0},{1,25},{9,17},{17,9},{25,1},{2,26},{10... | collective-permute-start | bytes 80 | tf_op jit(solution)/shard_map/ppermute | solution.py:252
  8.6 0.8 %copy.20 = s32[3,2]{1,0:T(4,128)S(1)} copy(s32[3,2]{0,1:T(2,128)} %param.10) | data formatting | bytes 48 | tf_op args[4]
  9.4 0.1 reshape.28
  9.5 0.0 copy-start.3
  9.5 0.7 %copy-done.3 = f32[64,8]{0,1:T(8,128)S(1)} copy-done((f32[64,8]{0,1:T(8,128)S(1)}, f32[64,8]{0,1:T(8,128)}, u32[]{:S(2)}) %copy-start.3) | copy-done | bytes 2072
  10.2 1.4 %shard_map.77.refs_1_ = bf16[192,192]{1,0:T(8,128)(2,1)S(1)} custom-call(f32[8,64]{1,0:T(8,128)S(1)} %bitcast.4), custom_call_target="tpu_custom_call" | custom-call | tf_op jit(solution)/shard_map/pallas_call | solution.py:240
  11.6 2.9 %collective-permute-done = s32[3,2]{0,1:T(2,128)S(1)} collective-permute-done((s32[3,2]{0,1:T(2,128)}, s32[3,2]{0,1:T(2,128)S(1)}, u32[]{:S(2)}, u32[]{:S(2)}) %collective-permute-start) | collective-permute-done | bytes 56 | tf_op jit(solution)/shard_map/ppermute | solution.py:252
  14.5 0.4 collective-permute-start.1
  14.8 0.1 copy.21
  14.9 0.1 reshape.29
  15.0 0.0 collective-permute-done.2
  15.0 0.1 copy.23
  15.1 0.1 reshape.31
  15.2 3.1 %collective-permute-done.1 = s32[3,2]{0,1:T(2,128)S(1)} collective-permute-done((s32[3,2]{0,1:T(2,128)}, s32[3,2]{0,1:T(2,128)S(1)}, u32[]{:S(2)}, u32[]{:S(2)}) %collective-permute-start.1) | collective-permute-done | bytes 56 | tf_op jit(solution)/shard_map/ppermute | solution.py:252
  18.3 0.1 copy.22
  18.3 0.1 reshape.30
  18.4 0.1 pad_add_fusion.refs_0_
  18.5 0.0 collective-permute-done.4.refs_5_
  18.5 0.0 collective-permute-done.3.refs_4_
  18.5 0.0 collective-permute-done.5.refs_6_
  18.5 0.0 copy-start.1
  18.5 0.9 %copy-done.1 = f32[16,3072]{1,0:T(8,128)S(1)} copy-done((f32[16,3072]{1,0:T(8,128)S(1)}, f32[16,3072]{1,0:T(8,128)}, u32[]{:S(2)}) %copy-start.1) | copy-done | bytes 196632
  19.5 0.0 copy-start.2
  19.5 0.7 %copy-done.2 = f32[3072]{0:T(1024)S(1)} copy-done((f32[3072]{0:T(1024)S(1)}, f32[3072]{0:T(1024)}, u32[]{:S(2)}) %copy-start.2) | copy-done | bytes 12312
  20.2 1.3 %shard_map.78 = (bf16[2,336,128]{2,1,0:T(8,128)(2,1)S(1)}, bf16[336,128]{1,0:T(8,128)(2,1)S(1)}, bf16[336,128]{1,0:T(8,128)(2,1)S(1)}, f32[64,128]{1,0:T(8,128)S(1)}) custom-call(s32[24]{0:T(128)S(1)} %pad_add_fusion.refs_0_, bf16[192,192]{1,0:T(8,128)(2,1)S(1)} %shard_map.77.refs_1_, f32[1,3072]{1,0:T(1,128)S(1)} %bitcast.3, f32[16,3072]{1,0:T(8,128)S(1)} %copy-done.1, ...), custom_call_target="tpu_custom_call" | custom-call | tf_op jit(solution)/shard_map/pallas_call | solution.py:240
  21.5 0.1 collective-permute-start.8
  21.5 0.7 %iota_compare_fusion.1 = pred[3,2,9]{0,2,1:T(8,128)(4,1)S(1)} fusion(s32[3,2]{0,1:T(2,128)} %param.10), kind=kLoop, calls=%fused_computation.3 | loop fusion | flops 54 | bytes 78 | tf_op jit(solution)/shard_map/lt | solution.py:275
  22.2 0.8 %copy.18 = s32[3,2,9]{0,2,1:T(8,128)S(1)} copy(s32[3,2,9]{2,1,0:T(2,128)} %param.9) | data formatting | bytes 432 | tf_op args[3]
  23.0 0.5 %collective-permute-start.6 = (bf16[336,128]{1,0:T(8,128)(2,1)S(1)}, bf16[336,128]{1,0:T(8,128)(2,1)S(1)}, u32[]{:S(2)}, u32[]{:S(2)}) collective-permute-start(bf16[336,128]{1,0:T(8,128)(2,1)S(1)} %get-tuple-element.11), channel_id=1, source_target_pairs={{0,1},{1,0},{2,3},{3,2},{4,5},{5,4},{6,7},{7,6},{8,9},{9,8},{10,11... | collective-permute-start | bytes 258056 | tf_op jit(solution)/shard_map/ppermute | solution.py:252
  23.5 0.7 %collective-permute-start.7 = (bf16[336,128]{1,0:T(8,128)(2,1)S(1)}, bf16[336,128]{1,0:T(8,128)(2,1)S(1)}, u32[]{:S(2)}, u32[]{:S(2)}) collective-permute-start(bf16[336,128]{1,0:T(8,128)(2,1)S(1)} %get-tuple-element.12), channel_id=1, source_target_pairs={{1,2},{3,4},{5,6},{2,1},{4,3},{6,5},{9,10},{11,12},{13,14},{10,9},... | collective-permute-start | bytes 258056 | tf_op jit(solution)/shard_map/ppermute | solution.py:294
  24.2 0.0 collective-permute-done.8
  24.2 5.0 %collective-permute-start.11 = (f32[64,128]{1,0:T(8,128)S(1)}, f32[64,128]{1,0:T(8,128)S(1)}, u32[]{:S(2)}, u32[]{:S(2)}) collective-permute-start(f32[64,128]{1,0:T(8,128)S(1)} %add.3.refs_7_), channel_id=1, source_target_pairs={{0,6},{1,7},{2,4},{3,5},{4,2},{5,3},{6,0},{7,1},{8,14},{9,15},{10,... | collective-permute-start | bytes 98312 | tf_op jit(solution)/shard_map/ppermute | solution.py:252
  29.2 0.0 collective-permute-start.10
  29.2 0.6 %collective-permute-start.9 = (f32[64,128]{1,0:T(8,128)S(1)}, f32[64,128]{1,0:T(8,128)S(1)}, u32[]{:S(2)}, u32[]{:S(2)}) collective-permute-start(f32[64,128]{1,0:T(8,128)S(1)} %add.3.refs_7_), channel_id=1, source_target_pairs={{0,2},{1,3},{2,0},{3,1},{4,6},{5,7},{6,4},{7,5},{8,10},{9,11},{10,... | collective-permute-start | bytes 98312 | tf_op jit(solution)/shard_map/ppermute | solution.py:252
  29.8 0.1 fusion.1
  30.0 0.1 reshape.33.present_ref.refs_0_
  30.0 0.0 copy-start
  30.0 1.1 %copy-done = s32[9,128,128]{2,1,0:T(8,128)S(1)} copy-done((s32[9,128,128]{2,1,0:T(8,128)S(1)}, s32[9,128,128]{2,1,0:T(8,128)}, u32[]{:S(2)}) %copy-start) | copy-done | bytes 589848
  31.1 0.6 %shard_map.79.mask_ref.refs_4_ = bf16[9,128,1024]{2,1,0:T(8,128)(2,1)S(1)} custom-call(s32[9,128,128]{2,1,0:T(8,128)S(1)} %copy-done), custom_call_target="tpu_custom_call" | custom-call | tf_op jit(solution)/shard_map/pallas_call | solution.py:240
  31.7 2.0 %shard_map.80 = (f32[512,64]{1,0:T(8,128)S(1)}, f32[8,16,128]{2,1,0:T(8,128)S(1)}) custom-call(s32[54]{0:T(128)S(1)} %reshape.33.present_ref.refs_0_, bf16[2,336,128]{2,1,0:T(8,128)(2,1)S(1)} %get-tuple-element.10.cols_ref.refs_1_, bf16[9,128,1024]{2,1,0:T(8,128)(2,1)S(1)} %shard_map.79.mask_ref.refs_4_), custom_call_target="tpu_custom_call" | custom-call | tf_op jit(solution)/shard_map/pallas_call | solution.py:240
  33.8 0.0 collective-permute-done.11.refs_10_
  33.8 0.2 collective-permute-done.10.refs_9_
  34.0 0.0 collective-permute-done.9.refs_8_
  34.0 0.0 collective-permute-done.6.refs_2_
  34.0 0.0 collective-permute-done.7.refs_3_
  34.0 4.1 %shard_map.81 = (f32[8,64,64]{2,1,0:T(8,128)}, f32[64,64]{1,0:T(8,128)}) custom-call(s32[54]{0:T(128)S(1)} %reshape.33.present_ref.refs_0_, bf16[2,336,128]{2,1,0:T(8,128)(2,1)S(1)} %get-tuple-element.10.cols_ref.refs_1_, bf16[336,128]{1,0:T(8,128)(2,1)S(1)} %collective-permute-done.6.refs_2_, bf16[336,128]{1,0:T(8,128)(2,1)S(1)} %collective-permute-done.7.refs_3_, ...), custom_call_target="tpu_custom_call" | custom-call | tf_op jit(solution)/shard_map/pallas_call | solution.py:240
  (3 shorter events, 0.0 us)
Async XLA Ops:
  0.6 17.9 %collective-permute-start.4 = (f32[16,3072]{1,0:T(8,128)}, f32[16,3072]{1,0:T(8,128)S(1)}, u32[]{:S(2)}, u32[]{:S(2)}) collective-permute-start(f32[16,3072]{1,0:T(8,128)} %refs_3_.1), channel_id=1, source_target_pairs={{0,16},{8,24},{16,0},{24,8},{1,17},{9,25},{17,1},{25,9},{2,18},{10... | collective-permute-start | bytes 589832 | tf_op jit(solution)/shard_map/ppermute | solution.py:252
  3.7 14.9 %collective-permute-start.3 = (f32[16,3072]{1,0:T(8,128)}, f32[16,3072]{1,0:T(8,128)S(1)}, u32[]{:S(2)}, u32[]{:S(2)}) collective-permute-start(f32[16,3072]{1,0:T(8,128)} %refs_3_.1), channel_id=1, source_target_pairs={{0,8},{8,0},{16,24},{24,16},{1,9},{9,1},{17,25},{25,17},{2,10},{10... | collective-permute-start | bytes 589832 | tf_op jit(solution)/shard_map/ppermute | solution.py:252
  5.2 13.4 %collective-permute-start.5 = (f32[16,3072]{1,0:T(8,128)}, f32[16,3072]{1,0:T(8,128)S(1)}, u32[]{:S(2)}, u32[]{:S(2)}) collective-permute-start(f32[16,3072]{1,0:T(8,128)} %refs_3_.1), channel_id=1, source_target_pairs={{0,24},{8,16},{16,8},{24,0},{1,25},{9,17},{17,9},{25,1},{2,26},{10... | collective-permute-start | bytes 589832 | tf_op jit(solution)/shard_map/ppermute | solution.py:252
  5.2 9.3 %collective-permute-start = (s32[3,2]{0,1:T(2,128)}, s32[3,2]{0,1:T(2,128)S(1)}, u32[]{:S(2)}, u32[]{:S(2)}) collective-permute-start(s32[3,2]{0,1:T(2,128)} %param.10), channel_id=1, source_target_pairs={{0,8},{8,0},{16,24},{24,16},{1,9},{9,1},{17,25},{25,17},{2,10},{10... | collective-permute-start | bytes 80 | tf_op jit(solution)/shard_map/ppermute | solution.py:252
  7.1 7.9 %collective-permute-start.2 = (s32[3,2]{0,1:T(2,128)}, s32[3,2]{0,1:T(2,128)S(1)}, u32[]{:S(2)}, u32[]{:S(2)}) collective-permute-start(s32[3,2]{0,1:T(2,128)} %param.10), channel_id=1, source_target_pairs={{0,24},{8,16},{16,8},{24,0},{1,25},{9,17},{17,9},{25,1},{2,26},{10... | collective-permute-start | bytes 80 | tf_op jit(solution)/shard_map/ppermute | solution.py:252
  9.5 0.7 %copy-start.3 = (f32[64,8]{0,1:T(8,128)S(1)}, f32[64,8]{0,1:T(8,128)}, u32[]{:S(2)}) copy-start(f32[64,8]{0,1:T(8,128)} %param.7) | copy-start | bytes 6148
  14.5 3.8 %collective-permute-start.1 = (s32[3,2]{0,1:T(2,128)}, s32[3,2]{0,1:T(2,128)S(1)}, u32[]{:S(2)}, u32[]{:S(2)}) collective-permute-start(s32[3,2]{0,1:T(2,128)} %param.10), channel_id=1, source_target_pairs={{0,16},{8,24},{16,0},{24,8},{1,17},{9,25},{17,1},{25,9},{2,18},{10... | collective-permute-start | bytes 80 | tf_op jit(solution)/shard_map/ppermute | solution.py:252
  18.5 0.9 %copy-start.1 = (f32[16,3072]{1,0:T(8,128)S(1)}, f32[16,3072]{1,0:T(8,128)}, u32[]{:S(2)}) copy-start(f32[16,3072]{1,0:T(8,128)} %refs_3_.1) | copy-start | bytes 589828
  19.5 0.7 %copy-start.2 = (f32[3072]{0:T(1024)S(1)}, f32[3072]{0:T(1024)}, u32[]{:S(2)}) copy-start(f32[3072]{0:T(1024)} %param.8) | copy-start | bytes 36868
  21.5 2.7 %collective-permute-start.8 = (f32[64,128]{1,0:T(8,128)S(1)}, f32[64,128]{1,0:T(8,128)S(1)}, u32[]{:S(2)}, u32[]{:S(2)}) collective-permute-start(f32[64,128]{1,0:T(8,128)S(1)} %get-tuple-element.15), channel_id=1, source_target_pairs={{0,1},{1,0},{2,3},{3,2},{4,5},{5,4},{6,7},{7,6},{8,9},{9,8},{10,11... | collective-permute-start | bytes 98312 | tf_op jit(solution)/shard_map/ppermute | solution.py:252
  23.0 11.0 %collective-permute-start.6 = (bf16[336,128]{1,0:T(8,128)(2,1)S(1)}, bf16[336,128]{1,0:T(8,128)(2,1)S(1)}, u32[]{:S(2)}, u32[]{:S(2)}) collective-permute-start(bf16[336,128]{1,0:T(8,128)(2,1)S(1)} %get-tuple-element.11), channel_id=1, source_target_pairs={{0,1},{1,0},{2,3},{3,2},{4,5},{5,4},{6,7},{7,6},{8,9},{9,8},{10,11... | collective-permute-start | bytes 258056 | tf_op jit(solution)/shard_map/ppermute | solution.py:252
  23.5 10.5 %collective-permute-start.7 = (bf16[336,128]{1,0:T(8,128)(2,1)S(1)}, bf16[336,128]{1,0:T(8,128)(2,1)S(1)}, u32[]{:S(2)}, u32[]{:S(2)}) collective-permute-start(bf16[336,128]{1,0:T(8,128)(2,1)S(1)} %get-tuple-element.12), channel_id=1, source_target_pairs={{1,2},{3,4},{5,6},{2,1},{4,3},{6,5},{9,10},{11,12},{13,14},{10,9},... | collective-permute-start | bytes 258056 | tf_op jit(solution)/shard_map/ppermute | solution.py:294
  24.2 9.6 %collective-permute-start.11 = (f32[64,128]{1,0:T(8,128)S(1)}, f32[64,128]{1,0:T(8,128)S(1)}, u32[]{:S(2)}, u32[]{:S(2)}) collective-permute-start(f32[64,128]{1,0:T(8,128)S(1)} %add.3.refs_7_), channel_id=1, source_target_pairs={{0,6},{1,7},{2,4},{3,5},{4,2},{5,3},{6,0},{7,1},{8,14},{9,15},{10,... | collective-permute-start | bytes 98312 | tf_op jit(solution)/shard_map/ppermute | solution.py:252
  29.2 4.8 %collective-permute-start.10 = (f32[64,128]{1,0:T(8,128)S(1)}, f32[64,128]{1,0:T(8,128)S(1)}, u32[]{:S(2)}, u32[]{:S(2)}) collective-permute-start(f32[64,128]{1,0:T(8,128)S(1)} %add.3.refs_7_), channel_id=1, source_target_pairs={{0,4},{1,5},{2,6},{3,7},{4,0},{5,1},{6,2},{7,3},{8,12},{9,13},{10,... | collective-permute-start | bytes 98312 | tf_op jit(solution)/shard_map/ppermute | solution.py:252
  29.2 4.8 %collective-permute-start.9 = (f32[64,128]{1,0:T(8,128)S(1)}, f32[64,128]{1,0:T(8,128)S(1)}, u32[]{:S(2)}, u32[]{:S(2)}) collective-permute-start(f32[64,128]{1,0:T(8,128)S(1)} %add.3.refs_7_), channel_id=1, source_target_pairs={{0,2},{1,3},{2,0},{3,1},{4,6},{5,7},{6,4},{7,5},{8,10},{9,11},{10,... | collective-permute-start | bytes 98312 | tf_op jit(solution)/shard_map/ppermute | solution.py:252
  30.0 1.1 %copy-start = (s32[9,128,128]{2,1,0:T(8,128)S(1)}, s32[9,128,128]{2,1,0:T(8,128)}, u32[]{:S(2)}) copy-start(s32[9,128,128]{2,1,0:T(8,128)} %bins_ref.1) | copy-start | bytes 1769476

commit v2 on v1

v2 whole, which is shorter than its diff:
```python
import math

import jax
import jax.numpy as jnp
from jax import lax
from jax.experimental import pallas as pl
from jax.experimental.pallas import tpu as pltpu
from jax.sharding import PartitionSpec as P

NCH = 64
MODES = 8
TILE = 128
NBIN = 8
NBR = 9
TA = 3
TB = 2
EXT = TA + 2
WROW = EXT * NCH
COLH = WROW + 16
CHUNK = 512

F32 = jnp.float32
BF16 = jnp.bfloat16
ROWS_BY_ROWS = (((1,), (1,)), ((), ()))
VMEM = pl.BlockSpec(memory_space=pltpu.VMEM)
SMEM = pl.BlockSpec(memory_space=pltpu.SMEM)
HBM = pl.BlockSpec(memory_space=pltpu.HBM)


def pieces(x):
    high = x.astype(BF16)
    rest = x - high.astype(F32)
    middle = rest.astype(BF16)
    low = (rest - middle.astype(F32)).astype(BF16)
    return high, middle, low


def prepare_kernel(counts_ref, maps_ref, joined_ref):
    local_channels, pixels = maps_ref.shape
    joined_ref[:, :pixels] = maps_ref[...]
    joined_ref[:, pixels:] = jnp.zeros((local_channels, joined_ref.shape[1] - pixels), F32)
    for tile in range(TA * TB):
        observed = jnp.where(counts_ref[tile % TB, tile // TB] > 0, 1.0, 0.0)
        row, lane = tile % local_channels, pixels + tile // local_channels * TILE
        joined_ref[row : row + 1, lane : lane + TILE] = jnp.full((1, TILE), observed)


def setting_kernel(
    local_channels,
    counts_ref,
    neighbours_ref,
    modes_ref,
    weight_ref,
    bins_ref,
    project_ref,
    padded_weight_ref,
    mask_ref,
    live_ref,
    held_counts,
    held_neighbours,
    held_modes,
    held_bins,
    copied,
):
    pixels = weight_ref.shape[1]
    edge = TB * TILE
    pairs = [
        (modes_ref, held_modes),
        (bins_ref, held_bins),
        (weight_ref, padded_weight_ref.at[:, pl.ds(edge, pixels)]),
        (counts_ref, held_counts),
        (neighbours_ref, held_neighbours),
    ]
    copies = [
        pltpu.make_async_copy(source, target, copied.at[number])
        for number, (source, target) in enumerate(pairs)
    ]
    for copy in copies:
        copy.start()
    padded_weight_ref[:, :edge] = jnp.zeros((1, edge), F32)
    padded_weight_ref[:, edge + pixels :] = jnp.zeros((1, edge), F32)
    copies[0].wait()
    vectors = held_modes[...].T
    lane = lax.broadcasted_iota(jnp.int32, (NCH, MODES), 1)
    for number in range(MODES):
        column = jnp.sum(jnp.where(lane == number, vectors, 0.0), axis=1, keepdims=True)
        inner = jnp.sum(column * vectors, axis=0, keepdims=True)
        square = jnp.sum(column * column, axis=0, keepdims=True)
        scale = 1.0 / jnp.sqrt(square + 1e-06)
        unit = column * scale
        reduced = vectors - unit * (inner * scale)
        vectors = jnp.where(lane == number, unit, jnp.where(lane > number, reduced, vectors))
    channel = lax.broadcasted_iota(jnp.int32, (NCH, NCH), 0)
    row = lax.broadcasted_iota(jnp.int32, (NCH, NCH), 1)
    holder = lax.axis_index("chan") ^ (row // local_channels)
    source = holder * local_channels + row % local_channels
    order = jnp.where(channel == source, 1.0, 0.0)
    ordered = lax.dot_general(
        order,
        vectors,
        (((0,), (0,)), ((), ())),
        precision=lax.Precision.HIGHEST,
        preferred_element_type=F32,
    )
    outer = lax.dot_general(
        vectors,
        ordered,
        ROWS_BY_ROWS,
        precision=lax.Precision.HIGHEST,
        preferred_element_type=F32,
    )
    high, middle, low = pieces(order - outer)
    none = jnp.zeros((NCH, NCH), BF16)
    project_ref[0:NCH, :] = jnp.concatenate([high, high, high], axis=1)
    project_ref[NCH : 2 * NCH, :] = jnp.concatenate([middle, middle, none], axis=1)
    project_ref[2 * NCH : 3 * NCH, :] = jnp.concatenate([low, none, none], axis=1)
    copies[1].wait()
    for code in range(NBR):
        table = held_bins[code]
        for level in range(NBIN):
            mask_ref[code, :, level * TILE : (level + 1) * TILE] = jnp.where(
                table == level, 1.0, 0.0
            ).astype(BF16)
    for copy in copies[2:]:
        copy.wait()
    for tile in range(TA * TB):
        count = held_counts[tile % TB, tile // TB]
        codes = jnp.zeros((), jnp.int32)
        for slot in range(NBR):
            code = held_neighbours[tile // TB, tile % TB, slot]
            codes = codes | jnp.where(slot < count, jnp.int32(1) << code, 0)
        for code in range(NBR):
            live = ((codes >> code) & 1).astype(F32)
            live_ref[code, tile] = jnp.full((16, TILE), live).astype(BF16)


def clean_kernel(block_count, flag_count, *refs):
    project_ref, weights_ref = refs[:2]
    block_refs = refs[2 : 2 + block_count]
    flag_refs = refs[2 + block_count : 2 + block_count + flag_count]
    cols_ref, near_ref, far_ref = refs[2 + block_count + flag_count :][:3]
    padded_ref, masked_ref, flags_ref = refs[5 + block_count + flag_count :]
    pixels = masked_ref.shape[1]
    row_pixels = TB * TILE
    region_pixels = TA * row_pixels
    region_tiles = TA * TB
    chan_index = lax.axis_index("chan")
    side = lax.axis_index("patch") % 2

    flags = [ref[...] for ref in flag_refs]
    flags += [ref[:8, pixels:] for ref in block_refs if ref.shape[1] > pixels]
    for step, rows in enumerate(flags):
        holder = chan_index ^ step
        flags_ref[pl.ds(pl.multiple_of(holder * 8, 8), 8), :] = rows
    for edge in (0, row_pixels + pixels):
        padded_ref[:, edge : edge + row_pixels] = jnp.zeros((NCH, row_pixels), BF16)

    project = project_ref[...]
    observed_tiles = jnp.zeros((1, TILE), F32)
    for begin in range(0, pixels, CHUNK):
        maps = jnp.concatenate([ref[:, begin : begin + CHUNK] for ref in block_refs], axis=0)
        split = jnp.concatenate(pieces(maps), axis=0)
        product = jnp.dot(project, split, preferred_element_type=F32)
        cleaned = (product[2 * NCH :] + product[NCH : 2 * NCH]) + product[:NCH]
        weights = weights_ref[:, row_pixels + begin : row_pixels + begin + CHUNK]
        weighted = cleaned * weights
        padded_ref[:, row_pixels + begin : row_pixels + begin + CHUNK] = weighted.astype(BF16)
        for place in range(begin, begin + CHUNK, TILE):
            tile = place // TILE
            at = tile // region_tiles * 8 + tile % region_tiles
            observed = flags_ref[at : at + 1, :]
            observed_tiles = observed_tiles + observed
            part = weighted[:, place - begin : place - begin + TILE]
            part = jnp.where(observed > 0, part, 0.0)
            masked_ref[:, place : place + TILE] = part.astype(BF16)
    covariance = lax.dot_general(
        masked_ref[...],
        padded_ref[:, row_pixels : row_pixels + pixels],
        ROWS_BY_ROWS,
        preferred_element_type=F32,
    )
    total = jnp.broadcast_to(observed_tiles[:, :NCH] * float(TILE), (NCH, NCH))
    near_ref[:NCH, :] = jnp.concatenate([covariance, total], axis=1)

    rows = lax.broadcasted_iota(jnp.int32, (16, TILE), 0)
    for col in range(TB):
        weight_rows = jnp.zeros((16, TILE), F32)
        for row in range(EXT):
            start = chan_index * region_pixels + row * row_pixels + col * TILE
            at = pl.ds(pl.multiple_of(start, TILE), TILE)
            cols_ref[col, row * NCH : (row + 1) * NCH, :] = padded_ref[:, at]
            weight_rows = jnp.where(rows == row, weights_ref[:, at], weight_rows)
        cols_ref[col, WROW:COLH, :] = weight_rows.astype(BF16)
    near_ref[NCH:, :] = cols_ref[1 - side].astype(F32)
    far_ref[...] = cols_ref[side]


def add_pairs(code, live_ref, centres, partners, mask_ref):
    row_shift = code // 3
    own = slice(NCH, (TA + 1) * NCH)
    left = jnp.concatenate(
        [column[own] for column in centres] + [column[WROW:] for column in centres], axis=0
    )
    binned = jnp.dot(left, mask_ref[code], preferred_element_type=F32).astype(BF16)
    rows = lax.broadcasted_iota(jnp.int32, (16, TILE), 0)
    right = []
    weight_sums = [jnp.zeros((16, TILE), F32) for _ in range(NBIN)]
    for col in range(TB):
        partner_weights = partners[col][WROW:].astype(F32)
        shifted = jnp.zeros((16, TILE), F32)
        for row in range(TA):
            live = live_ref[code, row * TB + col]
            place = row + row_shift
            tile = partners[col][place * NCH : (place + 1) * NCH]
            right.append(tile * jnp.concatenate([live] * (NCH // 16), axis=0))
            weight = partner_weights[place : place + 1] * live.astype(F32)[:1]
            shifted = jnp.where(rows == row + 1, weight, shifted)
        first = TA * TB * NCH + col * 16
        for level in range(NBIN):
            lanes = slice(level * TILE, (level + 1) * TILE)
            weight_sums[level] += binned[first : first + 16, lanes].astype(F32) * shifted
    right = jnp.concatenate(right, axis=1)
    left = jnp.concatenate(
        [
            jnp.concatenate(
                [
                    binned[at * NCH : (at + 1) * NCH, level * TILE : (level + 1) * TILE]
                    for at in range(TA * TB)
                ],
                axis=1,
            )
            for level in range(NBIN)
        ],
        axis=0,
    )
    sums = lax.dot_general(left, right, ROWS_BY_ROWS, preferred_element_type=F32)
    return sums, weight_sums


def inner_kernel(live_ref, cols_ref, mask_ref, sums_ref, weight_sums_ref, none_ref):
    none_ref[...] = jnp.zeros_like(none_ref)
    columns = [cols_ref[col] for col in range(TB)]
    for number, code in enumerate((1, 4, 7)):
        sums, weight_sums = add_pairs(code, live_ref, columns, columns, mask_ref)
        if number:
            sums_ref[...] += sums
        else:
            sums_ref[...] = sums
        for level in range(NBIN):
            if number:
                weight_sums_ref[level] += weight_sums[level]
            else:
                weight_sums_ref[level] = weight_sums[level]


def outer_kernel(
    live_ref,
    cols_ref,
    near_ref,
    far_ref,
    mask_ref,
    sums_in_ref,
    weight_in_ref,
    sums_ref,
    weight_sums_ref,
):
    even = lax.axis_index("patch") % 2 == 0
    columns = [cols_ref[col] for col in range(TB)]
    near, far = near_ref[NCH:].astype(BF16), far_ref[...]
    before = jnp.where(even, far, near)
    after = jnp.where(even, near, far)
    sums_ref[...] = sums_in_ref[...]
    weight_sums_ref[...] = weight_in_ref[...]
    for code in (0, 3, 6, 2, 5, 8):
        partners = [before, columns[0]] if code % 3 == 0 else [columns[1], after]
        sums, weight_sums = add_pairs(code, live_ref, columns, partners, mask_ref)
        sums_ref[...] += sums
        for level in range(NBIN):
            weight_sums_ref[level] += weight_sums[level]


def scale_kernel(sums_ref, weight_sums_ref, piece_ref, other_piece_ref, corr_ref, cov_ref):
    whole = piece_ref[...] + other_piece_ref[...]
    covariance = whole[:, :NCH] / whole[:, NCH:]
    cov_ref[...] = covariance
    channel = lax.broadcasted_iota(jnp.int32, (NCH, NCH), 0)
    other = lax.broadcasted_iota(jnp.int32, (NCH, NCH), 1)
    diagonal = jnp.where(channel == other, covariance, 0.0)
    spread_down = jnp.sqrt(jnp.sum(diagonal, axis=1, keepdims=True) + 1e-06)
    spread_across = jnp.sqrt(jnp.sum(diagonal, axis=0, keepdims=True) + 1e-06)
    norm_scale = spread_down * spread_across
    for level in range(NBIN):
        taper = 0.75 + 0.25 * math.cos(math.pi * level / NBIN)
        total = jnp.sum(
            jnp.sum(weight_sums_ref[level], axis=1, keepdims=True), axis=0, keepdims=True
        )
        pair_weight = jnp.maximum(total, 1.0)
        sums = sums_ref[level * NCH : (level + 1) * NCH]
        corr_ref[level] = (taper * sums) / (pair_weight * norm_scale)


def run(kernel, outs, args, scratch=(), spec=VMEM):
    return pl.pallas_call(
        kernel,
        out_shape=outs,
        in_specs=[spec] * len(args),
        out_specs=jax.tree.map(lambda _: VMEM, outs),
        scratch_shapes=list(scratch),
        compiler_params=pltpu.CompilerParams(vmem_limit_bytes=24 * 2**20),
    )(*args)


def exchange(x, axis, step):
    count = lax.axis_size(axis)
    return lax.ppermute(x, axis, [(i, i ^ step) for i in range(count)])


def per_device(sky_maps, mode_vectors, pixel_weight, neighbours, tile_counts, pair_bins):
    shape = jax.ShapeDtypeStruct
    chan_count = lax.axis_size("chan")
    patch_count = lax.axis_size("patch")
    local_channels, pixels = sky_maps.shape

    counts = tile_counts.T
    flag_lanes = -(-TA * TB // local_channels) * TILE
    joined = pl.pallas_call(
        prepare_kernel,
        out_shape=shape((local_channels, pixels + flag_lanes), F32),
        in_specs=[SMEM, VMEM],
        out_specs=VMEM,
        compiler_params=pltpu.CompilerParams(vmem_limit_bytes=24 * 2**20),
    )(counts, sky_maps)
    blocks = [joined] + [exchange(joined, "chan", step) for step in range(1, chan_count)]
    all_flags = []
    if local_channels % 16:
        for block in blocks:
            rows = [
                block[t % local_channels, pixels + t // local_channels * TILE :][:TILE]
                for t in range(TA * TB)
            ]
            all_flags.append(jnp.pad(jnp.stack(rows), ((0, 8 - TA * TB), (0, 0))))
        blocks = [jnp.concatenate([block[:, :pixels] for block in blocks], axis=0)]
    project, weights, mask, live = run(
        lambda *refs: setting_kernel(local_channels, *refs),
        (
            shape((3 * NCH, 3 * NCH), BF16),
            shape((1, pixels + 2 * TB * TILE), F32),
            shape((NBR, TILE, NBIN * TILE), BF16),
            shape((NBR, TA * TB, 16, TILE), BF16),
        ),
        [counts, neighbours, mode_vectors.T, pixel_weight.reshape(1, pixels), pair_bins],
        scratch=[
            pltpu.SMEM((TB, TA), jnp.int32),
            pltpu.SMEM((TA, TB, NBR), jnp.int32),
            pltpu.VMEM((MODES, NCH), F32),
            pltpu.VMEM((NBR, TILE, TILE), jnp.int32),
            pltpu.SemaphoreType.DMA((5,)),
        ],
        spec=HBM,
    )

    cols, near, far = run(
        lambda *refs: clean_kernel(len(blocks), len(all_flags), *refs),
        (shape((TB, COLH, TILE), BF16), shape((NCH + COLH, TILE), F32), shape((COLH, TILE), BF16)),
        [project, weights] + blocks + all_flags,
        scratch=[
            pltpu.VMEM((NCH, pixels + 2 * TB * TILE), BF16),
            pltpu.VMEM((NCH, pixels), BF16),
            pltpu.VMEM((chan_count * 8, TILE), F32),
        ],
    )

    received = exchange(near, "patch", 1)
    far_pairs = [(i, i + 1) for i in range(1, patch_count - 1, 2)]
    far = lax.ppermute(far, "patch", far_pairs + [(j, i) for i, j in far_pairs])
    piece = near[:NCH] + received[:NCH]
    other_piece = exchange(piece, "patch", 2)
    sums_shape = shape((NBIN * NCH, NCH), F32)
    weight_shape = shape((NBIN, 16, TILE), F32)
    pair_shapes = (sums_shape, weight_shape)
    none_shape = shape((NCH, 2 * NCH), F32)
    sums, weight_sums, none = run(inner_kernel, pair_shapes + (none_shape,), [live, cols, mask])
    step = 4
    while step < patch_count:
        piece = piece + other_piece + none
        other_piece = exchange(piece, "patch", step)
        step *= 2

    sums, weight_sums = run(
        outer_kernel, pair_shapes, [live, cols, received, far, mask, sums, weight_sums]
    )
    correlation, covariance = run(
        scale_kernel,
        (shape((NBIN, NCH, NCH), F32), shape((NCH, NCH), F32)),
        [sums, weight_sums, piece, other_piece],
    )
    return (correlation[None, None], covariance)


def solution(mesh):
    return jax.shard_map(
        per_device,
        mesh=mesh,
        in_specs=(
            P("chan", "patch"),
            P(),
            P("patch"),
            P("chan", "patch", None),
            P("chan", "patch"),
            P(),
        ),
        out_specs=(P("chan", "patch", None, None, None), P()),
        check_vma=False,
    )
```

time: 38.7 us -> 30.6 us (0.79)
  starting transfers between devices: 15.2 us -> 10.6 us
  waiting for transfers between devices: 6.17 us -> 5.22 us
  local copies, waits for them, and re-layouts: 5.66 us -> 4.74 us
  other arithmetic: 0.89 us -> 0.01 us
  Pallas kernels: 9.48 us -> 8.91 us
    ppermute x11 -> x6, starting transfers between devices: 14.5 us -> 9.99 us  [exchange(): return lax.ppermute(x, axis, [(i, i ^ step) for i in range(count)])]
    ppermute x11 -> x6, waiting for transfers between devices: 6.16 us -> 5.22 us  [exchange(): return lax.ppermute(x, axis, [(i, i ^ step) for i in range(count)])]
    lt x1 -> x0, other arithmetic: 0.69 us -> none  [per_device(): slot_live = codes[None, None, :] < tile_counts[:, :, None]]
    pallas_call x5 -> x6, Pallas kernels: 9.48 us -> 8.91 us  [the longest x5 8.35 us: run(): pl.pallas_call(kernel, out_shape=outs, in_specs=[spec] * len(args), out_s...]
    unnamed x10 -> x12, local copies, waits for them, and re-layouts: 4.96 us -> 4.74 us
  transfers between devices with their start and end apart: 12 -> 7, of which waited for: 3 -> 4; matrix products, arithmetic and copies ran while one was open for 8% -> 0% of each run, Pallas kernels for 11% -> 22%
where the time goes in v2:
time: 30.6 us; the launch traced here: 30.2 us
  starting transfers between devices  10.6 us (35%)
  Pallas kernels  8.91 us (29%)
  waiting for transfers between devices  5.22 us (17%)
  local copies, waits for them, and re-layouts  4.74 us (15%)
  between operations  0.71 us (2%)
    ppermute x6, starting transfers between devices, exchange(): return lax.ppermute(x, axis, [(i, i ^ step) for i in range(count)])  9.99 us
    pallas_call x5, Pallas kernels, run(): pl.pallas_call(kernel, out_shape=outs, in_specs=[spec] * len(args), out_s...  8.35 us
    ppermute x6, waiting for transfers between devices, exchange(): return lax.ppermute(x, axis, [(i, i ^ step) for i in range(count)])  5.22 us
    unnamed x12, local copies, waits for them, and re-layouts  4.74 us
    ppermute x1, starting transfers between devices, per_device(): far = lax.ppermute(far, 'patch', far_pairs + [(j, i) for i, j in far_pairs])  0.65 us
  transfers between devices with their start and end apart: 7, of which 4 were waited for; matrix products, arithmetic and copies ran while one was open for 0% of the time, Pallas kernels for 22%

profile of v2, /device:TPU:0, one launch (start us, length us, event | category | flops | bytes accessed | tf_op | source)
XLA Modules:
  0.0 30.2 jit_solution(16863984494659820207)
XLA Ops:
  0.6 0.0 copy-start.1
  0.6 0.9 %copy-done.1 = f32[16,3072]{1,0:T(8,128)S(1)} copy-done((f32[16,3072]{1,0:T(8,128)S(1)}, f32[16,3072]{1,0:T(8,128)}, u32[]{:S(2)}) %copy-start.1) | copy-done | bytes 196632
  1.6 0.0 copy-start.4
  1.6 0.7 %copy-done.4 = s32[3,2]{0,1:T(2,128)S(1)} copy-done((s32[3,2]{0,1:T(2,128)S(1)}, s32[3,2]{0,1:T(2,128)}, u32[]{:S(2)}) %copy-start.4) | copy-done | bytes 48
  2.2 0.6 %shard_map.78.refs_2_ = f32[16,3200]{1,0:T(8,128)S(1)} custom-call(s32[2,3]{1,0:T(2,128)S(1)} %bitcast.6, f32[16,3072]{1,0:T(8,128)S(1)} %copy-done.1), custom_call_target="tpu_custom_call" | custom-call | tf_op jit(solution)/shard_map/pallas_call | solution.py:326
  2.8 4.0 %collective-permute-start.2 = (f32[16,3200]{1,0:T(8,128)S(1)}, f32[16,3200]{1,0:T(8,128)S(1)}, u32[]{:S(2)}, u32[]{:S(2)}) collective-permute-start(f32[16,3200]{1,0:T(8,128)S(1)} %shard_map.78.refs_2_), channel_id=1, source_target_pairs={{0,24},{8,16},{16,8},{24,0},{1,25},{9,17},{17,9},{25,1},{2,26},{10... | collective-permute-start | bytes 614408 | tf_op jit(solution)/shard_map/ppermute | solution.py:315
  6.8 0.5 %collective-permute-start.1 = (f32[16,3200]{1,0:T(8,128)S(1)}, f32[16,3200]{1,0:T(8,128)S(1)}, u32[]{:S(2)}, u32[]{:S(2)}) collective-permute-start(f32[16,3200]{1,0:T(8,128)S(1)} %shard_map.78.refs_2_), channel_id=1, source_target_pairs={{0,16},{8,24},{16,0},{24,8},{1,17},{9,25},{17,1},{25,9},{2,18},{10... | collective-permute-start | bytes 614408 | tf_op jit(solution)/shard_map/ppermute | solution.py:315
  7.3 0.1 collective-permute-start
  7.4 0.0 copy-start
  7.4 1.1 %copy-done = s32[9,128,128]{2,1,0:T(8,128)S(1)} copy-done((s32[9,128,128]{2,1,0:T(8,128)S(1)}, s32[9,128,128]{2,1,0:T(8,128)}, u32[]{:S(2)}) %copy-start) | copy-done | bytes 589848
  8.5 0.0 copy-start.2
  8.5 0.7 %copy-done.2 = f32[3072]{0:T(1024)S(1)} copy-done((f32[3072]{0:T(1024)S(1)}, f32[3072]{0:T(1024)}, u32[]{:S(2)}) %copy-start.2) | copy-done | bytes 12312
  9.2 0.0 copy-start.3
  9.2 0.7 %copy-done.3 = f32[64,8]{0,1:T(8,128)S(1)} copy-done((f32[64,8]{0,1:T(8,128)S(1)}, f32[64,8]{0,1:T(8,128)}, u32[]{:S(2)}) %copy-start.3) | copy-done | bytes 2072
  9.9 0.0 copy-start.5
  9.9 0.7 %copy-done.5 = s32[3,2,9]{2,1,0:T(2,128)S(1)} copy-done((s32[3,2,9]{2,1,0:T(2,128)S(1)}, s32[3,2,9]{2,1,0:T(2,128)}, u32[]{:S(2)}) %copy-start.5) | copy-done | bytes 240
  10.6 2.4 %shard_map.77 = (bf16[192,192]{1,0:T(8,128)(2,1)S(1)}, f32[1,3584]{1,0:T(1,128)S(1)}, bf16[9,128,1024]{2,1,0:T(8,128)(2,1)S(1)}, bf16[9,6,16,128]{3,2,1,0:T(8,128)(2,1)S(1)}) custom-call(s32[2,3]{1,0:T(2,128)S(1)} %bitcast.7, s32[3,2,9]{2,1,0:T(2,128)S(1)} %copy-done.5, f32[8,64]{1,0:T(8,128)S(1)} %bitcast.5, f32[1,3072]{1,0:T(1,128)S(1)} %bitcast.4, ...), custom_call_target="tpu_custom_call" | custom-call | tf_op jit(solution)/shard_map/pallas_call | solution.py:303
  12.9 0.0 collective-permute-done.2.refs_5_
  12.9 3.3 %collective-permute-done.1.refs_4_ = f32[16,3200]{1,0:T(8,128)S(1)} collective-permute-done((f32[16,3200]{1,0:T(8,128)S(1)}, f32[16,3200]{1,0:T(8,128)S(1)}, u32[]{:S(2)}, u32[]{:S(2)}) %collective-permute-start.1) | collective-permute-done | bytes 204832 | tf_op jit(solution)/shard_map/ppermute | solution.py:315
  16.2 0.3 collective-permute-done.refs_3_
  16.5 0.8 %shard_map.79 = (bf16[2,336,128]{2,1,0:T(8,128)(2,1)S(1)}, f32[400,128]{1,0:T(8,128)S(1)}, bf16[336,128]{1,0:T(8,128)(2,1)S(1)}) custom-call(bf16[192,192]{1,0:T(8,128)(2,1)S(1)} %get-tuple-element.17.refs_0_, f32[1,3584]{1,0:T(1,128)S(1)} %get-tuple-element.18.refs_1_, f32[16,3200]{1,0:T(8,128)S(1)} %shard_map.78.refs_2_, ...), custom_call_target="tpu_custom_call" | custom-call | tf_op jit(solution)/shard_map/pallas_call | solution.py:303
  17.3 0.1 collective-permute-start.3
  17.4 1.4 %collective-permute-done.3.near_ref = f32[400,128]{1,0:T(8,128)S(1)} collective-permute-done((f32[400,128]{1,0:T(8,128)S(1)}, f32[400,128]{1,0:T(8,128)S(1)}, u32[]{:S(2)}, u32[]{:S(2)}) %collective-permute-start.3) | collective-permute-done | bytes 204832 | tf_op jit(solution)/shard_map/ppermute | solution.py:315
  18.8 1.6 %collective-permute-start.5 = (f32[64,128]{1,0:T(8,128)S(1)}, f32[64,128]{1,0:T(8,128)S(1)}, u32[]{:S(2)}, u32[]{:S(2)}) collective-permute-start(f32[64,128]{1,0:T(8,128)S(1)} %slice_add_fusion), channel_id=1, source_target_pairs={{0,2},{1,3},{2,0},{3,1},{4,6},{5,7},{6,4},{7,5},{8,10},{9,11},{10,... | collective-permute-start | bytes 98312 | tf_op jit(solution)/shard_map/ppermute | solution.py:315
  20.4 0.7 %collective-permute-start.4 = (bf16[336,128]{1,0:T(8,128)(2,1)S(1)}, bf16[336,128]{1,0:T(8,128)(2,1)S(1)}, u32[]{:S(2)}, u32[]{:S(2)}) collective-permute-start(bf16[336,128]{1,0:T(8,128)(2,1)S(1)} %get-tuple-element.21), channel_id=1, source_target_pairs={{1,2},{3,4},{5,6},{2,1},{4,3},{6,5},{9,10},{11,12},{13,14},{10,9},... | collective-permute-start | bytes 258056 | tf_op jit(solution)/shard_map/ppermute | solution.py:375
  21.1 1.5 %shard_map.80 = (f32[512,64]{1,0:T(8,128)S(1)}, f32[8,16,128]{2,1,0:T(8,128)S(1)}, f32[64,128]{1,0:T(8,128)S(1)}) custom-call(bf16[9,6,16,128]{3,2,1,0:T(8,128)(2,1)S(1)} %get-tuple-element.16.live_ref, bf16[2,336,128]{2,1,0:T(8,128)(2,1)S(1)} %get-tuple-element.19.cols_ref, bf16[9,128,1024]{2,1,0:T(8,128)(2,1)S(1)} %get-tuple-element.22.mask_ref), custom_call_target="tpu_custom_call" | custom-call | tf_op jit(solution)/shard_map/pallas_call | solution.py:303
  22.6 0.2 collective-permute-done.5
  22.7 3.7 %collective-permute-start.6 = (f32[64,128]{1,0:T(8,128)S(1)}, f32[64,128]{1,0:T(8,128)S(1)}, u32[]{:S(2)}, u32[]{:S(2)}) collective-permute-start(f32[64,128]{1,0:T(8,128)S(1)} %add_add_fusion.piece_ref), channel_id=1, source_target_pairs={{0,4},{1,5},{2,6},{3,7},{4,0},{5,1},{6,2},{7,3},{8,12},{9,13},{10,... | collective-permute-start | bytes 98312 | tf_op jit(solution)/shard_map/ppermute | solution.py:315
  26.5 0.0 collective-permute-done.4.far_ref
  26.5 2.8 %shard_map.81 = (f32[512,64]{1,0:T(8,128)S(1)}, f32[8,16,128]{2,1,0:T(8,128)S(1)}) custom-call(bf16[9,6,16,128]{3,2,1,0:T(8,128)(2,1)S(1)} %get-tuple-element.16.live_ref, bf16[2,336,128]{2,1,0:T(8,128)(2,1)S(1)} %get-tuple-element.19.cols_ref, f32[400,128]{1,0:T(8,128)S(1)} %collective-permute-done.3.near_ref, ...), custom_call_target="tpu_custom_call" | custom-call | tf_op jit(solution)/shard_map/pallas_call | solution.py:303
  29.3 0.0 collective-permute-done.6.other_piece_ref
  29.3 0.9 %shard_map.82 = (f32[8,64,64]{2,1,0:T(8,128)}, f32[64,64]{1,0:T(8,128)}) custom-call(f32[512,64]{1,0:T(8,128)S(1)} %get-tuple-element.25.sums_ref, f32[8,16,128]{2,1,0:T(8,128)S(1)} %get-tuple-element.26.weight_sums_ref, f32[64,128]{1,0:T(8,128)S(1)} %add_add_fusion.piece_ref, f32[64,128]{1,0:T(8,128)S(1)} %collective-permute-done.6.other_piece_ref), custom_call_target="tpu_custom_call" | custom-call | tf_op jit(solution)/shard_map/pallas_call | solution.py:303
  (2 shorter events, 0.0 us)
Async XLA Ops:
  0.6 0.9 %copy-start.1 = (f32[16,3072]{1,0:T(8,128)S(1)}, f32[16,3072]{1,0:T(8,128)}, u32[]{:S(2)}) copy-start(f32[16,3072]{1,0:T(8,128)} %maps_ref.1) | copy-start | bytes 589828
  1.6 0.7 %copy-start.4 = (s32[3,2]{0,1:T(2,128)S(1)}, s32[3,2]{0,1:T(2,128)}, u32[]{:S(2)}) copy-start(s32[3,2]{0,1:T(2,128)} %param.10) | copy-start | bytes 76
  2.8 10.1 %collective-permute-start.2 = (f32[16,3200]{1,0:T(8,128)S(1)}, f32[16,3200]{1,0:T(8,128)S(1)}, u32[]{:S(2)}, u32[]{:S(2)}) collective-permute-start(f32[16,3200]{1,0:T(8,128)S(1)} %shard_map.78.refs_2_), channel_id=1, source_target_pairs={{0,24},{8,16},{16,8},{24,0},{1,25},{9,17},{17,9},{25,1},{2,26},{10... | collective-permute-start | bytes 614408 | tf_op jit(solution)/shard_map/ppermute | solution.py:315
  6.8 9.5 %collective-permute-start.1 = (f32[16,3200]{1,0:T(8,128)S(1)}, f32[16,3200]{1,0:T(8,128)S(1)}, u32[]{:S(2)}, u32[]{:S(2)}) collective-permute-start(f32[16,3200]{1,0:T(8,128)S(1)} %shard_map.78.refs_2_), channel_id=1, source_target_pairs={{0,16},{8,24},{16,0},{24,8},{1,17},{9,25},{17,1},{25,9},{2,18},{10... | collective-permute-start | bytes 614408 | tf_op jit(solution)/shard_map/ppermute | solution.py:315
  7.3 9.3 %collective-permute-start = (f32[16,3200]{1,0:T(8,128)S(1)}, f32[16,3200]{1,0:T(8,128)S(1)}, u32[]{:S(2)}, u32[]{:S(2)}) collective-permute-start(f32[16,3200]{1,0:T(8,128)S(1)} %shard_map.78.refs_2_), channel_id=1, source_target_pairs={{0,8},{8,0},{16,24},{24,16},{1,9},{9,1},{17,25},{25,17},{2,10},{10... | collective-permute-start | bytes 614408 | tf_op jit(solution)/shard_map/ppermute | solution.py:315
  7.4 1.1 %copy-start = (s32[9,128,128]{2,1,0:T(8,128)S(1)}, s32[9,128,128]{2,1,0:T(8,128)}, u32[]{:S(2)}) copy-start(s32[9,128,128]{2,1,0:T(8,128)} %refs_4_.1) | copy-start | bytes 1769476
  8.5 0.7 %copy-start.2 = (f32[3072]{0:T(1024)S(1)}, f32[3072]{0:T(1024)}, u32[]{:S(2)}) copy-start(f32[3072]{0:T(1024)} %param.8) | copy-start | bytes 36868
  9.2 0.7 %copy-start.3 = (f32[64,8]{0,1:T(8,128)S(1)}, f32[64,8]{0,1:T(8,128)}, u32[]{:S(2)}) copy-start(f32[64,8]{0,1:T(8,128)} %param.7) | copy-start | bytes 6148
  9.9 0.7 %copy-start.5 = (s32[3,2,9]{2,1,0:T(2,128)S(1)}, s32[3,2,9]{2,1,0:T(2,128)}, u32[]{:S(2)}) copy-start(s32[3,2,9]{2,1,0:T(2,128)} %refs_1_.1) | copy-start | bytes 652
  17.3 1.5 %collective-permute-start.3 = (f32[400,128]{1,0:T(8,128)S(1)}, f32[400,128]{1,0:T(8,128)S(1)}, u32[]{:S(2)}, u32[]{:S(2)}) collective-permute-start(f32[400,128]{1,0:T(8,128)S(1)} %get-tuple-element.20), channel_id=1, source_target_pairs={{0,1},{1,0},{2,3},{3,2},{4,5},{5,4},{6,7},{7,6},{8,9},{9,8},{10,11... | collective-permute-start | bytes 614408 | tf_op jit(solution)/shard_map/ppermute | solution.py:315
  18.8 3.9 %collective-permute-start.5 = (f32[64,128]{1,0:T(8,128)S(1)}, f32[64,128]{1,0:T(8,128)S(1)}, u32[]{:S(2)}, u32[]{:S(2)}) collective-permute-start(f32[64,128]{1,0:T(8,128)S(1)} %slice_add_fusion), channel_id=1, source_target_pairs={{0,2},{1,3},{2,0},{3,1},{4,6},{5,7},{6,4},{7,5},{8,10},{9,11},{10,... | collective-permute-start | bytes 98312 | tf_op jit(solution)/shard_map/ppermute | solution.py:315
  20.4 6.1 %collective-permute-start.4 = (bf16[336,128]{1,0:T(8,128)(2,1)S(1)}, bf16[336,128]{1,0:T(8,128)(2,1)S(1)}, u32[]{:S(2)}, u32[]{:S(2)}) collective-permute-start(bf16[336,128]{1,0:T(8,128)(2,1)S(1)} %get-tuple-element.21), channel_id=1, source_target_pairs={{1,2},{3,4},{5,6},{2,1},{4,3},{6,5},{9,10},{11,12},{13,14},{10,9},... | collective-permute-start | bytes 258056 | tf_op jit(solution)/shard_map/ppermute | solution.py:375
  22.7 6.6 %collective-permute-start.6 = (f32[64,128]{1,0:T(8,128)S(1)}, f32[64,128]{1,0:T(8,128)S(1)}, u32[]{:S(2)}, u32[]{:S(2)}) collective-permute-start(f32[64,128]{1,0:T(8,128)S(1)} %add_add_fusion.piece_ref), channel_id=1, source_target_pairs={{0,4},{1,5},{2,6},{3,7},{4,0},{5,1},{6,2},{7,3},{8,12},{9,13},{10,... | collective-permute-start | bytes 98312 | tf_op jit(solution)/shard_map/ppermute | solution.py:315

commit v3 on v2

v3 whole, which is shorter than its diff:
```python
import math

import jax
import jax.numpy as jnp
from jax import lax
from jax.experimental import pallas as pl
from jax.experimental.pallas import tpu as pltpu
from jax.sharding import PartitionSpec as P

NCH = 64
MODES = 8
TILE = 128
NBIN = 8
NBR = 9
TA = 3
TB = 2
EXT = TA + 2
WROW = EXT * NCH
COLH = WROW + 16
ROW = TB * TILE
REGION = TA * ROW

F32 = jnp.float32
BF16 = jnp.bfloat16
ROWS_BY_ROWS = (((1,), (1,)), ((), ()))
VMEM = pl.BlockSpec(memory_space=pltpu.VMEM)
HBM = pl.BlockSpec(memory_space=pltpu.HBM)


def pieces(x):
    high = x.astype(BF16)
    rest = x - high.astype(F32)
    middle = rest.astype(BF16)
    low = (rest - middle.astype(F32)).astype(BF16)
    return high, middle, low


def prepare_kernel(maps_ref, *refs):
    *block_refs, held, copied = refs
    chan_index = lax.axis_index("chan")
    last = len(block_refs) - 1
    pixels = maps_ref.shape[1]
    copy = pltpu.make_async_copy(maps_ref, held, copied)
    copy.start()
    copy.wait()
    for step, ref in enumerate(block_refs):
        holder = chan_index ^ step
        start = pl.multiple_of(holder * REGION, ROW)
        above = pl.multiple_of(jnp.maximum(start - ROW, 0), ROW)
        below = pl.multiple_of(jnp.minimum(start + REGION, pixels - ROW), ROW)
        ref[:, :ROW] = jnp.where(holder > 0, held[:, pl.ds(above, ROW)], 0.0)
        ref[:, ROW : ROW + REGION] = held[:, pl.ds(start, REGION)]
        ref[:, ROW + REGION :] = jnp.where(holder < last, held[:, pl.ds(below, ROW)], 0.0)


def setting_kernel(
    local_channels,
    counts_ref,
    neighbours_ref,
    modes_ref,
    weight_ref,
    bins_ref,
    project_ref,
    padded_weight_ref,
    mask_ref,
    live_ref,
    held_counts,
    held_neighbours,
    held_modes,
    held_bins,
    copied,
):
    pixels = weight_ref.shape[1]
    edge = ROW
    pairs = [
        (modes_ref, held_modes),
        (bins_ref, held_bins),
        (weight_ref, padded_weight_ref.at[:, pl.ds(edge, pixels)]),
        (counts_ref, held_counts),
        (neighbours_ref, held_neighbours),
    ]
    copies = [
        pltpu.make_async_copy(source, target, copied.at[number])
        for number, (source, target) in enumerate(pairs)
    ]
    for copy in copies:
        copy.start()
    padded_weight_ref[:, :edge] = jnp.zeros((1, edge), F32)
    padded_weight_ref[:, edge + pixels :] = jnp.zeros((1, edge), F32)
    copies[0].wait()
    vectors = held_modes[...].T
    lane = lax.broadcasted_iota(jnp.int32, (NCH, MODES), 1)
    for number in range(MODES):
        column = jnp.sum(jnp.where(lane == number, vectors, 0.0), axis=1, keepdims=True)
        inner = jnp.sum(column * vectors, axis=0, keepdims=True)
        square = jnp.sum(column * column, axis=0, keepdims=True)
        scale = 1.0 / jnp.sqrt(square + 1e-06)
        unit = column * scale
        reduced = vectors - unit * (inner * scale)
        vectors = jnp.where(lane == number, unit, jnp.where(lane > number, reduced, vectors))
    channel = lax.broadcasted_iota(jnp.int32, (NCH, NCH), 0)
    row = lax.broadcasted_iota(jnp.int32, (NCH, NCH), 1)
    holder = lax.axis_index("chan") ^ (row // local_channels)
    source = holder * local_channels + row % local_channels
    order = jnp.where(channel == source, 1.0, 0.0)
    ordered = lax.dot_general(
        order,
        vectors,
        (((0,), (0,)), ((), ())),
        precision=lax.Precision.HIGHEST,
        preferred_element_type=F32,
    )
    outer = lax.dot_general(
        vectors,
        ordered,
        ROWS_BY_ROWS,
        precision=lax.Precision.HIGHEST,
        preferred_element_type=F32,
    )
    high, middle, low = pieces(order - outer)
    none = jnp.zeros((NCH, NCH), BF16)
    project_ref[0:NCH, :] = jnp.concatenate([high, high, high], axis=1)
    project_ref[NCH : 2 * NCH, :] = jnp.concatenate([middle, middle, none], axis=1)
    project_ref[2 * NCH : 3 * NCH, :] = jnp.concatenate([low, none, none], axis=1)
    copies[1].wait()
    for code in range(NBR):
        table = held_bins[code]
        for level in range(NBIN):
            mask_ref[code, :, level * TILE : (level + 1) * TILE] = jnp.where(
                table == level, 1.0, 0.0
            ).astype(BF16)
    for copy in copies[2:]:
        copy.wait()
    for tile in range(TA * TB):
        count = held_counts[tile % TB, tile // TB]
        codes = jnp.zeros((), jnp.int32)
        for slot in range(NBR):
            code = held_neighbours[tile // TB, tile % TB, slot]
            codes = codes | jnp.where(slot < count, jnp.int32(1) << code, 0)
        for code in range(NBR):
            live = ((codes >> code) & 1).astype(F32)
            live_ref[code, tile] = jnp.full((16, TILE), live).astype(BF16)
        observed = jnp.where(count > 0, 1.0, 0.0)
        live_ref[NBR, tile] = jnp.full((16, TILE), observed).astype(BF16)


def clean_kernel(block_count, project_ref, weights_ref, live_ref, *refs):
    block_refs = refs[:block_count]
    cols_ref, near_ref, far_ref, cov_ref = refs[block_count:]
    chan_index = lax.axis_index("chan")
    side = lax.axis_index("patch") % 2
    start = pl.multiple_of(chan_index * REGION, ROW)
    weights = weights_ref[:, pl.ds(start, ROW + REGION + ROW)]
    project = project_ref[...]
    own, masked = [], []
    observed_tiles = jnp.zeros((1, TILE), F32)
    for row in range(EXT):
        lanes = slice(row * ROW, (row + 1) * ROW)
        maps = jnp.concatenate([ref[:, lanes] for ref in block_refs], axis=0)
        split = jnp.concatenate(pieces(maps), axis=0)
        product = jnp.dot(project, split, preferred_element_type=F32)
        cleaned = (product[2 * NCH :] + product[NCH : 2 * NCH]) + product[:NCH]
        weighted = (cleaned * weights[:, lanes]).astype(BF16)
        for col in range(TB):
            tile = weighted[:, col * TILE : (col + 1) * TILE]
            cols_ref[col, row * NCH : (row + 1) * NCH, :] = tile
            if 0 < row <= TA:
                observed = live_ref[NBR, (row - 1) * TB + col]
                observed_tiles = observed_tiles + observed[:1].astype(F32)
                own.append(tile)
                masked.append(tile * jnp.concatenate([observed] * (NCH // 16), axis=0))
    covariance = lax.dot_general(
        jnp.concatenate(masked, axis=1),
        jnp.concatenate(own, axis=1),
        ROWS_BY_ROWS,
        preferred_element_type=F32,
    )
    total = jnp.broadcast_to(observed_tiles[:, :NCH] * float(TILE), (NCH, NCH))
    cov_ref[...] = jnp.concatenate([covariance, total], axis=1)

    rows = lax.broadcasted_iota(jnp.int32, (16, TILE), 0)
    for col in range(TB):
        weight_rows = jnp.zeros((16, TILE), F32)
        for row in range(EXT):
            at = row * ROW + col * TILE
            weight_rows = jnp.where(rows == row, weights[:, at : at + TILE], weight_rows)
        cols_ref[col, WROW:COLH, :] = weight_rows.astype(BF16)
    near_ref[...] = cols_ref[1 - side]
    far_ref[...] = cols_ref[side]


def add_pairs(code, row_shift, live_ref, centres, partners, mask_ref):
    own = slice(NCH, (TA + 1) * NCH)
    left = jnp.concatenate(
        [column[own] for column in centres] + [column[WROW:] for column in centres], axis=0
    )
    binned = jnp.dot(left, mask_ref[code], preferred_element_type=F32).astype(BF16)
    rows = lax.broadcasted_iota(jnp.int32, (16, TILE), 0)
    right = []
    weight_sums = [jnp.zeros((16, TILE), F32) for _ in range(NBIN)]
    for col in range(TB):
        partner_weights = partners[col][WROW:].astype(F32)
        shifted = jnp.zeros((16, TILE), F32)
        for row in range(TA):
            live = live_ref[code, row * TB + col]
            place = row + row_shift
            tile = partners[col][place * NCH : (place + 1) * NCH]
            right.append(tile * jnp.concatenate([live] * (NCH // 16), axis=0))
            weight = partner_weights[place : place + 1] * live.astype(F32)[:1]
            shifted = jnp.where(rows == row + 1, weight, shifted)
        first = TA * TB * NCH + col * 16
        for level in range(NBIN):
            lanes = slice(level * TILE, (level + 1) * TILE)
            weight_sums[level] += binned[first : first + 16, lanes].astype(F32) * shifted
    right = jnp.concatenate(right, axis=1)
    left = jnp.concatenate(
        [
            jnp.concatenate(
                [
                    binned[at * NCH : (at + 1) * NCH, level * TILE : (level + 1) * TILE]
                    for at in range(TA * TB)
                ],
                axis=1,
            )
            for level in range(NBIN)
        ],
        axis=0,
    )
    sums = lax.dot_general(left, right, ROWS_BY_ROWS, preferred_element_type=F32)
    return sums, weight_sums


def pair_kernel(jobs, first, live_ref, mask_ref, cols_ref, *refs):
    halo_refs = {}
    for name in ("near", "far"):
        if any(kind == name for kind, _ in jobs):
            halo_refs[name], *refs = refs
    if not first:
        sums_in_ref, weight_in_ref, *refs = refs
    sums_ref, weight_sums_ref, none_ref = refs
    none_ref[...] = jnp.zeros_like(none_ref)
    even = lax.axis_index("patch") % 2 == 0
    columns = [cols_ref[col] for col in range(TB)]
    for number, (kind, row_shift) in enumerate(jobs):
        if kind == "own":
            code, partners = 3 * row_shift + 1, columns
        else:
            beside = halo_refs[kind][...]
            after = even if kind == "near" else jnp.logical_not(even)
            code = jnp.where(after, 3 * row_shift + 2, 3 * row_shift)
            partners = [
                jnp.where(after, columns[1], beside),
                jnp.where(after, beside, columns[0]),
            ]
        sums, weight_sums = add_pairs(code, row_shift, live_ref, columns, partners, mask_ref)
        if number:
            sums_ref[...] += sums
        else:
            sums_ref[...] = sums if first else sums_in_ref[...] + sums
        for level in range(NBIN):
            if number:
                weight_sums_ref[level] += weight_sums[level]
            elif first:
                weight_sums_ref[level] = weight_sums[level]
            else:
                weight_sums_ref[level] = weight_in_ref[level] + weight_sums[level]


def scale_kernel(sums_ref, weight_sums_ref, *refs):
    *piece_refs, corr_ref, cov_ref = refs
    whole = piece_refs[0][...]
    for ref in piece_refs[1:]:
        whole = whole + ref[...]
    covariance = whole[:, :NCH] / whole[:, NCH:]
    cov_ref[...] = covariance
    channel = lax.broadcasted_iota(jnp.int32, (NCH, NCH), 0)
    other = lax.broadcasted_iota(jnp.int32, (NCH, NCH), 1)
    diagonal = jnp.where(channel == other, covariance, 0.0)
    spread_down = jnp.sqrt(jnp.sum(diagonal, axis=1, keepdims=True) + 1e-06)
    spread_across = jnp.sqrt(jnp.sum(diagonal, axis=0, keepdims=True) + 1e-06)
    norm_scale = spread_down * spread_across
    for level in range(NBIN):
        taper = 0.75 + 0.25 * math.cos(math.pi * level / NBIN)
        total = jnp.sum(
            jnp.sum(weight_sums_ref[level], axis=1, keepdims=True), axis=0, keepdims=True
        )
        pair_weight = jnp.maximum(total, 1.0)
        sums = sums_ref[level * NCH : (level + 1) * NCH]
        corr_ref[level] = (taper * sums) / (pair_weight * norm_scale)


def run(kernel, outs, args, scratch=(), spec=VMEM):
    if spec is HBM:
        args = [pltpu.with_memory_space_constraint(arg, pltpu.HBM) for arg in args]
    return pl.pallas_call(
        kernel,
        out_shape=outs,
        in_specs=[spec] * len(args),
        out_specs=jax.tree.map(lambda _: VMEM, outs),
        scratch_shapes=list(scratch),
        compiler_params=pltpu.CompilerParams(vmem_limit_bytes=24 * 2**20),
    )(*args)


def exchange(x, axis, step):
    count = lax.axis_size(axis)
    return lax.ppermute(x, axis, [(i, i ^ step) for i in range(count)])


def per_device(sky_maps, mode_vectors, pixel_weight, neighbours, tile_counts, pair_bins):
    shape = jax.ShapeDtypeStruct
    chan_count = lax.axis_size("chan")
    patch_count = lax.axis_size("patch")
    local_channels, pixels = sky_maps.shape

    counts = tile_counts.T
    block = shape((local_channels, ROW + REGION + ROW), F32)
    blocks = run(
        prepare_kernel,
        (block,) * chan_count,
        [sky_maps],
        scratch=[pltpu.VMEM((local_channels, pixels), F32), pltpu.SemaphoreType.DMA],
        spec=HBM,
    )
    blocks = [blocks[0]] + [exchange(blocks[s], "chan", s) for s in range(1, chan_count)]
    if local_channels % 16:
        blocks = [jnp.concatenate(blocks, axis=0)]
    project, weights, mask, live = run(
        lambda *refs: setting_kernel(local_channels, *refs),
        (
            shape((3 * NCH, 3 * NCH), BF16),
            shape((1, pixels + 2 * TB * TILE), F32),
            shape((NBR, TILE, NBIN * TILE), BF16),
            shape((NBR + 1, TA * TB, 16, TILE), BF16),
        ),
        [counts, neighbours, mode_vectors.T, pixel_weight.reshape(1, pixels), pair_bins],
        scratch=[
            pltpu.SMEM((TB, TA), jnp.int32),
            pltpu.SMEM((TA, TB, NBR), jnp.int32),
            pltpu.VMEM((MODES, NCH), F32),
            pltpu.VMEM((NBR, TILE, TILE), jnp.int32),
            pltpu.SemaphoreType.DMA((5,)),
        ],
        spec=HBM,
    )

    column = shape((COLH, TILE), BF16)
    piece_shape = shape((NCH, 2 * NCH), F32)
    cols, near, far, piece = run(
        lambda *refs: clean_kernel(len(blocks), *refs),
        (shape((TB, COLH, TILE), BF16), column, column, piece_shape),
        [project, weights, live] + blocks,
    )

    core_piece = exchange(piece, "patch", 1)
    halos = {"near": exchange(near, "patch", 1)}
    far_pairs = [(i, i + 1) for i in range(1, patch_count - 1, 2)]
    halos["far"] = lax.ppermute(far, "patch", far_pairs + [(j, i) for i, j in far_pairs])
    piece = piece + core_piece
    rounds = []
    for axis, stride, count in (("patch", 2, patch_count), ("chan", 1, chan_count)):
        while stride < count:
            group = min(4, count // stride)
            rounds.append((axis, [stride * k for k in range(1, group)]))
            stride *= group
    jobs = [(kind, row_shift) for kind in ("own", "near", "far") for row_shift in range(3)]
    cuts = [jobs[:4], jobs[4:]]
    sums = ()
    for number, (axis, steps) in enumerate(rounds):
        parts = [piece] + [exchange(piece, axis, step) for step in steps]
        none = []
        if number < len(cuts):
            kinds = [kind for kind in halos if any(kind == job[0] for job in cuts[number])]
            *sums, zeros = run(
                lambda *refs: pair_kernel(cuts[number], not number, *refs),
                (shape((NBIN * NCH, NCH), F32), shape((NBIN, 16, TILE), F32), piece_shape),
                [live, mask, cols] + [halos[kind] for kind in kinds] + list(sums),
            )
            none = [zeros]
        if number < len(rounds) - 1:
            piece = sum(parts[1:] + none, parts[0])
    correlation, covariance = run(
        scale_kernel,
        (shape((NBIN, NCH, NCH), F32), shape((NCH, NCH), F32)),
        [*sums, *parts],
    )
    return (correlation[None, None], covariance)


def solution(mesh):
    return jax.shard_map(
        per_device,
        mesh=mesh,
        in_specs=(
            P("chan", "patch"),
            P(),
            P("patch"),
            P("chan", "patch", None),
            P("chan", "patch"),
            P(),
        ),
        out_specs=(P("chan", "patch", None, None, None), P()),
        check_vma=False,
    )
```

time: 30.6 us -> 29.4 us (0.961)
  local copies, waits for them, and re-layouts: 4.74 us -> 0 us
  starting transfers between devices: 10.6 us -> 13.7 us
  Pallas kernels: 8.91 us -> 10.1 us
  waiting for transfers between devices: 5.22 us -> 4.67 us
    unnamed x12 -> x0, local copies, waits for them, and re-layouts: 4.74 us -> none
    ppermute x6 -> x11, starting transfers between devices: 9.99 us -> 13.1 us  [exchange(): return lax.ppermute(x, axis, [(i, i ^ step) for i in range(count)])]
    pallas_call x5 -> x6, Pallas kernels: 8.35 us -> 10.1 us  [run(): pl.pallas_call(kernel, out_shape=outs, in_specs=[spec] * len(args), out_s...]
    pallas_call x1 -> x0, Pallas kernels: 0.56 us -> none  [per_device(): pl.pallas_call(prepare_kernel, out_shape=shape((local_channels, pixels +...]
    ppermute x6 -> x11, waiting for transfers between devices: 5.22 us -> 4.67 us  [exchange(): return lax.ppermute(x, axis, [(i, i ^ step) for i in range(count)])]
  transfers between devices with their start and end apart: 7 -> 12, of which waited for: 4 -> 4; matrix products, arithmetic and copies ran while one was open for 0% -> 0% of each run, Pallas kernels for 22% -> 27%
where the time goes in v3:
time: 29.4 us; the launch traced here: 29.2 us
  starting transfers between devices  13.7 us (47%)
  Pallas kernels  10.1 us (34%)
  waiting for transfers between devices  4.67 us (16%)
  between operations  0.71 us (2%)
    ppermute x11, starting transfers between devices, exchange(): return lax.ppermute(x, axis, [(i, i ^ step) for i in range(count)])  13.1 us
    pallas_call x6, Pallas kernels, run(): pl.pallas_call(kernel, out_shape=outs, in_specs=[spec] * len(args), out_s...  10.1 us
    ppermute x11, waiting for transfers between devices, exchange(): return lax.ppermute(x, axis, [(i, i ^ step) for i in range(count)])  4.67 us
    ppermute x1, starting transfers between devices, per_device(): lax.ppermute(far, 'patch', far_pairs + [(j, i) for i, j in far_pairs])  0.65 us
  transfers between devices with their start and end apart: 12, of which 4 were waited for; matrix products, arithmetic and copies ran while one was open for 0% of the time, Pallas kernels for 27%

profile of v3, /device:TPU:0, one launch (start us, length us, event | category | flops | bytes accessed | tf_op | source)
XLA Modules:
  0.0 29.2 jit_solution(14644223734560351238)
XLA Ops:
  0.6 1.0 %shard_map.78 = (f32[16,1280]{1,0:T(8,128)S(1)}, f32[16,1280]{1,0:T(8,128)S(1)}, f32[16,1280]{1,0:T(8,128)S(1)}, f32[16,1280]{1,0:T(8,128)S(1)}) custom-call(f32[16,3072]{1,0:T(8,128)} %maps_ref.1), custom_call_target="tpu_custom_call" | custom-call | tf_op jit(solution)/shard_map/pallas_call | solution.py:295
  1.6 3.0 %collective-permute-start = (f32[16,1280]{1,0:T(8,128)S(1)}, f32[16,1280]{1,0:T(8,128)S(1)}, u32[]{:S(2)}, u32[]{:S(2)}) collective-permute-start(f32[16,1280]{1,0:T(8,128)S(1)} %get-tuple-element.26), channel_id=1, source_target_pairs={{0,8},{8,0},{16,24},{24,16},{1,9},{9,1},{17,25},{25,17},{2,10},{10... | collective-permute-start | bytes 245768 | tf_op jit(solution)/shard_map/ppermute | solution.py:307
  4.6 1.5 %collective-permute-start.1 = (f32[16,1280]{1,0:T(8,128)S(1)}, f32[16,1280]{1,0:T(8,128)S(1)}, u32[]{:S(2)}, u32[]{:S(2)}) collective-permute-start(f32[16,1280]{1,0:T(8,128)S(1)} %get-tuple-element.27), channel_id=1, source_target_pairs={{0,16},{8,24},{16,0},{24,8},{1,17},{9,25},{17,1},{25,9},{2,18},{10... | collective-permute-start | bytes 245768 | tf_op jit(solution)/shard_map/ppermute | solution.py:307
  6.1 0.0 collective-permute-start.2
  6.1 2.9 %shard_map.77 = (bf16[192,192]{1,0:T(8,128)(2,1)S(1)}, f32[1,3584]{1,0:T(1,128)S(1)}, bf16[9,128,1024]{2,1,0:T(8,128)(2,1)S(1)}, bf16[10,6,16,128]{3,2,1,0:T(8,128)(2,1)S(1)}) custom-call(s32[2,3]{1,0:T(2,128)} %bitcast.6, s32[3,2,9]{2,1,0:T(2,128)} %refs_1_.1, f32[8,64]{1,0:T(8,128)} %bitcast.5, f32[1,3072]{1,0:T(1,128)} %bitcast.4, s32[9,128,128]{2,1,0:T(8,128)} %refs_4_.1), custom_call_target="tpu_custom_call" | custom-call | tf_op jit(solution)/shard_map/pallas_call | solution.py:295
  9.1 0.0 collective-permute-done.refs_4_
  9.1 0.9 %collective-permute-done.1.refs_5_ = f32[16,1280]{1,0:T(8,128)S(1)} collective-permute-done((f32[16,1280]{1,0:T(8,128)S(1)}, f32[16,1280]{1,0:T(8,128)S(1)}, u32[]{:S(2)}, u32[]{:S(2)}) %collective-permute-start.1) | collective-permute-done | bytes 81952 | tf_op jit(solution)/shard_map/ppermute | solution.py:307
  9.9 1.5 %collective-permute-done.2.refs_6_ = f32[16,1280]{1,0:T(8,128)S(1)} collective-permute-done((f32[16,1280]{1,0:T(8,128)S(1)}, f32[16,1280]{1,0:T(8,128)S(1)}, u32[]{:S(2)}, u32[]{:S(2)}) %collective-permute-start.2) | collective-permute-done | bytes 81952 | tf_op jit(solution)/shard_map/ppermute | solution.py:307
  11.5 0.4 %shard_map.79 = (bf16[2,336,128]{2,1,0:T(8,128)(2,1)S(1)}, bf16[336,128]{1,0:T(8,128)(2,1)S(1)}, bf16[336,128]{1,0:T(8,128)(2,1)S(1)}, f32[64,128]{1,0:T(8,128)S(1)}) custom-call(bf16[192,192]{1,0:T(8,128)(2,1)S(1)} %get-tuple-element.23.refs_0_, f32[1,3584]{1,0:T(1,128)S(1)} %get-tuple-element.24.refs_1_, ...), custom_call_target="tpu_custom_call" | custom-call | tf_op jit(solution)/shard_map/pallas_call | solution.py:295
  11.9 0.1 collective-permute-start.3
  12.0 0.5 %collective-permute-start.5 = (f32[64,128]{1,0:T(8,128)S(1)}, f32[64,128]{1,0:T(8,128)S(1)}, u32[]{:S(2)}, u32[]{:S(2)}) collective-permute-start(f32[64,128]{1,0:T(8,128)S(1)} %get-tuple-element.36), channel_id=1, source_target_pairs={{0,1},{1,0},{2,3},{3,2},{4,5},{5,4},{6,7},{7,6},{8,9},{9,8},{10,11... | collective-permute-start | bytes 98312 | tf_op jit(solution)/shard_map/ppermute | solution.py:307
  12.5 0.9 %collective-permute-done.5 = f32[64,128]{1,0:T(8,128)S(1)} collective-permute-done((f32[64,128]{1,0:T(8,128)S(1)}, f32[64,128]{1,0:T(8,128)S(1)}, u32[]{:S(2)}, u32[]{:S(2)}) %collective-permute-start.5) | collective-permute-done | bytes 32800 | tf_op jit(solution)/shard_map/ppermute | solution.py:307
  13.3 3.6 %collective-permute-start.8 = (f32[64,128]{1,0:T(8,128)S(1)}, f32[64,128]{1,0:T(8,128)S(1)}, u32[]{:S(2)}, u32[]{:S(2)}) collective-permute-start(f32[64,128]{1,0:T(8,128)S(1)} %add.15), channel_id=1, source_target_pairs={{0,6},{1,7},{2,4},{3,5},{4,2},{5,3},{6,0},{7,1},{8,14},{9,15},{10,... | collective-permute-start | bytes 98312 | tf_op jit(solution)/shard_map/ppermute | solution.py:307
  16.9 0.0 collective-permute-start.7
  16.9 0.8 %collective-permute-start.6 = (f32[64,128]{1,0:T(8,128)S(1)}, f32[64,128]{1,0:T(8,128)S(1)}, u32[]{:S(2)}, u32[]{:S(2)}) collective-permute-start(f32[64,128]{1,0:T(8,128)S(1)} %add.15), channel_id=1, source_target_pairs={{0,2},{1,3},{2,0},{3,1},{4,6},{5,7},{6,4},{7,5},{8,10},{9,11},{10,... | collective-permute-start | bytes 98312 | tf_op jit(solution)/shard_map/ppermute | solution.py:307
  17.7 0.7 %collective-permute-start.4 = (bf16[336,128]{1,0:T(8,128)(2,1)S(1)}, bf16[336,128]{1,0:T(8,128)(2,1)S(1)}, u32[]{:S(2)}, u32[]{:S(2)}) collective-permute-start(bf16[336,128]{1,0:T(8,128)(2,1)S(1)} %get-tuple-element.31), channel_id=1, source_target_pairs={{1,2},{3,4},{5,6},{2,1},{4,3},{6,5},{9,10},{11,12},{13,14},{10,9},... | collective-permute-start | bytes 258056 | tf_op jit(solution)/shard_map/ppermute | solution.py:358
  18.4 0.0 collective-permute-done.3.refs_3_
  18.4 1.9 %shard_map.80 = (f32[512,64]{1,0:T(8,128)S(1)}, f32[8,16,128]{2,1,0:T(8,128)S(1)}, f32[64,128]{1,0:T(8,128)S(1)}) custom-call(bf16[10,6,16,128]{3,2,1,0:T(8,128)(2,1)S(1)} %get-tuple-element.21.refs_2_.refs_0_, bf16[9,128,1024]{2,1,0:T(8,128)(2,1)S(1)} %get-tuple-element.22.refs_1_, bf16[2,336,128]{2,1,0:T(8,128)(2,1)S(1)} %get-tuple-element.29.refs_2_, ...), custom_call_target="tpu_custom_call" | custom-call | tf_op jit(solution)/shard_map/pallas_call | solution.py:295
  20.3 0.0 collective-permute-done.8
  20.3 1.4 %collective-permute-done.7 = f32[64,128]{1,0:T(8,128)S(1)} collective-permute-done((f32[64,128]{1,0:T(8,128)S(1)}, f32[64,128]{1,0:T(8,128)S(1)}, u32[]{:S(2)}, u32[]{:S(2)}) %collective-permute-start.7) | collective-permute-done | bytes 32800 | tf_op jit(solution)/shard_map/ppermute | solution.py:307
  21.7 0.0 collective-permute-done.6
  21.8 0.8 %collective-permute-start.11 = (f32[64,128]{1,0:T(8,128)S(1)}, f32[64,128]{1,0:T(8,128)S(1)}, u32[]{:S(2)}, u32[]{:S(2)}) collective-permute-start(f32[64,128]{1,0:T(8,128)S(1)} %add_add_fusion.refs_0_), channel_id=1, source_target_pairs={{0,24},{8,16},{16,8},{24,0},{1,25},{9,17},{17,9},{25,1},{2,26},{10... | collective-permute-start | bytes 98312 | tf_op jit(solution)/shard_map/ppermute | solution.py:307
  22.5 1.3 %collective-permute-start.10 = (f32[64,128]{1,0:T(8,128)S(1)}, f32[64,128]{1,0:T(8,128)S(1)}, u32[]{:S(2)}, u32[]{:S(2)}) collective-permute-start(f32[64,128]{1,0:T(8,128)S(1)} %add_add_fusion.refs_0_), channel_id=1, source_target_pairs={{0,16},{8,24},{16,0},{24,8},{1,17},{9,25},{17,1},{25,9},{2,18},{10... | collective-permute-start | bytes 98312 | tf_op jit(solution)/shard_map/ppermute | solution.py:307
  23.8 1.5 %collective-permute-start.9 = (f32[64,128]{1,0:T(8,128)S(1)}, f32[64,128]{1,0:T(8,128)S(1)}, u32[]{:S(2)}, u32[]{:S(2)}) collective-permute-start(f32[64,128]{1,0:T(8,128)S(1)} %add_add_fusion.refs_0_), channel_id=1, source_target_pairs={{0,8},{8,0},{16,24},{24,16},{1,9},{9,1},{17,25},{25,17},{2,10},{10... | collective-permute-start | bytes 98312 | tf_op jit(solution)/shard_map/ppermute | solution.py:307
  25.3 0.0 collective-permute-done.4.refs_4_
  25.3 2.9 %shard_map.81 = (f32[512,64]{1,0:T(8,128)S(1)}, f32[8,16,128]{2,1,0:T(8,128)S(1)}, f32[64,128]{1,0:T(8,128)}) custom-call(bf16[10,6,16,128]{3,2,1,0:T(8,128)(2,1)S(1)} %get-tuple-element.21.refs_2_.refs_0_, bf16[9,128,1024]{2,1,0:T(8,128)(2,1)S(1)} %get-tuple-element.22.refs_1_, bf16[2,336,128]{2,1,0:T(8,128)(2,1)S(1)} %get-tuple-element.29.refs_2_, ...), custom_call_target="tpu_custom_call" | custom-call | tf_op jit(solution)/shard_map/pallas_call | solution.py:295
  28.2 0.0 collective-permute-done.11.refs_3_
  28.2 0.0 collective-permute-done.10.refs_2_
  28.2 0.0 collective-permute-done.9.refs_1_
  28.2 0.9 %shard_map.82 = (f32[8,64,64]{2,1,0:T(8,128)}, f32[64,64]{1,0:T(8,128)}) custom-call(f32[512,64]{1,0:T(8,128)S(1)} %get-tuple-element.34.sums_ref, f32[8,16,128]{2,1,0:T(8,128)S(1)} %get-tuple-element.35.weight_sums_ref, f32[64,128]{1,0:T(8,128)S(1)} %add_add_fusion.refs_0_, f32[64,128]{1,0:T(8,128)S(1)} %collective-permute-done.9.refs_1_, ...), custom_call_target="tpu_custom_call" | custom-call | tf_op jit(solution)/shard_map/pallas_call | solution.py:295
  (2 shorter events, 0.0 us)
Async XLA Ops:
  1.6 7.5 %collective-permute-start = (f32[16,1280]{1,0:T(8,128)S(1)}, f32[16,1280]{1,0:T(8,128)S(1)}, u32[]{:S(2)}, u32[]{:S(2)}) collective-permute-start(f32[16,1280]{1,0:T(8,128)S(1)} %get-tuple-element.26), channel_id=1, source_target_pairs={{0,8},{8,0},{16,24},{24,16},{1,9},{9,1},{17,25},{25,17},{2,10},{10... | collective-permute-start | bytes 245768 | tf_op jit(solution)/shard_map/ppermute | solution.py:307
  4.6 5.3 %collective-permute-start.1 = (f32[16,1280]{1,0:T(8,128)S(1)}, f32[16,1280]{1,0:T(8,128)S(1)}, u32[]{:S(2)}, u32[]{:S(2)}) collective-permute-start(f32[16,1280]{1,0:T(8,128)S(1)} %get-tuple-element.27), channel_id=1, source_target_pairs={{0,16},{8,24},{16,0},{24,8},{1,17},{9,25},{17,1},{25,9},{2,18},{10... | collective-permute-start | bytes 245768 | tf_op jit(solution)/shard_map/ppermute | solution.py:307
  6.1 5.3 %collective-permute-start.2 = (f32[16,1280]{1,0:T(8,128)S(1)}, f32[16,1280]{1,0:T(8,128)S(1)}, u32[]{:S(2)}, u32[]{:S(2)}) collective-permute-start(f32[16,1280]{1,0:T(8,128)S(1)} %get-tuple-element.28), channel_id=1, source_target_pairs={{0,24},{8,16},{16,8},{24,0},{1,25},{9,17},{17,9},{25,1},{2,26},{10... | collective-permute-start | bytes 245768 | tf_op jit(solution)/shard_map/ppermute | solution.py:307
  11.9 6.5 %collective-permute-start.3 = (bf16[336,128]{1,0:T(8,128)(2,1)S(1)}, bf16[336,128]{1,0:T(8,128)(2,1)S(1)}, u32[]{:S(2)}, u32[]{:S(2)}) collective-permute-start(bf16[336,128]{1,0:T(8,128)(2,1)S(1)} %get-tuple-element.30), channel_id=1, source_target_pairs={{0,1},{1,0},{2,3},{3,2},{4,5},{5,4},{6,7},{7,6},{8,9},{9,8},{10,11... | collective-permute-start | bytes 258056 | tf_op jit(solution)/shard_map/ppermute | solution.py:307
  12.0 1.4 %collective-permute-start.5 = (f32[64,128]{1,0:T(8,128)S(1)}, f32[64,128]{1,0:T(8,128)S(1)}, u32[]{:S(2)}, u32[]{:S(2)}) collective-permute-start(f32[64,128]{1,0:T(8,128)S(1)} %get-tuple-element.36), channel_id=1, source_target_pairs={{0,1},{1,0},{2,3},{3,2},{4,5},{5,4},{6,7},{7,6},{8,9},{9,8},{10,11... | collective-permute-start | bytes 98312 | tf_op jit(solution)/shard_map/ppermute | solution.py:307
  13.3 7.0 %collective-permute-start.8 = (f32[64,128]{1,0:T(8,128)S(1)}, f32[64,128]{1,0:T(8,128)S(1)}, u32[]{:S(2)}, u32[]{:S(2)}) collective-permute-start(f32[64,128]{1,0:T(8,128)S(1)} %add.15), channel_id=1, source_target_pairs={{0,6},{1,7},{2,4},{3,5},{4,2},{5,3},{6,0},{7,1},{8,14},{9,15},{10,... | collective-permute-start | bytes 98312 | tf_op jit(solution)/shard_map/ppermute | solution.py:307
  16.9 4.8 %collective-permute-start.7 = (f32[64,128]{1,0:T(8,128)S(1)}, f32[64,128]{1,0:T(8,128)S(1)}, u32[]{:S(2)}, u32[]{:S(2)}) collective-permute-start(f32[64,128]{1,0:T(8,128)S(1)} %add.15), channel_id=1, source_target_pairs={{0,4},{1,5},{2,6},{3,7},{4,0},{5,1},{6,2},{7,3},{8,12},{9,13},{10,... | collective-permute-start | bytes 98312 | tf_op jit(solution)/shard_map/ppermute | solution.py:307
  16.9 4.8 %collective-permute-start.6 = (f32[64,128]{1,0:T(8,128)S(1)}, f32[64,128]{1,0:T(8,128)S(1)}, u32[]{:S(2)}, u32[]{:S(2)}) collective-permute-start(f32[64,128]{1,0:T(8,128)S(1)} %add.15), channel_id=1, source_target_pairs={{0,2},{1,3},{2,0},{3,1},{4,6},{5,7},{6,4},{7,5},{8,10},{9,11},{10,... | collective-permute-start | bytes 98312 | tf_op jit(solution)/shard_map/ppermute | solution.py:307
  17.7 7.6 %collective-permute-start.4 = (bf16[336,128]{1,0:T(8,128)(2,1)S(1)}, bf16[336,128]{1,0:T(8,128)(2,1)S(1)}, u32[]{:S(2)}, u32[]{:S(2)}) collective-permute-start(bf16[336,128]{1,0:T(8,128)(2,1)S(1)} %get-tuple-element.31), channel_id=1, source_target_pairs={{1,2},{3,4},{5,6},{2,1},{4,3},{6,5},{9,10},{11,12},{13,14},{10,9},... | collective-permute-start | bytes 258056 | tf_op jit(solution)/shard_map/ppermute | solution.py:358
  21.8 6.5 %collective-permute-start.11 = (f32[64,128]{1,0:T(8,128)S(1)}, f32[64,128]{1,0:T(8,128)S(1)}, u32[]{:S(2)}, u32[]{:S(2)}) collective-permute-start(f32[64,128]{1,0:T(8,128)S(1)} %add_add_fusion.refs_0_), channel_id=1, source_target_pairs={{0,24},{8,16},{16,8},{24,0},{1,25},{9,17},{17,9},{25,1},{2,26},{10... | collective-permute-start | bytes 98312 | tf_op jit(solution)/shard_map/ppermute | solution.py:307
  22.5 5.7 %collective-permute-start.10 = (f32[64,128]{1,0:T(8,128)S(1)}, f32[64,128]{1,0:T(8,128)S(1)}, u32[]{:S(2)}, u32[]{:S(2)}) collective-permute-start(f32[64,128]{1,0:T(8,128)S(1)} %add_add_fusion.refs_0_), channel_id=1, source_target_pairs={{0,16},{8,24},{16,0},{24,8},{1,17},{9,25},{17,1},{25,9},{2,18},{10... | collective-permute-start | bytes 98312 | tf_op jit(solution)/shard_map/ppermute | solution.py:307
  23.8 4.4 %collective-permute-start.9 = (f32[64,128]{1,0:T(8,128)S(1)}, f32[64,128]{1,0:T(8,128)S(1)}, u32[]{:S(2)}, u32[]{:S(2)}) collective-permute-start(f32[64,128]{1,0:T(8,128)S(1)} %add_add_fusion.refs_0_), channel_id=1, source_target_pairs={{0,8},{8,0},{16,24},{24,16},{1,9},{9,1},{17,25},{25,17},{2,10},{10... | collective-permute-start | bytes 98312 | tf_op jit(solution)/shard_map/ppermute | solution.py:307

commit v4 on v3

--- a/solution.py
+++ b/solution.py
@@ -14,11 +14,12 @@
 NBR = 9
 TA = 3
 TB = 2
+HALF = NCH // 2
 EXT = TA + 2
 WROW = EXT * NCH
 COLH = WROW + 16
 ROW = TB * TILE
-REGION = TA * ROW
+SPAN = 2 * TA + 1
 
 F32 = jnp.float32
 BF16 = jnp.bfloat16
@@ -35,22 +36,38 @@
     return high, middle, low
 
 
-def prepare_kernel(maps_ref, *refs):
-    *block_refs, held, copied = refs
+def first_row(chan_index):
+    return (chan_index - chan_index % 2) * TA - 1 + chan_index % 2
+
+
+def prepare_kernel(counts_ref, maps_ref, *refs):
+    *block_refs, held_counts, held, copied = refs
     chan_index = lax.axis_index("chan")
-    last = len(block_refs) - 1
-    pixels = maps_ref.shape[1]
-    copy = pltpu.make_async_copy(maps_ref, held, copied)
+    local_channels, pixels = maps_ref.shape
+    rows = pixels // ROW
+    count_copy = pltpu.make_async_copy(counts_ref, held_counts, copied.at[0])
+    copy = pltpu.make_async_copy(maps_ref, held, copied.at[1])
+    count_copy.start()
     copy.start()
+    flag_ref = block_refs[1]
+    flag_ref[:, SPAN * ROW :] = jnp.zeros((local_channels, flag_ref.shape[1] - SPAN * ROW), F32)
+    count_copy.wait()
+    for tile in range(TA * TB):
+        observed = jnp.where(held_counts[tile % TB, tile // TB] > 0, 1.0, 0.0)
+        row, lane = tile % local_channels, SPAN * ROW + tile // local_channels * TILE
+        flag_ref[row : row + 1, lane : lane + TILE] = jnp.full((1, TILE), observed)
     copy.wait()
     for step, ref in enumerate(block_refs):
-        holder = chan_index ^ step
-        start = pl.multiple_of(holder * REGION, ROW)
-        above = pl.multiple_of(jnp.maximum(start - ROW, 0), ROW)
-        below = pl.multiple_of(jnp.minimum(start + REGION, pixels - ROW), ROW)
-        ref[:, :ROW] = jnp.where(holder > 0, held[:, pl.ds(above, ROW)], 0.0)
-        ref[:, ROW : ROW + REGION] = held[:, pl.ds(start, REGION)]
-        ref[:, ROW + REGION :] = jnp.where(holder < last, held[:, pl.ds(below, ROW)], 0.0)
+        first = first_row(chan_index ^ step)
+        last = first + SPAN - 1
+        above = pl.multiple_of(jnp.maximum(first, 0) * ROW, ROW)
+        middle = pl.multiple_of((first + 1) * ROW, ROW)
+        below = pl.multiple_of(jnp.minimum(last, rows - 1) * ROW, ROW)
+        ref[:, :ROW] = jnp.where(first >= 0, held[:, pl.ds(above, ROW)], 0.0)
+        ref[:, ROW : (SPAN - 1) * ROW] = held[:, pl.ds(middle, (SPAN - 2) * ROW)]
+        ref[:, (SPAN - 1) * ROW : SPAN * ROW] = jnp.where(
+            last < rows, held[:, pl.ds(below, ROW)], 0.0
+        )
 
 
 def setting_kernel(
@@ -146,15 +163,18 @@
 
 def clean_kernel(block_count, project_ref, weights_ref, live_ref, *refs):
     block_refs = refs[:block_count]
-    cols_ref, near_ref, far_ref, cov_ref = refs[block_count:]
+    *flag_refs, cols_ref, near_ref, far_ref, cov_ref, tiles_ref = refs[block_count:]
+    if flag_refs:
+        flags = flag_refs[0][...]
+    else:
+        flags = block_refs[1][:8, SPAN * ROW :]
     chan_index = lax.axis_index("chan")
+    place = chan_index % 2
     side = lax.axis_index("patch") % 2
-    start = pl.multiple_of(chan_index * REGION, ROW)
-    weights = weights_ref[:, pl.ds(start, ROW + REGION + ROW)]
+    start = pl.multiple_of((first_row(chan_index) + 1) * ROW, ROW)
+    weights = weights_ref[:, pl.ds(start, SPAN * ROW)]
     project = project_ref[...]
-    own, masked = [], []
-    observed_tiles = jnp.zeros((1, TILE), F32)
-    for row in range(EXT):
+    for row in range(SPAN):
         lanes = slice(row * ROW, (row + 1) * ROW)
         maps = jnp.concatenate([ref[:, lanes] for ref in block_refs], axis=0)
         split = jnp.concatenate(pieces(maps), axis=0)
@@ -162,28 +182,36 @@
         cleaned = (product[2 * NCH :] + product[NCH : 2 * NCH]) + product[:NCH]
         weighted = (cleaned * weights[:, lanes]).astype(BF16)
         for col in range(TB):
-            tile = weighted[:, col * TILE : (col + 1) * TILE]
-            cols_ref[col, row * NCH : (row + 1) * NCH, :] = tile
-            if 0 < row <= TA:
-                observed = live_ref[NBR, (row - 1) * TB + col]
-                observed_tiles = observed_tiles + observed[:1].astype(F32)
-                own.append(tile)
-                masked.append(tile * jnp.concatenate([observed] * (NCH // 16), axis=0))
+            tiles_ref[row, col] = weighted[:, col * TILE : (col + 1) * TILE]
+
+    both, masked = [], []
+    observed_tiles = jnp.zeros((1, TILE), F32)
+    for row in range(2 * TA):
+        for col in range(TB):
+            tile = row % TA * TB + col
+            own = live_ref[NBR, tile].astype(F32)[:1]
+            observed = jnp.where(place == row // TA, own, flags[tile : tile + 1])
+            observed_tiles = observed_tiles + observed
+            both.append(tiles_ref[row + 1 - place, col])
+            masked.append(both[-1] * jnp.broadcast_to(observed, (NCH, TILE)).astype(BF16))
+    both = jnp.concatenate(both, axis=1)
     covariance = lax.dot_general(
         jnp.concatenate(masked, axis=1),
-        jnp.concatenate(own, axis=1),
+        jnp.concatenate([both, both[HALF:], both[HALF:]], axis=0),
         ROWS_BY_ROWS,
         preferred_element_type=F32,
     )
-    total = jnp.broadcast_to(observed_tiles[:, :NCH] * float(TILE), (NCH, NCH))
-    cov_ref[...] = jnp.concatenate([covariance, total], axis=1)
+    lane = lax.broadcasted_iota(jnp.int32, (HALF, TILE), 1)
+    lower = jnp.where(lane < 3 * HALF, covariance[HALF:], observed_tiles * float(TILE))
+    cov_ref[...] = jnp.where(lane < NCH, covariance[:HALF], lower)
 
     rows = lax.broadcasted_iota(jnp.int32, (16, TILE), 0)
     for col in range(TB):
         weight_rows = jnp.zeros((16, TILE), F32)
         for row in range(EXT):
-            at = row * ROW + col * TILE
-            weight_rows = jnp.where(rows == row, weights[:, at : at + TILE], weight_rows)
+            cols_ref[col, row * NCH : (row + 1) * NCH, :] = tiles_ref[2 * place + row, col]
+            at = pl.multiple_of((chan_index * TA + row) * ROW + col * TILE, TILE)
+            weight_rows = jnp.where(rows == row, weights_ref[:, pl.ds(at, TILE)], weight_rows)
         cols_ref[col, WROW:COLH, :] = weight_rows.astype(BF16)
     near_ref[...] = cols_ref[1 - side]
     far_ref[...] = cols_ref[side]
@@ -271,7 +299,10 @@
     whole = piece_refs[0][...]
     for ref in piece_refs[1:]:
         whole = whole + ref[...]
-    covariance = whole[:, :NCH] / whole[:, NCH:]
+    lane = lax.broadcasted_iota(jnp.int32, (HALF, TILE), 1)
+    turned = jnp.concatenate([whole, jnp.zeros((TILE - HALF, TILE), F32)], axis=0).T
+    lower = jnp.where(lane < HALF, turned[HALF:NCH], pltpu.roll(whole, TILE - HALF, axis=1))
+    covariance = jnp.concatenate([whole, lower], axis=0)[:, :NCH] / whole[:1, TILE - 1 :]
     cov_ref[...] = covariance
     channel = lax.broadcasted_iota(jnp.int32, (NCH, NCH), 0)
     other = lax.broadcasted_iota(jnp.int32, (NCH, NCH), 1)
@@ -314,17 +345,31 @@
     local_channels, pixels = sky_maps.shape
 
     counts = tile_counts.T
-    block = shape((local_channels, ROW + REGION + ROW), F32)
+    flag_lanes = -(-TA * TB // local_channels) * TILE
+    block_shapes = [
+        shape((local_channels, SPAN * ROW + flag_lanes * (step == 1)), F32)
+        for step in range(chan_count)
+    ]
     blocks = run(
         prepare_kernel,
-        (block,) * chan_count,
-        [sky_maps],
-        scratch=[pltpu.VMEM((local_channels, pixels), F32), pltpu.SemaphoreType.DMA],
+        tuple(block_shapes),
+        [counts, sky_maps],
+        scratch=[
+            pltpu.SMEM((TB, TA), jnp.int32),
+            pltpu.VMEM((local_channels, pixels), F32),
+            pltpu.SemaphoreType.DMA((2,)),
+        ],
         spec=HBM,
     )
     blocks = [blocks[0]] + [exchange(blocks[s], "chan", s) for s in range(1, chan_count)]
+    flags = []
     if local_channels % 16:
-        blocks = [jnp.concatenate(blocks, axis=0)]
+        rows = [
+            blocks[1][t % local_channels, SPAN * ROW + t // local_channels * TILE :][:TILE]
+            for t in range(TA * TB)
+        ]
+        flags = [jnp.pad(jnp.stack(rows), ((0, 8 - TA * TB), (0, 0)))]
+        blocks = [jnp.concatenate([block[:, : SPAN * ROW] for block in blocks], axis=0)]
     project, weights, mask, live = run(
         lambda *refs: setting_kernel(local_channels, *refs),
         (
@@ -345,26 +390,26 @@
     )
 
     column = shape((COLH, TILE), BF16)
-    piece_shape = shape((NCH, 2 * NCH), F32)
+    piece_shape = shape((HALF, TILE), F32)
     cols, near, far, piece = run(
         lambda *refs: clean_kernel(len(blocks), *refs),
         (shape((TB, COLH, TILE), BF16), column, column, piece_shape),
-        [project, weights, live] + blocks,
-    )
-
-    core_piece = exchange(piece, "patch", 1)
+        [project, weights, live] + blocks + flags,
+        scratch=[pltpu.VMEM((SPAN, TB, NCH, TILE), BF16)],
+    )
+
     halos = {"near": exchange(near, "patch", 1)}
-    far_pairs = [(i, i + 1) for i in range(1, patch_count - 1, 2)]
+    far_pairs = [(i, (i + 1) % patch_count) for i in range(1, patch_count, 2)]
     halos["far"] = lax.ppermute(far, "patch", far_pairs + [(j, i) for i, j in far_pairs])
-    piece = piece + core_piece
-    rounds = []
-    for axis, stride, count in (("patch", 2, patch_count), ("chan", 1, chan_count)):
+    rounds = [("patch", [1])]
+    for axis, count in (("patch", patch_count), ("chan", chan_count)):
+        stride = 2
         while stride < count:
             group = min(4, count // stride)
             rounds.append((axis, [stride * k for k in range(1, group)]))
             stride *= group
     jobs = [(kind, row_shift) for kind in ("own", "near", "far") for row_shift in range(3)]
-    cuts = [jobs[:4], jobs[4:]]
+    cuts = [jobs[:2], jobs[2:6], jobs[6:]]
     sums = ()
     for number, (axis, steps) in enumerate(rounds):
         parts = [piece] + [exchange(piece, axis, step) for step in steps]

time: 29.4 us -> 28.3 us (0.963)
  waiting for transfers between devices: 4.67 us -> 3.28 us
  Pallas kernels: 10.1 us -> 10.6 us
    ppermute x11 -> x9, starting transfers between devices: 13.1 us -> 11 us  [exchange(): return lax.ppermute(x, axis, [(i, i ^ step) for i in range(count)])]
    ppermute x11 -> x9, waiting for transfers between devices: 4.67 us -> 2.81 us  [exchange(): return lax.ppermute(x, axis, [(i, i ^ step) for i in range(count)])]
    ppermute x1, starting transfers between devices: 0.65 us -> 2.44 us  [per_device(): lax.ppermute(far, 'patch', far_pairs + [(j, i) for i, j in far_pairs])]
    pallas_call x6 -> x7, Pallas kernels: 10.1 us -> 10.6 us  [run(): pl.pallas_call(kernel, out_shape=outs, in_specs=[spec] * len(args), out_s...]
    ppermute x1, waiting for transfers between devices: 0.01 us -> 0.46 us  [per_device(): lax.ppermute(far, 'patch', far_pairs + [(j, i) for i, j in far_pairs])]
  transfers between devices with their start and end apart: 12 -> 10, of which waited for: 4 -> 3; matrix products, arithmetic and copies ran while one was open for 0% -> 0% of each run, Pallas kernels for 27% -> 28%
where the time goes in v4:
time: 28.3 us; the launch traced here: 28.1 us
  starting transfers between devices  13.5 us (48%)
  Pallas kernels  10.6 us (37%)
  waiting for transfers between devices  3.28 us (12%)
  between operations  0.72 us (3%)
    ppermute x9, starting transfers between devices, exchange(): return lax.ppermute(x, axis, [(i, i ^ step) for i in range(count)])  11 us
    pallas_call x7, Pallas kernels, run(): pl.pallas_call(kernel, out_shape=outs, in_specs=[spec] * len(args), out_s...  10.6 us
    ppermute x9, waiting for transfers between devices, exchange(): return lax.ppermute(x, axis, [(i, i ^ step) for i in range(count)])  2.81 us
    ppermute x1, starting transfers between devices, per_device(): lax.ppermute(far, 'patch', far_pairs + [(j, i) for i, j in far_pairs])  2.44 us
  transfers between devices with their start and end apart: 10, of which 3 were waited for; matrix products, arithmetic and copies ran while one was open for 0% of the time, Pallas kernels for 28%

profile of v4, /device:TPU:0, one launch (start us, length us, event | category | flops | bytes accessed | tf_op | source)
XLA Modules:
  0.0 28.1 jit_solution(15589138421116247829)
XLA Ops:
  0.6 1.0 %shard_map.78 = (f32[16,1792]{1,0:T(8,128)S(1)}, f32[16,1920]{1,0:T(8,128)S(1)}, f32[16,1792]{1,0:T(8,128)S(1)}, f32[16,1792]{1,0:T(8,128)S(1)}) custom-call(s32[2,3]{1,0:T(2,128)} %bitcast.6, f32[16,3072]{1,0:T(8,128)} %maps_ref.1), custom_call_target="tpu_custom_call" | custom-call | tf_op jit(solution)/shard_map/pallas_call | solution.py:326
  1.6 3.0 %collective-permute-start = (f32[16,1920]{1,0:T(8,128)S(1)}, f32[16,1920]{1,0:T(8,128)S(1)}, u32[]{:S(2)}, u32[]{:S(2)}) collective-permute-start(f32[16,1920]{1,0:T(8,128)S(1)} %get-tuple-element.29), channel_id=1, source_target_pairs={{0,8},{8,0},{16,24},{24,16},{1,9},{9,1},{17,25},{25,17},{2,10},{10... | collective-permute-start | bytes 368648 | tf_op jit(solution)/shard_map/ppermute | solution.py:338
  4.6 1.5 %collective-permute-start.1 = (f32[16,1792]{1,0:T(8,128)S(1)}, f32[16,1792]{1,0:T(8,128)S(1)}, u32[]{:S(2)}, u32[]{:S(2)}) collective-permute-start(f32[16,1792]{1,0:T(8,128)S(1)} %get-tuple-element.30), channel_id=1, source_target_pairs={{0,16},{8,24},{16,0},{24,8},{1,17},{9,25},{17,1},{25,9},{2,18},{10... | collective-permute-start | bytes 344072 | tf_op jit(solution)/shard_map/ppermute | solution.py:338
  6.1 0.0 collective-permute-start.2
  6.2 2.9 %shard_map.77 = (bf16[192,192]{1,0:T(8,128)(2,1)S(1)}, f32[1,3584]{1,0:T(1,128)S(1)}, bf16[9,128,1024]{2,1,0:T(8,128)(2,1)S(1)}, bf16[10,6,16,128]{3,2,1,0:T(8,128)(2,1)S(1)}) custom-call(s32[2,3]{1,0:T(2,128)} %bitcast.7, s32[3,2,9]{2,1,0:T(2,128)} %refs_1_.1, f32[8,64]{1,0:T(8,128)} %bitcast.5, f32[1,3072]{1,0:T(1,128)} %bitcast.4, s32[9,128,128]{2,1,0:T(8,128)} %refs_4_.1), custom_call_target="tpu_custom_call" | custom-call | tf_op jit(solution)/shard_map/pallas_call | solution.py:326
  9.1 1.9 %collective-permute-done.1.refs_5_ = f32[16,1792]{1,0:T(8,128)S(1)} collective-permute-done((f32[16,1792]{1,0:T(8,128)S(1)}, f32[16,1792]{1,0:T(8,128)S(1)}, u32[]{:S(2)}, u32[]{:S(2)}) %collective-permute-start.1) | collective-permute-done | bytes 114720 | tf_op jit(solution)/shard_map/ppermute | solution.py:338
  11.0 0.9 %collective-permute-done.2.refs_6_ = f32[16,1792]{1,0:T(8,128)S(1)} collective-permute-done((f32[16,1792]{1,0:T(8,128)S(1)}, f32[16,1792]{1,0:T(8,128)S(1)}, u32[]{:S(2)}, u32[]{:S(2)}) %collective-permute-start.2) | collective-permute-done | bytes 114720 | tf_op jit(solution)/shard_map/ppermute | solution.py:338
  11.9 0.0 collective-permute-done.refs_4_
  11.9 0.7 %shard_map.79 = (bf16[2,336,128]{2,1,0:T(8,128)(2,1)S(1)}, bf16[336,128]{1,0:T(8,128)(2,1)S(1)}, bf16[336,128]{1,0:T(8,128)(2,1)S(1)}, f32[32,128]{1,0:T(8,128)S(1)}) custom-call(bf16[192,192]{1,0:T(8,128)(2,1)S(1)} %get-tuple-element.26.refs_0_, f32[1,3584]{1,0:T(1,128)S(1)} %get-tuple-element.27.refs_1_, ...), custom_call_target="tpu_custom_call" | custom-call | tf_op jit(solution)/shard_map/pallas_call | solution.py:326
  12.5 0.1 collective-permute-start.5
  12.6 0.5 %collective-permute-start.4 = (bf16[336,128]{1,0:T(8,128)(2,1)S(1)}, bf16[336,128]{1,0:T(8,128)(2,1)S(1)}, u32[]{:S(2)}, u32[]{:S(2)}) collective-permute-start(bf16[336,128]{1,0:T(8,128)(2,1)S(1)} %get-tuple-element.34), channel_id=1, source_target_pairs={{0,1},{1,0},{2,3},{3,2},{4,5},{5,4},{6,7},{7,6},{8,9},{9,8},{10,11... | collective-permute-start | bytes 258056 | tf_op jit(solution)/shard_map/ppermute | solution.py:338
  13.1 1.1 %shard_map.80 = (f32[512,64]{1,0:T(8,128)S(1)}, f32[8,16,128]{2,1,0:T(8,128)S(1)}, f32[32,128]{1,0:T(8,128)S(1)}) custom-call(bf16[10,6,16,128]{3,2,1,0:T(8,128)(2,1)S(1)} %get-tuple-element.24.refs_2_.refs_0_, bf16[9,128,1024]{2,1,0:T(8,128)(2,1)S(1)} %get-tuple-element.25.refs_1_, bf16[2,336,128]{2,1,0:T(8,128)(2,1)S(1)} %get-tuple-element.32.refs_2_), custom_call_target="tpu_custom_call" | custom-call | tf_op jit(solution)/shard_map/pallas_call | solution.py:326
  14.2 0.0 collective-permute-done.5
  14.2 3.7 %collective-permute-start.8 = (f32[32,128]{1,0:T(8,128)S(1)}, f32[32,128]{1,0:T(8,128)S(1)}, u32[]{:S(2)}, u32[]{:S(2)}) collective-permute-start(f32[32,128]{1,0:T(8,128)S(1)} %add_add_fusion.1), channel_id=1, source_target_pairs={{0,6},{1,7},{2,4},{3,5},{4,2},{5,3},{6,0},{7,1},{8,14},{9,15},{10,... | collective-permute-start | bytes 49160 | tf_op jit(solution)/shard_map/ppermute | solution.py:338
  17.9 0.0 collective-permute-start.7
  17.9 0.8 %collective-permute-start.6 = (f32[32,128]{1,0:T(8,128)S(1)}, f32[32,128]{1,0:T(8,128)S(1)}, u32[]{:S(2)}, u32[]{:S(2)}) collective-permute-start(f32[32,128]{1,0:T(8,128)S(1)} %add_add_fusion.1), channel_id=1, source_target_pairs={{0,2},{1,3},{2,0},{3,1},{4,6},{5,7},{6,4},{7,5},{8,10},{9,11},{10,... | collective-permute-start | bytes 49160 | tf_op jit(solution)/shard_map/ppermute | solution.py:338
  18.7 2.4 %collective-permute-start.3 = (bf16[336,128]{1,0:T(8,128)(2,1)S(1)}, bf16[336,128]{1,0:T(8,128)(2,1)S(1)}, u32[]{:S(2)}, u32[]{:S(2)}) collective-permute-start(bf16[336,128]{1,0:T(8,128)(2,1)S(1)} %get-tuple-element.33), channel_id=1, source_target_pairs={{1,2},{3,4},{5,6},{7,0},{2,1},{4,3},{6,5},{0,7},{9,10},{11,12},{13... | collective-permute-start | bytes 258056 | tf_op jit(solution)/shard_map/ppermute | solution.py:403
  21.1 0.0 collective-permute-done.4.refs_3_
  21.1 1.9 %shard_map.81 = (f32[512,64]{1,0:T(8,128)S(1)}, f32[8,16,128]{2,1,0:T(8,128)S(1)}, f32[32,128]{1,0:T(8,128)S(1)}) custom-call(bf16[10,6,16,128]{3,2,1,0:T(8,128)(2,1)S(1)} %get-tuple-element.24.refs_2_.refs_0_, bf16[9,128,1024]{2,1,0:T(8,128)(2,1)S(1)} %get-tuple-element.25.refs_1_, bf16[2,336,128]{2,1,0:T(8,128)(2,1)S(1)} %get-tuple-element.32.refs_2_, ...), custom_call_target="tpu_custom_call" | custom-call | tf_op jit(solution)/shard_map/pallas_call | solution.py:326
  23.1 0.0 collective-permute-done.8
  23.1 0.0 collective-permute-done.7
  23.1 0.0 collective-permute-done.6
  23.1 1.5 %collective-permute-start.9 = (f32[32,128]{1,0:T(8,128)S(1)}, f32[32,128]{1,0:T(8,128)S(1)}, u32[]{:S(2)}, u32[]{:S(2)}) collective-permute-start(f32[32,128]{1,0:T(8,128)S(1)} %add_add_fusion.refs_0_), channel_id=1, source_target_pairs={{0,16},{8,24},{16,0},{24,8},{1,17},{9,25},{17,1},{25,9},{2,18},{10... | collective-permute-start | bytes 49160 | tf_op jit(solution)/shard_map/ppermute | solution.py:338
  24.6 0.5 %collective-permute-done.3.refs_3_ = bf16[336,128]{1,0:T(8,128)(2,1)S(1)} collective-permute-done((bf16[336,128]{1,0:T(8,128)(2,1)S(1)}, bf16[336,128]{1,0:T(8,128)(2,1)S(1)}, u32[]{:S(2)}, u32[]{:S(2)}) %collective-permute-start.3) | collective-permute-done | bytes 86048 | tf_op jit(solution)/shard_map/ppermute | solution.py:403
  25.0 2.1 %shard_map.82 = (f32[512,64]{1,0:T(8,128)S(1)}, f32[8,16,128]{2,1,0:T(8,128)S(1)}, f32[32,128]{1,0:T(8,128)}) custom-call(bf16[10,6,16,128]{3,2,1,0:T(8,128)(2,1)S(1)} %get-tuple-element.24.refs_2_.refs_0_, bf16[9,128,1024]{2,1,0:T(8,128)(2,1)S(1)} %get-tuple-element.25.refs_1_, bf16[2,336,128]{2,1,0:T(8,128)(2,1)S(1)} %get-tuple-element.32.refs_2_, ...), custom_call_target="tpu_custom_call" | custom-call | tf_op jit(solution)/shard_map/pallas_call | solution.py:326
  27.1 0.0 collective-permute-done.9.refs_1_
  27.1 0.9 %shard_map.83 = (f32[8,64,64]{2,1,0:T(8,128)}, f32[64,64]{1,0:T(8,128)}) custom-call(f32[512,64]{1,0:T(8,128)S(1)} %get-tuple-element.39.sums_ref, f32[8,16,128]{2,1,0:T(8,128)S(1)} %get-tuple-element.40.weight_sums_ref, f32[32,128]{1,0:T(8,128)S(1)} %add_add_fusion.refs_0_, f32[32,128]{1,0:T(8,128)S(1)} %collective-permute-done.9.refs_1_), custom_call_target="tpu_custom_call" | custom-call | tf_op jit(solution)/shard_map/pallas_call | solution.py:326
  (2 shorter events, 0.0 us)
Async XLA Ops:
  1.6 10.3 %collective-permute-start = (f32[16,1920]{1,0:T(8,128)S(1)}, f32[16,1920]{1,0:T(8,128)S(1)}, u32[]{:S(2)}, u32[]{:S(2)}) collective-permute-start(f32[16,1920]{1,0:T(8,128)S(1)} %get-tuple-element.29), channel_id=1, source_target_pairs={{0,8},{8,0},{16,24},{24,16},{1,9},{9,1},{17,25},{25,17},{2,10},{10... | collective-permute-start | bytes 368648 | tf_op jit(solution)/shard_map/ppermute | solution.py:338
  4.6 6.4 %collective-permute-start.1 = (f32[16,1792]{1,0:T(8,128)S(1)}, f32[16,1792]{1,0:T(8,128)S(1)}, u32[]{:S(2)}, u32[]{:S(2)}) collective-permute-start(f32[16,1792]{1,0:T(8,128)S(1)} %get-tuple-element.30), channel_id=1, source_target_pairs={{0,16},{8,24},{16,0},{24,8},{1,17},{9,25},{17,1},{25,9},{2,18},{10... | collective-permute-start | bytes 344072 | tf_op jit(solution)/shard_map/ppermute | solution.py:338
  6.1 5.7 %collective-permute-start.2 = (f32[16,1792]{1,0:T(8,128)S(1)}, f32[16,1792]{1,0:T(8,128)S(1)}, u32[]{:S(2)}, u32[]{:S(2)}) collective-permute-start(f32[16,1792]{1,0:T(8,128)S(1)} %get-tuple-element.31), channel_id=1, source_target_pairs={{0,24},{8,16},{16,8},{24,0},{1,25},{9,17},{17,9},{25,1},{2,26},{10... | collective-permute-start | bytes 344072 | tf_op jit(solution)/shard_map/ppermute | solution.py:338
  12.5 1.7 %collective-permute-start.5 = (f32[32,128]{1,0:T(8,128)S(1)}, f32[32,128]{1,0:T(8,128)S(1)}, u32[]{:S(2)}, u32[]{:S(2)}) collective-permute-start(f32[32,128]{1,0:T(8,128)S(1)} %get-tuple-element.41), channel_id=1, source_target_pairs={{0,1},{1,0},{2,3},{3,2},{4,5},{5,4},{6,7},{7,6},{8,9},{9,8},{10,11... | collective-permute-start | bytes 49160 | tf_op jit(solution)/shard_map/ppermute | solution.py:338
  12.6 8.5 %collective-permute-start.4 = (bf16[336,128]{1,0:T(8,128)(2,1)S(1)}, bf16[336,128]{1,0:T(8,128)(2,1)S(1)}, u32[]{:S(2)}, u32[]{:S(2)}) collective-permute-start(bf16[336,128]{1,0:T(8,128)(2,1)S(1)} %get-tuple-element.34), channel_id=1, source_target_pairs={{0,1},{1,0},{2,3},{3,2},{4,5},{5,4},{6,7},{7,6},{8,9},{9,8},{10,11... | collective-permute-start | bytes 258056 | tf_op jit(solution)/shard_map/ppermute | solution.py:338
  14.2 8.9 %collective-permute-start.8 = (f32[32,128]{1,0:T(8,128)S(1)}, f32[32,128]{1,0:T(8,128)S(1)}, u32[]{:S(2)}, u32[]{:S(2)}) collective-permute-start(f32[32,128]{1,0:T(8,128)S(1)} %add_add_fusion.1), channel_id=1, source_target_pairs={{0,6},{1,7},{2,4},{3,5},{4,2},{5,3},{6,0},{7,1},{8,14},{9,15},{10,... | collective-permute-start | bytes 49160 | tf_op jit(solution)/shard_map/ppermute | solution.py:338
  17.9 5.2 %collective-permute-start.7 = (f32[32,128]{1,0:T(8,128)S(1)}, f32[32,128]{1,0:T(8,128)S(1)}, u32[]{:S(2)}, u32[]{:S(2)}) collective-permute-start(f32[32,128]{1,0:T(8,128)S(1)} %add_add_fusion.1), channel_id=1, source_target_pairs={{0,4},{1,5},{2,6},{3,7},{4,0},{5,1},{6,2},{7,3},{8,12},{9,13},{10,... | collective-permute-start | bytes 49160 | tf_op jit(solution)/shard_map/ppermute | solution.py:338
  17.9 5.2 %collective-permute-start.6 = (f32[32,128]{1,0:T(8,128)S(1)}, f32[32,128]{1,0:T(8,128)S(1)}, u32[]{:S(2)}, u32[]{:S(2)}) collective-permute-start(f32[32,128]{1,0:T(8,128)S(1)} %add_add_fusion.1), channel_id=1, source_target_pairs={{0,2},{1,3},{2,0},{3,1},{4,6},{5,7},{6,4},{7,5},{8,10},{9,11},{10,... | collective-permute-start | bytes 49160 | tf_op jit(solution)/shard_map/ppermute | solution.py:338
  18.7 6.4 %collective-permute-start.3 = (bf16[336,128]{1,0:T(8,128)(2,1)S(1)}, bf16[336,128]{1,0:T(8,128)(2,1)S(1)}, u32[]{:S(2)}, u32[]{:S(2)}) collective-permute-start(bf16[336,128]{1,0:T(8,128)(2,1)S(1)} %get-tuple-element.33), channel_id=1, source_target_pairs={{1,2},{3,4},{5,6},{7,0},{2,1},{4,3},{6,5},{0,7},{9,10},{11,12},{13... | collective-permute-start | bytes 258056 | tf_op jit(solution)/shard_map/ppermute | solution.py:403
  23.1 4.0 %collective-permute-start.9 = (f32[32,128]{1,0:T(8,128)S(1)}, f32[32,128]{1,0:T(8,128)S(1)}, u32[]{:S(2)}, u32[]{:S(2)}) collective-permute-start(f32[32,128]{1,0:T(8,128)S(1)} %add_add_fusion.refs_0_), channel_id=1, source_target_pairs={{0,16},{8,24},{16,0},{24,8},{1,17},{9,25},{17,1},{25,9},{2,18},{10... | collective-permute-start | bytes 49160 | tf_op jit(solution)/shard_map/ppermute | solution.py:338

commit v5 on v4

--- a/solution.py
+++ b/solution.py
@@ -265,22 +265,25 @@
             halo_refs[name], *refs = refs
     if not first:
         sums_in_ref, weight_in_ref, *refs = refs
-    sums_ref, weight_sums_ref, none_ref = refs
-    none_ref[...] = jnp.zeros_like(none_ref)
+    sums_ref, weight_sums_ref, *none_refs = refs
+    for ref in none_refs:
+        ref[...] = jnp.zeros_like(ref)
     even = lax.axis_index("patch") % 2 == 0
     columns = [cols_ref[col] for col in range(TB)]
+    after = {"near": even, "far": jnp.logical_not(even)}
+    partners = {"own": columns}
+    for kind, ref in halo_refs.items():
+        partners[kind] = [
+            jnp.where(after[kind], columns[1], ref[...]),
+            jnp.where(after[kind], ref[...], columns[0]),
+        ]
     for number, (kind, row_shift) in enumerate(jobs):
-        if kind == "own":
-            code, partners = 3 * row_shift + 1, columns
-        else:
-            beside = halo_refs[kind][...]
-            after = even if kind == "near" else jnp.logical_not(even)
-            code = jnp.where(after, 3 * row_shift + 2, 3 * row_shift)
-            partners = [
-                jnp.where(after, columns[1], beside),
-                jnp.where(after, beside, columns[0]),
-            ]
-        sums, weight_sums = add_pairs(code, row_shift, live_ref, columns, partners, mask_ref)
+        code = 3 * row_shift + 1
+        if kind != "own":
+            code = code + jnp.where(after[kind], 1, -1)
+        sums, weight_sums = add_pairs(
+            code, row_shift, live_ref, columns, partners[kind], mask_ref
+        )
         if number:
             sums_ref[...] += sums
         else:
@@ -409,19 +412,21 @@
             rounds.append((axis, [stride * k for k in range(1, group)]))
             stride *= group
     jobs = [(kind, row_shift) for kind in ("own", "near", "far") for row_shift in range(3)]
-    cuts = [jobs[:2], jobs[2:6], jobs[6:]]
+    cuts = [jobs[:1], jobs[1:5], jobs[5:]]
     sums = ()
     for number, (axis, steps) in enumerate(rounds):
         parts = [piece] + [exchange(piece, axis, step) for step in steps]
         none = []
         if number < len(cuts):
             kinds = [kind for kind in halos if any(kind == job[0] for job in cuts[number])]
-            *sums, zeros = run(
+            last = number == len(rounds) - 1
+            outs = (shape((NBIN * NCH, NCH), F32), shape((NBIN, 16, TILE), F32))
+            outs = run(
                 lambda *refs: pair_kernel(cuts[number], not number, *refs),
-                (shape((NBIN * NCH, NCH), F32), shape((NBIN, 16, TILE), F32), piece_shape),
+                outs if last else outs + (piece_shape,),
                 [live, mask, cols] + [halos[kind] for kind in kinds] + list(sums),
             )
-            none = [zeros]
+            sums, none = outs[:2], list(outs[2:])
         if number < len(rounds) - 1:
             piece = sum(parts[1:] + none, parts[0])
     correlation, covariance = run(

time: 28.3 us -> 27.7 us (0.979)
  Pallas kernels: 10.6 us -> 10 us
    pallas_call x7, Pallas kernels: 10.6 us -> 10 us  [run(): pl.pallas_call(kernel, out_shape=outs, in_specs=[spec] * len(args), out_s...]
  transfers between devices with their start and end apart: 10 -> 10, of which waited for: 3 -> 3; matrix products, arithmetic and copies ran while one was open for 0% -> 0% of each run, Pallas kernels for 28% -> 27%
where the time goes in v5:
time: 27.7 us; the launch traced here: 27.5 us
  starting transfers between devices  13.5 us (49%)
  Pallas kernels  10 us (36%)
  waiting for transfers between devices  3.27 us (12%)
  between operations  0.73 us (3%)
    ppermute x9, starting transfers between devices, exchange(): return lax.ppermute(x, axis, [(i, i ^ step) for i in range(count)])  11 us
    pallas_call x7, Pallas kernels, run(): pl.pallas_call(kernel, out_shape=outs, in_specs=[spec] * len(args), out_s...  10 us
    ppermute x9, waiting for transfers between devices, exchange(): return lax.ppermute(x, axis, [(i, i ^ step) for i in range(count)])  2.81 us
    ppermute x1, starting transfers between devices, per_device(): lax.ppermute(far, 'patch', far_pairs + [(j, i) for i, j in far_pairs])  2.46 us
  transfers between devices with their start and end apart: 10, of which 3 were waited for; matrix products, arithmetic and copies ran while one was open for 0% of the time, Pallas kernels for 27%

profile of v5, /device:TPU:0, one launch (start us, length us, event | category | flops | bytes accessed | tf_op | source)
XLA Modules:
  0.0 27.5 jit_solution(14404378423645047684)
XLA Ops:
  0.6 1.0 %shard_map.78 = (f32[16,1792]{1,0:T(8,128)S(1)}, f32[16,1920]{1,0:T(8,128)S(1)}, f32[16,1792]{1,0:T(8,128)S(1)}, f32[16,1792]{1,0:T(8,128)S(1)}) custom-call(s32[2,3]{1,0:T(2,128)} %bitcast.6, f32[16,3072]{1,0:T(8,128)} %maps_ref.1), custom_call_target="tpu_custom_call" | custom-call | tf_op jit(solution)/shard_map/pallas_call | solution.py:329
  1.6 3.0 %collective-permute-start = (f32[16,1920]{1,0:T(8,128)S(1)}, f32[16,1920]{1,0:T(8,128)S(1)}, u32[]{:S(2)}, u32[]{:S(2)}) collective-permute-start(f32[16,1920]{1,0:T(8,128)S(1)} %get-tuple-element.29), channel_id=1, source_target_pairs={{0,8},{8,0},{16,24},{24,16},{1,9},{9,1},{17,25},{25,17},{2,10},{10... | collective-permute-start | bytes 368648 | tf_op jit(solution)/shard_map/ppermute | solution.py:341
  4.6 1.5 %collective-permute-start.1 = (f32[16,1792]{1,0:T(8,128)S(1)}, f32[16,1792]{1,0:T(8,128)S(1)}, u32[]{:S(2)}, u32[]{:S(2)}) collective-permute-start(f32[16,1792]{1,0:T(8,128)S(1)} %get-tuple-element.30), channel_id=1, source_target_pairs={{0,16},{8,24},{16,0},{24,8},{1,17},{9,25},{17,1},{25,9},{2,18},{10... | collective-permute-start | bytes 344072 | tf_op jit(solution)/shard_map/ppermute | solution.py:341
  6.1 0.0 collective-permute-start.2
  6.2 2.9 %shard_map.77 = (bf16[192,192]{1,0:T(8,128)(2,1)S(1)}, f32[1,3584]{1,0:T(1,128)S(1)}, bf16[9,128,1024]{2,1,0:T(8,128)(2,1)S(1)}, bf16[10,6,16,128]{3,2,1,0:T(8,128)(2,1)S(1)}) custom-call(s32[2,3]{1,0:T(2,128)} %bitcast.7, s32[3,2,9]{2,1,0:T(2,128)} %refs_1_.1, f32[8,64]{1,0:T(8,128)} %bitcast.5, f32[1,3072]{1,0:T(1,128)} %bitcast.4, s32[9,128,128]{2,1,0:T(8,128)} %refs_4_.1), custom_call_target="tpu_custom_call" | custom-call | tf_op jit(solution)/shard_map/pallas_call | solution.py:329
  9.1 1.9 %collective-permute-done.1.refs_5_ = f32[16,1792]{1,0:T(8,128)S(1)} collective-permute-done((f32[16,1792]{1,0:T(8,128)S(1)}, f32[16,1792]{1,0:T(8,128)S(1)}, u32[]{:S(2)}, u32[]{:S(2)}) %collective-permute-start.1) | collective-permute-done | bytes 114720 | tf_op jit(solution)/shard_map/ppermute | solution.py:341
  11.0 0.9 %collective-permute-done.2.refs_6_ = f32[16,1792]{1,0:T(8,128)S(1)} collective-permute-done((f32[16,1792]{1,0:T(8,128)S(1)}, f32[16,1792]{1,0:T(8,128)S(1)}, u32[]{:S(2)}, u32[]{:S(2)}) %collective-permute-start.2) | collective-permute-done | bytes 114720 | tf_op jit(solution)/shard_map/ppermute | solution.py:341
  11.9 0.0 collective-permute-done.refs_4_
  11.9 0.7 %shard_map.79 = (bf16[2,336,128]{2,1,0:T(8,128)(2,1)S(1)}, bf16[336,128]{1,0:T(8,128)(2,1)S(1)}, bf16[336,128]{1,0:T(8,128)(2,1)S(1)}, f32[32,128]{1,0:T(8,128)S(1)}) custom-call(bf16[192,192]{1,0:T(8,128)(2,1)S(1)} %get-tuple-element.26.refs_0_, f32[1,3584]{1,0:T(1,128)S(1)} %get-tuple-element.27.refs_1_, ...), custom_call_target="tpu_custom_call" | custom-call | tf_op jit(solution)/shard_map/pallas_call | solution.py:329
  12.5 0.1 collective-permute-start.5
  12.6 0.5 %collective-permute-start.3 = (bf16[336,128]{1,0:T(8,128)(2,1)S(1)}, bf16[336,128]{1,0:T(8,128)(2,1)S(1)}, u32[]{:S(2)}, u32[]{:S(2)}) collective-permute-start(bf16[336,128]{1,0:T(8,128)(2,1)S(1)} %get-tuple-element.33), channel_id=1, source_target_pairs={{0,1},{1,0},{2,3},{3,2},{4,5},{5,4},{6,7},{7,6},{8,9},{9,8},{10,11... | collective-permute-start | bytes 258056 | tf_op jit(solution)/shard_map/ppermute | solution.py:341
  13.1 0.7 %shard_map.80 = (f32[512,64]{1,0:T(8,128)S(1)}, f32[8,16,128]{2,1,0:T(8,128)S(1)}, f32[32,128]{1,0:T(8,128)S(1)}) custom-call(bf16[10,6,16,128]{3,2,1,0:T(8,128)(2,1)S(1)} %get-tuple-element.24.refs_2_.refs_0_, bf16[9,128,1024]{2,1,0:T(8,128)(2,1)S(1)} %get-tuple-element.25.refs_1_, bf16[2,336,128]{2,1,0:T(8,128)(2,1)S(1)} %get-tuple-element.32.refs_2_), custom_call_target="tpu_custom_call" | custom-call | tf_op jit(solution)/shard_map/pallas_call | solution.py:329
  13.8 0.0 collective-permute-done.5
  13.8 3.7 %collective-permute-start.8 = (f32[32,128]{1,0:T(8,128)S(1)}, f32[32,128]{1,0:T(8,128)S(1)}, u32[]{:S(2)}, u32[]{:S(2)}) collective-permute-start(f32[32,128]{1,0:T(8,128)S(1)} %add_add_fusion.1), channel_id=1, source_target_pairs={{0,6},{1,7},{2,4},{3,5},{4,2},{5,3},{6,0},{7,1},{8,14},{9,15},{10,... | collective-permute-start | bytes 49160 | tf_op jit(solution)/shard_map/ppermute | solution.py:341
  17.5 0.0 collective-permute-start.7
  17.5 0.8 %collective-permute-start.6 = (f32[32,128]{1,0:T(8,128)S(1)}, f32[32,128]{1,0:T(8,128)S(1)}, u32[]{:S(2)}, u32[]{:S(2)}) collective-permute-start(f32[32,128]{1,0:T(8,128)S(1)} %add_add_fusion.1), channel_id=1, source_target_pairs={{0,2},{1,3},{2,0},{3,1},{4,6},{5,7},{6,4},{7,5},{8,10},{9,11},{10,... | collective-permute-start | bytes 49160 | tf_op jit(solution)/shard_map/ppermute | solution.py:341
  18.3 2.5 %collective-permute-start.4 = (bf16[336,128]{1,0:T(8,128)(2,1)S(1)}, bf16[336,128]{1,0:T(8,128)(2,1)S(1)}, u32[]{:S(2)}, u32[]{:S(2)}) collective-permute-start(bf16[336,128]{1,0:T(8,128)(2,1)S(1)} %get-tuple-element.34), channel_id=1, source_target_pairs={{1,2},{3,4},{5,6},{7,0},{2,1},{4,3},{6,5},{0,7},{9,10},{11,12},{13... | collective-permute-start | bytes 258056 | tf_op jit(solution)/shard_map/ppermute | solution.py:406
  20.7 0.0 collective-permute-done.3.refs_3_
  20.7 1.9 %shard_map.81 = (f32[512,64]{1,0:T(8,128)S(1)}, f32[8,16,128]{2,1,0:T(8,128)S(1)}, f32[32,128]{1,0:T(8,128)S(1)}) custom-call(bf16[10,6,16,128]{3,2,1,0:T(8,128)(2,1)S(1)} %get-tuple-element.24.refs_2_.refs_0_, bf16[9,128,1024]{2,1,0:T(8,128)(2,1)S(1)} %get-tuple-element.25.refs_1_, bf16[2,336,128]{2,1,0:T(8,128)(2,1)S(1)} %get-tuple-element.32.refs_2_, ...), custom_call_target="tpu_custom_call" | custom-call | tf_op jit(solution)/shard_map/pallas_call | solution.py:329
  22.7 0.0 collective-permute-done.8
  22.7 0.0 collective-permute-done.7
  22.7 0.0 collective-permute-done.6
  22.7 1.5 %collective-permute-start.9 = (f32[32,128]{1,0:T(8,128)S(1)}, f32[32,128]{1,0:T(8,128)S(1)}, u32[]{:S(2)}, u32[]{:S(2)}) collective-permute-start(f32[32,128]{1,0:T(8,128)S(1)} %add_add_fusion.refs_0_), channel_id=1, source_target_pairs={{0,16},{8,24},{16,0},{24,8},{1,17},{9,25},{17,1},{25,9},{2,18},{10... | collective-permute-start | bytes 49160 | tf_op jit(solution)/shard_map/ppermute | solution.py:341
  24.2 0.5 %collective-permute-done.4.refs_4_ = bf16[336,128]{1,0:T(8,128)(2,1)S(1)} collective-permute-done((bf16[336,128]{1,0:T(8,128)(2,1)S(1)}, bf16[336,128]{1,0:T(8,128)(2,1)S(1)}, u32[]{:S(2)}, u32[]{:S(2)}) %collective-permute-start.4) | collective-permute-done | bytes 86048 | tf_op jit(solution)/shard_map/ppermute | solution.py:406
  24.6 1.9 %shard_map.82 = (f32[512,64]{1,0:T(8,128)S(1)}, f32[8,16,128]{2,1,0:T(8,128)S(1)}) custom-call(bf16[10,6,16,128]{3,2,1,0:T(8,128)(2,1)S(1)} %get-tuple-element.24.refs_2_.refs_0_, bf16[9,128,1024]{2,1,0:T(8,128)(2,1)S(1)} %get-tuple-element.25.refs_1_, bf16[2,336,128]{2,1,0:T(8,128)(2,1)S(1)} %get-tuple-element.32.refs_2_, ...), custom_call_target="tpu_custom_call" | custom-call | tf_op jit(solution)/shard_map/pallas_call | solution.py:329
  26.6 0.0 collective-permute-done.9.refs_1_
  26.6 1.0 %shard_map.83 = (f32[8,64,64]{2,1,0:T(8,128)}, f32[64,64]{1,0:T(8,128)}) custom-call(f32[512,64]{1,0:T(8,128)S(1)} %get-tuple-element.39.sums_ref, f32[8,16,128]{2,1,0:T(8,128)S(1)} %get-tuple-element.40.weight_sums_ref, f32[32,128]{1,0:T(8,128)S(1)} %add_add_fusion.refs_0_, f32[32,128]{1,0:T(8,128)S(1)} %collective-permute-done.9.refs_1_), custom_call_target="tpu_custom_call" | custom-call | tf_op jit(solution)/shard_map/pallas_call | solution.py:329
  (2 shorter events, 0.0 us)
Async XLA Ops:
  1.6 10.3 %collective-permute-start = (f32[16,1920]{1,0:T(8,128)S(1)}, f32[16,1920]{1,0:T(8,128)S(1)}, u32[]{:S(2)}, u32[]{:S(2)}) collective-permute-start(f32[16,1920]{1,0:T(8,128)S(1)} %get-tuple-element.29), channel_id=1, source_target_pairs={{0,8},{8,0},{16,24},{24,16},{1,9},{9,1},{17,25},{25,17},{2,10},{10... | collective-permute-start | bytes 368648 | tf_op jit(solution)/shard_map/ppermute | solution.py:341
  4.6 6.4 %collective-permute-start.1 = (f32[16,1792]{1,0:T(8,128)S(1)}, f32[16,1792]{1,0:T(8,128)S(1)}, u32[]{:S(2)}, u32[]{:S(2)}) collective-permute-start(f32[16,1792]{1,0:T(8,128)S(1)} %get-tuple-element.30), channel_id=1, source_target_pairs={{0,16},{8,24},{16,0},{24,8},{1,17},{9,25},{17,1},{25,9},{2,18},{10... | collective-permute-start | bytes 344072 | tf_op jit(solution)/shard_map/ppermute | solution.py:341
  6.1 5.7 %collective-permute-start.2 = (f32[16,1792]{1,0:T(8,128)S(1)}, f32[16,1792]{1,0:T(8,128)S(1)}, u32[]{:S(2)}, u32[]{:S(2)}) collective-permute-start(f32[16,1792]{1,0:T(8,128)S(1)} %get-tuple-element.31), channel_id=1, source_target_pairs={{0,24},{8,16},{16,8},{24,0},{1,25},{9,17},{17,9},{25,1},{2,26},{10... | collective-permute-start | bytes 344072 | tf_op jit(solution)/shard_map/ppermute | solution.py:341
  12.5 1.2 %collective-permute-start.5 = (f32[32,128]{1,0:T(8,128)S(1)}, f32[32,128]{1,0:T(8,128)S(1)}, u32[]{:S(2)}, u32[]{:S(2)}) collective-permute-start(f32[32,128]{1,0:T(8,128)S(1)} %get-tuple-element.41), channel_id=1, source_target_pairs={{0,1},{1,0},{2,3},{3,2},{4,5},{5,4},{6,7},{7,6},{8,9},{9,8},{10,11... | collective-permute-start | bytes 49160 | tf_op jit(solution)/shard_map/ppermute | solution.py:341
  12.6 8.1 %collective-permute-start.3 = (bf16[336,128]{1,0:T(8,128)(2,1)S(1)}, bf16[336,128]{1,0:T(8,128)(2,1)S(1)}, u32[]{:S(2)}, u32[]{:S(2)}) collective-permute-start(bf16[336,128]{1,0:T(8,128)(2,1)S(1)} %get-tuple-element.33), channel_id=1, source_target_pairs={{0,1},{1,0},{2,3},{3,2},{4,5},{5,4},{6,7},{7,6},{8,9},{9,8},{10,11... | collective-permute-start | bytes 258056 | tf_op jit(solution)/shard_map/ppermute | solution.py:341
  13.8 8.9 %collective-permute-start.8 = (f32[32,128]{1,0:T(8,128)S(1)}, f32[32,128]{1,0:T(8,128)S(1)}, u32[]{:S(2)}, u32[]{:S(2)}) collective-permute-start(f32[32,128]{1,0:T(8,128)S(1)} %add_add_fusion.1), channel_id=1, source_target_pairs={{0,6},{1,7},{2,4},{3,5},{4,2},{5,3},{6,0},{7,1},{8,14},{9,15},{10,... | collective-permute-start | bytes 49160 | tf_op jit(solution)/shard_map/ppermute | solution.py:341
  17.5 5.2 %collective-permute-start.7 = (f32[32,128]{1,0:T(8,128)S(1)}, f32[32,128]{1,0:T(8,128)S(1)}, u32[]{:S(2)}, u32[]{:S(2)}) collective-permute-start(f32[32,128]{1,0:T(8,128)S(1)} %add_add_fusion.1), channel_id=1, source_target_pairs={{0,4},{1,5},{2,6},{3,7},{4,0},{5,1},{6,2},{7,3},{8,12},{9,13},{10,... | collective-permute-start | bytes 49160 | tf_op jit(solution)/shard_map/ppermute | solution.py:341
  17.5 5.2 %collective-permute-start.6 = (f32[32,128]{1,0:T(8,128)S(1)}, f32[32,128]{1,0:T(8,128)S(1)}, u32[]{:S(2)}, u32[]{:S(2)}) collective-permute-start(f32[32,128]{1,0:T(8,128)S(1)} %add_add_fusion.1), channel_id=1, source_target_pairs={{0,2},{1,3},{2,0},{3,1},{4,6},{5,7},{6,4},{7,5},{8,10},{9,11},{10,... | collective-permute-start | bytes 49160 | tf_op jit(solution)/shard_map/ppermute | solution.py:341
  18.3 6.4 %collective-permute-start.4 = (bf16[336,128]{1,0:T(8,128)(2,1)S(1)}, bf16[336,128]{1,0:T(8,128)(2,1)S(1)}, u32[]{:S(2)}, u32[]{:S(2)}) collective-permute-start(bf16[336,128]{1,0:T(8,128)(2,1)S(1)} %get-tuple-element.34), channel_id=1, source_target_pairs={{1,2},{3,4},{5,6},{7,0},{2,1},{4,3},{6,5},{0,7},{9,10},{11,12},{13... | collective-permute-start | bytes 258056 | tf_op jit(solution)/shard_map/ppermute | solution.py:406
  22.7 3.9 %collective-permute-start.9 = (f32[32,128]{1,0:T(8,128)S(1)}, f32[32,128]{1,0:T(8,128)S(1)}, u32[]{:S(2)}, u32[]{:S(2)}) collective-permute-start(f32[32,128]{1,0:T(8,128)S(1)} %add_add_fusion.refs_0_), channel_id=1, source_target_pairs={{0,16},{8,24},{16,0},{24,8},{1,17},{9,25},{17,1},{25,9},{2,18},{10... | collective-permute-start | bytes 49160 | tf_op jit(solution)/shard_map/ppermute | solution.py:341

commit v6 on v5

--- a/solution.py
+++ b/solution.py
@@ -341,6 +341,33 @@
     return lax.ppermute(x, axis, [(i, i ^ step) for i in range(count)])
 
 
+def exchange_across(x, chan_step, patch_step):
+    if not chan_step:
+        return exchange(x, "patch", patch_step)
+    if not patch_step:
+        return exchange(x, "chan", chan_step)
+    count = lax.axis_size("patch")
+    pairs = [
+        (chan * count + patch, (chan ^ chan_step) * count + (patch ^ patch_step))
+        for chan in range(lax.axis_size("chan"))
+        for patch in range(count)
+    ]
+    return lax.ppermute(x, ("chan", "patch"), pairs)
+
+
+def sum_rounds(chan_count, patch_count):
+    far = [(0, 1 << n) for n in range(2, patch_count.bit_length() - 1)]
+    far += [(1 << n, 0) for n in range(2, chan_count.bit_length() - 1)]
+    groups = [[(0, 1)]] + [far[at : at + 2] for at in range(0, len(far), 2)] + [[(0, 2), (2, 0)]]
+    rounds = []
+    for group in groups:
+        partners = [(0, 0)]
+        for chan_step, patch_step in group:
+            partners += [(chan ^ chan_step, patch ^ patch_step) for chan, patch in partners]
+        rounds.append(partners[1:])
+    return rounds
+
+
 def per_device(sky_maps, mode_vectors, pixel_weight, neighbours, tile_counts, pair_bins):
     shape = jax.ShapeDtypeStruct
     chan_count = lax.axis_size("chan")
@@ -404,18 +431,12 @@
     halos = {"near": exchange(near, "patch", 1)}
     far_pairs = [(i, (i + 1) % patch_count) for i in range(1, patch_count, 2)]
     halos["far"] = lax.ppermute(far, "patch", far_pairs + [(j, i) for i, j in far_pairs])
-    rounds = [("patch", [1])]
-    for axis, count in (("patch", patch_count), ("chan", chan_count)):
-        stride = 2
-        while stride < count:
-            group = min(4, count // stride)
-            rounds.append((axis, [stride * k for k in range(1, group)]))
-            stride *= group
+    rounds = sum_rounds(chan_count, patch_count)
     jobs = [(kind, row_shift) for kind in ("own", "near", "far") for row_shift in range(3)]
     cuts = [jobs[:1], jobs[1:5], jobs[5:]]
     sums = ()
-    for number, (axis, steps) in enumerate(rounds):
-        parts = [piece] + [exchange(piece, axis, step) for step in steps]
+    for number, partners in enumerate(rounds):
+        parts = [piece] + [exchange_across(piece, *steps) for steps in partners]
         none = []
         if number < len(cuts):
             kinds = [kind for kind in halos if any(kind == job[0] for job in cuts[number])]

time: 27.7 us -> 26.5 us (0.957)
  starting transfers between devices: 13.5 us -> 12.1 us
    ppermute x0 -> x1, starting transfers between devices: none -> 1.72 us  [exchange_across(): return lax.ppermute(x, ('chan', 'patch'), pairs)]
    ppermute x1, starting transfers between devices: 2.46 us -> 0.78 us  [per_device(): lax.ppermute(far, 'patch', far_pairs + [(j, i) for i, j in far_pairs])]
    ppermute x9 -> x8, starting transfers between devices: 11 us -> 9.6 us  [exchange(): return lax.ppermute(x, axis, [(i, i ^ step) for i in range(count)])]
    ppermute x9 -> x8, waiting for transfers between devices: 2.81 us -> 3.38 us  [exchange(): return lax.ppermute(x, axis, [(i, i ^ step) for i in range(count)])]
    ppermute x1, waiting for transfers between devices: 0.46 us -> 0.01 us  [per_device(): lax.ppermute(far, 'patch', far_pairs + [(j, i) for i, j in far_pairs])]
  transfers between devices with their start and end apart: 10 -> 10, of which waited for: 3 -> 3; matrix products, arithmetic and copies ran while one was open for 0% -> 0% of each run, Pallas kernels for 27% -> 28%
where the time goes in v6:
time: 26.5 us; the launch traced here: 26.3 us
  starting transfers between devices  12.1 us (46%)
  Pallas kernels  10 us (38%)
  waiting for transfers between devices  3.38 us (13%)
  between operations  0.73 us (3%)
    pallas_call x7, Pallas kernels, run(): pl.pallas_call(kernel, out_shape=outs, in_specs=[spec] * len(args), out_s...  10 us
    ppermute x8, starting transfers between devices, exchange(): return lax.ppermute(x, axis, [(i, i ^ step) for i in range(count)])  9.6 us
    ppermute x8, waiting for transfers between devices, exchange(): return lax.ppermute(x, axis, [(i, i ^ step) for i in range(count)])  3.38 us
    ppermute x1, starting transfers between devices, exchange_across(): return lax.ppermute(x, ('chan', 'patch'), pairs)  1.72 us
    ppermute x1, starting transfers between devices, per_device(): lax.ppermute(far, 'patch', far_pairs + [(j, i) for i, j in far_pairs])  0.78 us
  transfers between devices with their start and end apart: 10, of which 3 were waited for; matrix products, arithmetic and copies ran while one was open for 0% of the time, Pallas kernels for 28%

profile of v6, /device:TPU:0, one launch (start us, length us, event | category | flops | bytes accessed | tf_op | source)
XLA Modules:
  0.0 26.3 jit_solution(13807775975202565486)
XLA Ops:
  0.6 1.0 %shard_map.78 = (f32[16,1792]{1,0:T(8,128)S(1)}, f32[16,1920]{1,0:T(8,128)S(1)}, f32[16,1792]{1,0:T(8,128)S(1)}, f32[16,1792]{1,0:T(8,128)S(1)}) custom-call(s32[2,3]{1,0:T(2,128)} %bitcast.6, f32[16,3072]{1,0:T(8,128)} %maps_ref.1), custom_call_target="tpu_custom_call" | custom-call | tf_op jit(solution)/shard_map/pallas_call | solution.py:329
  1.6 3.0 %collective-permute-start = (f32[16,1920]{1,0:T(8,128)S(1)}, f32[16,1920]{1,0:T(8,128)S(1)}, u32[]{:S(2)}, u32[]{:S(2)}) collective-permute-start(f32[16,1920]{1,0:T(8,128)S(1)} %get-tuple-element.29), channel_id=1, source_target_pairs={{0,8},{8,0},{16,24},{24,16},{1,9},{9,1},{17,25},{25,17},{2,10},{10... | collective-permute-start | bytes 368648 | tf_op jit(solution)/shard_map/ppermute | solution.py:341
  4.6 1.5 %collective-permute-start.1 = (f32[16,1792]{1,0:T(8,128)S(1)}, f32[16,1792]{1,0:T(8,128)S(1)}, u32[]{:S(2)}, u32[]{:S(2)}) collective-permute-start(f32[16,1792]{1,0:T(8,128)S(1)} %get-tuple-element.30), channel_id=1, source_target_pairs={{0,16},{8,24},{16,0},{24,8},{1,17},{9,25},{17,1},{25,9},{2,18},{10... | collective-permute-start | bytes 344072 | tf_op jit(solution)/shard_map/ppermute | solution.py:341
  6.1 0.0 collective-permute-start.2
  6.2 2.9 %shard_map.77 = (bf16[192,192]{1,0:T(8,128)(2,1)S(1)}, f32[1,3584]{1,0:T(1,128)S(1)}, bf16[9,128,1024]{2,1,0:T(8,128)(2,1)S(1)}, bf16[10,6,16,128]{3,2,1,0:T(8,128)(2,1)S(1)}) custom-call(s32[2,3]{1,0:T(2,128)} %bitcast.7, s32[3,2,9]{2,1,0:T(2,128)} %refs_1_.1, f32[8,64]{1,0:T(8,128)} %bitcast.5, f32[1,3072]{1,0:T(1,128)} %bitcast.4, s32[9,128,128]{2,1,0:T(8,128)} %refs_4_.1), custom_call_target="tpu_custom_call" | custom-call | tf_op jit(solution)/shard_map/pallas_call | solution.py:329
  9.1 1.9 %collective-permute-done.1.refs_5_ = f32[16,1792]{1,0:T(8,128)S(1)} collective-permute-done((f32[16,1792]{1,0:T(8,128)S(1)}, f32[16,1792]{1,0:T(8,128)S(1)}, u32[]{:S(2)}, u32[]{:S(2)}) %collective-permute-start.1) | collective-permute-done | bytes 114720 | tf_op jit(solution)/shard_map/ppermute | solution.py:341
  11.0 0.9 %collective-permute-done.2.refs_6_ = f32[16,1792]{1,0:T(8,128)S(1)} collective-permute-done((f32[16,1792]{1,0:T(8,128)S(1)}, f32[16,1792]{1,0:T(8,128)S(1)}, u32[]{:S(2)}, u32[]{:S(2)}) %collective-permute-start.2) | collective-permute-done | bytes 114720 | tf_op jit(solution)/shard_map/ppermute | solution.py:341
  11.9 0.0 collective-permute-done.refs_4_
  11.9 0.7 %shard_map.79 = (bf16[2,336,128]{2,1,0:T(8,128)(2,1)S(1)}, bf16[336,128]{1,0:T(8,128)(2,1)S(1)}, bf16[336,128]{1,0:T(8,128)(2,1)S(1)}, f32[32,128]{1,0:T(8,128)S(1)}) custom-call(bf16[192,192]{1,0:T(8,128)(2,1)S(1)} %get-tuple-element.26.refs_0_, f32[1,3584]{1,0:T(1,128)S(1)} %get-tuple-element.27.refs_1_, ...), custom_call_target="tpu_custom_call" | custom-call | tf_op jit(solution)/shard_map/pallas_call | solution.py:329
  12.5 0.1 collective-permute-start.5
  12.6 0.5 %collective-permute-start.3 = (bf16[336,128]{1,0:T(8,128)(2,1)S(1)}, bf16[336,128]{1,0:T(8,128)(2,1)S(1)}, u32[]{:S(2)}, u32[]{:S(2)}) collective-permute-start(bf16[336,128]{1,0:T(8,128)(2,1)S(1)} %get-tuple-element.33), channel_id=1, source_target_pairs={{0,1},{1,0},{2,3},{3,2},{4,5},{5,4},{6,7},{7,6},{8,9},{9,8},{10,11... | collective-permute-start | bytes 258056 | tf_op jit(solution)/shard_map/ppermute | solution.py:341
  13.1 0.7 %shard_map.80 = (f32[512,64]{1,0:T(8,128)S(1)}, f32[8,16,128]{2,1,0:T(8,128)S(1)}, f32[32,128]{1,0:T(8,128)S(1)}) custom-call(bf16[10,6,16,128]{3,2,1,0:T(8,128)(2,1)S(1)} %get-tuple-element.24.refs_2_.refs_0_, bf16[9,128,1024]{2,1,0:T(8,128)(2,1)S(1)} %get-tuple-element.25.refs_1_, bf16[2,336,128]{2,1,0:T(8,128)(2,1)S(1)} %get-tuple-element.32.refs_2_), custom_call_target="tpu_custom_call" | custom-call | tf_op jit(solution)/shard_map/pallas_call | solution.py:329
  13.8 0.0 collective-permute-done.5
  13.8 2.7 %collective-permute-start.6 = (f32[32,128]{1,0:T(8,128)S(1)}, f32[32,128]{1,0:T(8,128)S(1)}, u32[]{:S(2)}, u32[]{:S(2)}) collective-permute-start(f32[32,128]{1,0:T(8,128)S(1)} %add_add_fusion.1), channel_id=1, source_target_pairs={{0,4},{1,5},{2,6},{3,7},{4,0},{5,1},{6,2},{7,3},{8,12},{9,13},{10,... | collective-permute-start | bytes 49160 | tf_op jit(solution)/shard_map/ppermute | solution.py:341
  16.5 0.8 %collective-permute-start.4 = (bf16[336,128]{1,0:T(8,128)(2,1)S(1)}, bf16[336,128]{1,0:T(8,128)(2,1)S(1)}, u32[]{:S(2)}, u32[]{:S(2)}) collective-permute-start(bf16[336,128]{1,0:T(8,128)(2,1)S(1)} %get-tuple-element.34), channel_id=1, source_target_pairs={{1,2},{3,4},{5,6},{7,0},{2,1},{4,3},{6,5},{0,7},{9,10},{11,12},{13... | collective-permute-start | bytes 258056 | tf_op jit(solution)/shard_map/ppermute | solution.py:433
  17.2 0.0 collective-permute-done.3.refs_3_
  17.2 1.9 %shard_map.81 = (f32[512,64]{1,0:T(8,128)S(1)}, f32[8,16,128]{2,1,0:T(8,128)S(1)}, f32[32,128]{1,0:T(8,128)S(1)}) custom-call(bf16[10,6,16,128]{3,2,1,0:T(8,128)(2,1)S(1)} %get-tuple-element.24.refs_2_.refs_0_, bf16[9,128,1024]{2,1,0:T(8,128)(2,1)S(1)} %get-tuple-element.25.refs_1_, bf16[2,336,128]{2,1,0:T(8,128)(2,1)S(1)} %get-tuple-element.32.refs_2_, ...), custom_call_target="tpu_custom_call" | custom-call | tf_op jit(solution)/shard_map/pallas_call | solution.py:329
  19.2 0.0 collective-permute-done.6
  19.2 1.7 %collective-permute-start.9 = (f32[32,128]{1,0:T(8,128)S(1)}, f32[32,128]{1,0:T(8,128)S(1)}, u32[]{:S(2)}, u32[]{:S(2)}) collective-permute-start(f32[32,128]{1,0:T(8,128)S(1)} %add_add_fusion.refs_0_), channel_id=1, source_target_pairs={{0,18},{1,19},{2,16},{3,17},{4,22},{5,23},{6,20},{7,21},{8,26},{9,... | collective-permute-start | bytes 49160 | tf_op jit(solution)/shard_map/ppermute | solution.py:355
  20.9 0.6 %collective-permute-start.8 = (f32[32,128]{1,0:T(8,128)S(1)}, f32[32,128]{1,0:T(8,128)S(1)}, u32[]{:S(2)}, u32[]{:S(2)}) collective-permute-start(f32[32,128]{1,0:T(8,128)S(1)} %add_add_fusion.refs_0_), channel_id=1, source_target_pairs={{0,16},{8,24},{16,0},{24,8},{1,17},{9,25},{17,1},{25,9},{2,18},{10... | collective-permute-start | bytes 49160 | tf_op jit(solution)/shard_map/ppermute | solution.py:341
  21.6 1.2 %collective-permute-start.7 = (f32[32,128]{1,0:T(8,128)S(1)}, f32[32,128]{1,0:T(8,128)S(1)}, u32[]{:S(2)}, u32[]{:S(2)}) collective-permute-start(f32[32,128]{1,0:T(8,128)S(1)} %add_add_fusion.refs_0_), channel_id=1, source_target_pairs={{0,2},{1,3},{2,0},{3,1},{4,6},{5,7},{6,4},{7,5},{8,10},{9,11},{10,... | collective-permute-start | bytes 49160 | tf_op jit(solution)/shard_map/ppermute | solution.py:341
  22.8 0.0 collective-permute-done.4.refs_4_
  22.8 1.9 %shard_map.82 = (f32[512,64]{1,0:T(8,128)S(1)}, f32[8,16,128]{2,1,0:T(8,128)S(1)}) custom-call(bf16[10,6,16,128]{3,2,1,0:T(8,128)(2,1)S(1)} %get-tuple-element.24.refs_2_.refs_0_, bf16[9,128,1024]{2,1,0:T(8,128)(2,1)S(1)} %get-tuple-element.25.refs_1_, bf16[2,336,128]{2,1,0:T(8,128)(2,1)S(1)} %get-tuple-element.32.refs_2_, ...), custom_call_target="tpu_custom_call" | custom-call | tf_op jit(solution)/shard_map/pallas_call | solution.py:329
  24.7 0.0 collective-permute-done.9.refs_3_
  24.7 0.0 collective-permute-done.8.refs_2_
  24.7 0.6 %collective-permute-done.7.refs_1_ = f32[32,128]{1,0:T(8,128)S(1)} collective-permute-done((f32[32,128]{1,0:T(8,128)S(1)}, f32[32,128]{1,0:T(8,128)S(1)}, u32[]{:S(2)}, u32[]{:S(2)}) %collective-permute-start.7) | collective-permute-done | bytes 16416 | tf_op jit(solution)/shard_map/ppermute | solution.py:341
  25.3 1.0 %shard_map.83 = (f32[8,64,64]{2,1,0:T(8,128)}, f32[64,64]{1,0:T(8,128)}) custom-call(f32[512,64]{1,0:T(8,128)S(1)} %get-tuple-element.39.sums_ref, f32[8,16,128]{2,1,0:T(8,128)S(1)} %get-tuple-element.40.weight_sums_ref, f32[32,128]{1,0:T(8,128)S(1)} %add_add_fusion.refs_0_, f32[32,128]{1,0:T(8,128)S(1)} %collective-permute-done.7.refs_1_, ...), custom_call_target="tpu_custom_call" | custom-call | tf_op jit(solution)/shard_map/pallas_call | solution.py:329
  (2 shorter events, 0.0 us)
Async XLA Ops:
  1.6 10.3 %collective-permute-start = (f32[16,1920]{1,0:T(8,128)S(1)}, f32[16,1920]{1,0:T(8,128)S(1)}, u32[]{:S(2)}, u32[]{:S(2)}) collective-permute-start(f32[16,1920]{1,0:T(8,128)S(1)} %get-tuple-element.29), channel_id=1, source_target_pairs={{0,8},{8,0},{16,24},{24,16},{1,9},{9,1},{17,25},{25,17},{2,10},{10... | collective-permute-start | bytes 368648 | tf_op jit(solution)/shard_map/ppermute | solution.py:341
  4.6 6.4 %collective-permute-start.1 = (f32[16,1792]{1,0:T(8,128)S(1)}, f32[16,1792]{1,0:T(8,128)S(1)}, u32[]{:S(2)}, u32[]{:S(2)}) collective-permute-start(f32[16,1792]{1,0:T(8,128)S(1)} %get-tuple-element.30), channel_id=1, source_target_pairs={{0,16},{8,24},{16,0},{24,8},{1,17},{9,25},{17,1},{25,9},{2,18},{10... | collective-permute-start | bytes 344072 | tf_op jit(solution)/shard_map/ppermute | solution.py:341
  6.1 5.7 %collective-permute-start.2 = (f32[16,1792]{1,0:T(8,128)S(1)}, f32[16,1792]{1,0:T(8,128)S(1)}, u32[]{:S(2)}, u32[]{:S(2)}) collective-permute-start(f32[16,1792]{1,0:T(8,128)S(1)} %get-tuple-element.31), channel_id=1, source_target_pairs={{0,24},{8,16},{16,8},{24,0},{1,25},{9,17},{17,9},{25,1},{2,26},{10... | collective-permute-start | bytes 344072 | tf_op jit(solution)/shard_map/ppermute | solution.py:341
  12.5 1.2 %collective-permute-start.5 = (f32[32,128]{1,0:T(8,128)S(1)}, f32[32,128]{1,0:T(8,128)S(1)}, u32[]{:S(2)}, u32[]{:S(2)}) collective-permute-start(f32[32,128]{1,0:T(8,128)S(1)} %get-tuple-element.41), channel_id=1, source_target_pairs={{0,1},{1,0},{2,3},{3,2},{4,5},{5,4},{6,7},{7,6},{8,9},{9,8},{10,11... | collective-permute-start | bytes 49160 | tf_op jit(solution)/shard_map/ppermute | solution.py:341
  12.6 4.6 %collective-permute-start.3 = (bf16[336,128]{1,0:T(8,128)(2,1)S(1)}, bf16[336,128]{1,0:T(8,128)(2,1)S(1)}, u32[]{:S(2)}, u32[]{:S(2)}) collective-permute-start(bf16[336,128]{1,0:T(8,128)(2,1)S(1)} %get-tuple-element.33), channel_id=1, source_target_pairs={{0,1},{1,0},{2,3},{3,2},{4,5},{5,4},{6,7},{7,6},{8,9},{9,8},{10,11... | collective-permute-start | bytes 258056 | tf_op jit(solution)/shard_map/ppermute | solution.py:341
  13.8 5.4 %collective-permute-start.6 = (f32[32,128]{1,0:T(8,128)S(1)}, f32[32,128]{1,0:T(8,128)S(1)}, u32[]{:S(2)}, u32[]{:S(2)}) collective-permute-start(f32[32,128]{1,0:T(8,128)S(1)} %add_add_fusion.1), channel_id=1, source_target_pairs={{0,4},{1,5},{2,6},{3,7},{4,0},{5,1},{6,2},{7,3},{8,12},{9,13},{10,... | collective-permute-start | bytes 49160 | tf_op jit(solution)/shard_map/ppermute | solution.py:341
  16.5 6.3 %collective-permute-start.4 = (bf16[336,128]{1,0:T(8,128)(2,1)S(1)}, bf16[336,128]{1,0:T(8,128)(2,1)S(1)}, u32[]{:S(2)}, u32[]{:S(2)}) collective-permute-start(bf16[336,128]{1,0:T(8,128)(2,1)S(1)} %get-tuple-element.34), channel_id=1, source_target_pairs={{1,2},{3,4},{5,6},{7,0},{2,1},{4,3},{6,5},{0,7},{9,10},{11,12},{13... | collective-permute-start | bytes 258056 | tf_op jit(solution)/shard_map/ppermute | solution.py:433
  19.2 5.5 %collective-permute-start.9 = (f32[32,128]{1,0:T(8,128)S(1)}, f32[32,128]{1,0:T(8,128)S(1)}, u32[]{:S(2)}, u32[]{:S(2)}) collective-permute-start(f32[32,128]{1,0:T(8,128)S(1)} %add_add_fusion.refs_0_), channel_id=1, source_target_pairs={{0,18},{1,19},{2,16},{3,17},{4,22},{5,23},{6,20},{7,21},{8,26},{9,... | collective-permute-start | bytes 49160 | tf_op jit(solution)/shard_map/ppermute | solution.py:355
  20.9 3.8 %collective-permute-start.8 = (f32[32,128]{1,0:T(8,128)S(1)}, f32[32,128]{1,0:T(8,128)S(1)}, u32[]{:S(2)}, u32[]{:S(2)}) collective-permute-start(f32[32,128]{1,0:T(8,128)S(1)} %add_add_fusion.refs_0_), channel_id=1, source_target_pairs={{0,16},{8,24},{16,0},{24,8},{1,17},{9,25},{17,1},{25,9},{2,18},{10... | collective-permute-start | bytes 49160 | tf_op jit(solution)/shard_map/ppermute | solution.py:341
  21.6 3.7 %collective-permute-start.7 = (f32[32,128]{1,0:T(8,128)S(1)}, f32[32,128]{1,0:T(8,128)S(1)}, u32[]{:S(2)}, u32[]{:S(2)}) collective-permute-start(f32[32,128]{1,0:T(8,128)S(1)} %add_add_fusion.refs_0_), channel_id=1, source_target_pairs={{0,2},{1,3},{2,0},{3,1},{4,6},{5,7},{6,4},{7,5},{8,10},{9,11},{10,... | collective-permute-start | bytes 49160 | tf_op jit(solution)/shard_map/ppermute | solution.py:341

commit v7 on v6

--- a/solution.py
+++ b/solution.py
@@ -364,7 +364,7 @@
         partners = [(0, 0)]
         for chan_step, patch_step in group:
             partners += [(chan ^ chan_step, patch ^ patch_step) for chan, patch in partners]
-        rounds.append(partners[1:])
+        rounds.append([(chan, patch | 1) for chan, patch in partners[1:]])
     return rounds
 
 

time: 26.5 us -> 25.8 us (0.974)
  waiting for transfers between devices: 3.38 us -> 2.82 us
    ppermute x8 -> x7, starting transfers between devices: 9.6 us -> 8.73 us  [exchange(): return lax.ppermute(x, axis, [(i, i ^ step) for i in range(count)])]
    ppermute x1, starting transfers between devices: 0.78 us -> 1.38 us  [per_device(): lax.ppermute(far, 'patch', far_pairs + [(j, i) for i, j in far_pairs])]
    ppermute x8 -> x7, waiting for transfers between devices: 3.38 us -> 2.81 us  [exchange(): return lax.ppermute(x, axis, [(i, i ^ step) for i in range(count)])]
    ppermute x1 -> x2, starting transfers between devices: 1.72 us -> 1.93 us  [exchange_across(): return lax.ppermute(x, ('chan', 'patch'), pairs)]
  transfers between devices with their start and end apart: 10 -> 10, of which waited for: 3 -> 2; matrix products, arithmetic and copies ran while one was open for 0% -> 0% of each run, Pallas kernels for 28% -> 29%
where the time goes in v7:
time: 25.8 us; the launch traced here: 25.6 us
  starting transfers between devices  12 us (47%)
  Pallas kernels  10 us (39%)
  waiting for transfers between devices  2.82 us (11%)
  between operations  0.73 us (3%)
    pallas_call x7, Pallas kernels, run(): pl.pallas_call(kernel, out_shape=outs, in_specs=[spec] * len(args), out_s...  10 us
    ppermute x7, starting transfers between devices, exchange(): return lax.ppermute(x, axis, [(i, i ^ step) for i in range(count)])  8.73 us
    ppermute x7, waiting for transfers between devices, exchange(): return lax.ppermute(x, axis, [(i, i ^ step) for i in range(count)])  2.81 us
    ppermute x2, starting transfers between devices, exchange_across(): return lax.ppermute(x, ('chan', 'patch'), pairs)  1.93 us
    ppermute x1, starting transfers between devices, per_device(): lax.ppermute(far, 'patch', far_pairs + [(j, i) for i, j in far_pairs])  1.38 us
  transfers between devices with their start and end apart: 10, of which 2 were waited for; matrix products, arithmetic and copies ran while one was open for 0% of the time, Pallas kernels for 29%

profile of v7, /device:TPU:0, one launch (start us, length us, event | category | flops | bytes accessed | tf_op | source)
XLA Modules:
  0.0 25.6 jit_solution(3304249227162531801)
XLA Ops:
  0.6 1.0 %shard_map.78 = (f32[16,1792]{1,0:T(8,128)S(1)}, f32[16,1920]{1,0:T(8,128)S(1)}, f32[16,1792]{1,0:T(8,128)S(1)}, f32[16,1792]{1,0:T(8,128)S(1)}) custom-call(s32[2,3]{1,0:T(2,128)} %bitcast.6, f32[16,3072]{1,0:T(8,128)} %maps_ref.1), custom_call_target="tpu_custom_call" | custom-call | tf_op jit(solution)/shard_map/pallas_call | solution.py:329
  1.6 3.0 %collective-permute-start = (f32[16,1920]{1,0:T(8,128)S(1)}, f32[16,1920]{1,0:T(8,128)S(1)}, u32[]{:S(2)}, u32[]{:S(2)}) collective-permute-start(f32[16,1920]{1,0:T(8,128)S(1)} %get-tuple-element.29), channel_id=1, source_target_pairs={{0,8},{8,0},{16,24},{24,16},{1,9},{9,1},{17,25},{25,17},{2,10},{10... | collective-permute-start | bytes 368648 | tf_op jit(solution)/shard_map/ppermute | solution.py:341
  4.6 1.5 %collective-permute-start.1 = (f32[16,1792]{1,0:T(8,128)S(1)}, f32[16,1792]{1,0:T(8,128)S(1)}, u32[]{:S(2)}, u32[]{:S(2)}) collective-permute-start(f32[16,1792]{1,0:T(8,128)S(1)} %get-tuple-element.30), channel_id=1, source_target_pairs={{0,16},{8,24},{16,0},{24,8},{1,17},{9,25},{17,1},{25,9},{2,18},{10... | collective-permute-start | bytes 344072 | tf_op jit(solution)/shard_map/ppermute | solution.py:341
  6.1 0.0 collective-permute-start.2
  6.2 2.9 %shard_map.77 = (bf16[192,192]{1,0:T(8,128)(2,1)S(1)}, f32[1,3584]{1,0:T(1,128)S(1)}, bf16[9,128,1024]{2,1,0:T(8,128)(2,1)S(1)}, bf16[10,6,16,128]{3,2,1,0:T(8,128)(2,1)S(1)}) custom-call(s32[2,3]{1,0:T(2,128)} %bitcast.7, s32[3,2,9]{2,1,0:T(2,128)} %refs_1_.1, f32[8,64]{1,0:T(8,128)} %bitcast.5, f32[1,3072]{1,0:T(1,128)} %bitcast.4, s32[9,128,128]{2,1,0:T(8,128)} %refs_4_.1), custom_call_target="tpu_custom_call" | custom-call | tf_op jit(solution)/shard_map/pallas_call | solution.py:329
  9.1 1.9 %collective-permute-done.1.refs_5_ = f32[16,1792]{1,0:T(8,128)S(1)} collective-permute-done((f32[16,1792]{1,0:T(8,128)S(1)}, f32[16,1792]{1,0:T(8,128)S(1)}, u32[]{:S(2)}, u32[]{:S(2)}) %collective-permute-start.1) | collective-permute-done | bytes 114720 | tf_op jit(solution)/shard_map/ppermute | solution.py:341
  11.0 0.9 %collective-permute-done.2.refs_6_ = f32[16,1792]{1,0:T(8,128)S(1)} collective-permute-done((f32[16,1792]{1,0:T(8,128)S(1)}, f32[16,1792]{1,0:T(8,128)S(1)}, u32[]{:S(2)}, u32[]{:S(2)}) %collective-permute-start.2) | collective-permute-done | bytes 114720 | tf_op jit(solution)/shard_map/ppermute | solution.py:341
  11.9 0.0 collective-permute-done.refs_4_
  11.9 0.7 %shard_map.79 = (bf16[2,336,128]{2,1,0:T(8,128)(2,1)S(1)}, bf16[336,128]{1,0:T(8,128)(2,1)S(1)}, bf16[336,128]{1,0:T(8,128)(2,1)S(1)}, f32[32,128]{1,0:T(8,128)S(1)}) custom-call(bf16[192,192]{1,0:T(8,128)(2,1)S(1)} %get-tuple-element.26.refs_0_, f32[1,3584]{1,0:T(1,128)S(1)} %get-tuple-element.27.refs_1_, ...), custom_call_target="tpu_custom_call" | custom-call | tf_op jit(solution)/shard_map/pallas_call | solution.py:329
  12.5 0.1 collective-permute-start.5
  12.6 0.5 %collective-permute-start.3 = (bf16[336,128]{1,0:T(8,128)(2,1)S(1)}, bf16[336,128]{1,0:T(8,128)(2,1)S(1)}, u32[]{:S(2)}, u32[]{:S(2)}) collective-permute-start(bf16[336,128]{1,0:T(8,128)(2,1)S(1)} %get-tuple-element.33), channel_id=1, source_target_pairs={{0,1},{1,0},{2,3},{3,2},{4,5},{5,4},{6,7},{7,6},{8,9},{9,8},{10,11... | collective-permute-start | bytes 258056 | tf_op jit(solution)/shard_map/ppermute | solution.py:341
  13.1 0.7 %shard_map.80 = (f32[512,64]{1,0:T(8,128)S(1)}, f32[8,16,128]{2,1,0:T(8,128)S(1)}, f32[32,128]{1,0:T(8,128)S(1)}) custom-call(bf16[10,6,16,128]{3,2,1,0:T(8,128)(2,1)S(1)} %get-tuple-element.24.refs_2_.refs_0_, bf16[9,128,1024]{2,1,0:T(8,128)(2,1)S(1)} %get-tuple-element.25.refs_1_, bf16[2,336,128]{2,1,0:T(8,128)(2,1)S(1)} %get-tuple-element.32.refs_2_), custom_call_target="tpu_custom_call" | custom-call | tf_op jit(solution)/shard_map/pallas_call | solution.py:329
  13.8 0.0 collective-permute-done.5
  13.8 2.3 %collective-permute-start.6 = (f32[32,128]{1,0:T(8,128)S(1)}, f32[32,128]{1,0:T(8,128)S(1)}, u32[]{:S(2)}, u32[]{:S(2)}) collective-permute-start(f32[32,128]{1,0:T(8,128)S(1)} %add_add_fusion.1), channel_id=1, source_target_pairs={{0,5},{1,4},{2,7},{3,6},{4,1},{5,0},{6,3},{7,2},{8,13},{9,12},{10,... | collective-permute-start | bytes 49160 | tf_op jit(solution)/shard_map/ppermute | solution.py:341
  16.2 1.4 %collective-permute-start.4 = (bf16[336,128]{1,0:T(8,128)(2,1)S(1)}, bf16[336,128]{1,0:T(8,128)(2,1)S(1)}, u32[]{:S(2)}, u32[]{:S(2)}) collective-permute-start(bf16[336,128]{1,0:T(8,128)(2,1)S(1)} %get-tuple-element.34), channel_id=1, source_target_pairs={{1,2},{3,4},{5,6},{7,0},{2,1},{4,3},{6,5},{0,7},{9,10},{11,12},{13... | collective-permute-start | bytes 258056 | tf_op jit(solution)/shard_map/ppermute | solution.py:433
  17.5 0.0 collective-permute-done.3.refs_3_
  17.5 1.9 %shard_map.81 = (f32[512,64]{1,0:T(8,128)S(1)}, f32[8,16,128]{2,1,0:T(8,128)S(1)}, f32[32,128]{1,0:T(8,128)S(1)}) custom-call(bf16[10,6,16,128]{3,2,1,0:T(8,128)(2,1)S(1)} %get-tuple-element.24.refs_2_.refs_0_, bf16[9,128,1024]{2,1,0:T(8,128)(2,1)S(1)} %get-tuple-element.25.refs_1_, bf16[2,336,128]{2,1,0:T(8,128)(2,1)S(1)} %get-tuple-element.32.refs_2_, ...), custom_call_target="tpu_custom_call" | custom-call | tf_op jit(solution)/shard_map/pallas_call | solution.py:329
  19.5 0.0 collective-permute-done.6
  19.5 1.1 %collective-permute-start.9 = (f32[32,128]{1,0:T(8,128)S(1)}, f32[32,128]{1,0:T(8,128)S(1)}, u32[]{:S(2)}, u32[]{:S(2)}) collective-permute-start(f32[32,128]{1,0:T(8,128)S(1)} %add_add_fusion.refs_0_), channel_id=1, source_target_pairs={{0,19},{1,18},{2,17},{3,16},{4,23},{5,22},{6,21},{7,20},{8,27},{9,... | collective-permute-start | bytes 49160 | tf_op jit(solution)/shard_map/ppermute | solution.py:355
  20.6 0.8 %collective-permute-start.8 = (f32[32,128]{1,0:T(8,128)S(1)}, f32[32,128]{1,0:T(8,128)S(1)}, u32[]{:S(2)}, u32[]{:S(2)}) collective-permute-start(f32[32,128]{1,0:T(8,128)S(1)} %add_add_fusion.refs_0_), channel_id=1, source_target_pairs={{0,17},{1,16},{2,19},{3,18},{4,21},{5,20},{6,23},{7,22},{8,25},{9,... | collective-permute-start | bytes 49160 | tf_op jit(solution)/shard_map/ppermute | solution.py:355
  21.4 1.3 %collective-permute-start.7 = (f32[32,128]{1,0:T(8,128)S(1)}, f32[32,128]{1,0:T(8,128)S(1)}, u32[]{:S(2)}, u32[]{:S(2)}) collective-permute-start(f32[32,128]{1,0:T(8,128)S(1)} %add_add_fusion.refs_0_), channel_id=1, source_target_pairs={{0,3},{1,2},{2,1},{3,0},{4,7},{5,6},{6,5},{7,4},{8,11},{9,10},{10,... | collective-permute-start | bytes 49160 | tf_op jit(solution)/shard_map/ppermute | solution.py:341
  22.7 0.0 collective-permute-done.4.refs_4_
  22.7 1.9 %shard_map.82 = (f32[512,64]{1,0:T(8,128)S(1)}, f32[8,16,128]{2,1,0:T(8,128)S(1)}) custom-call(bf16[10,6,16,128]{3,2,1,0:T(8,128)(2,1)S(1)} %get-tuple-element.24.refs_2_.refs_0_, bf16[9,128,1024]{2,1,0:T(8,128)(2,1)S(1)} %get-tuple-element.25.refs_1_, bf16[2,336,128]{2,1,0:T(8,128)(2,1)S(1)} %get-tuple-element.32.refs_2_, ...), custom_call_target="tpu_custom_call" | custom-call | tf_op jit(solution)/shard_map/pallas_call | solution.py:329
  24.6 0.0 collective-permute-done.9.refs_3_
  24.7 0.0 collective-permute-done.8.refs_2_
  24.7 0.0 collective-permute-done.7.refs_1_
  24.7 1.0 %shard_map.83 = (f32[8,64,64]{2,1,0:T(8,128)}, f32[64,64]{1,0:T(8,128)}) custom-call(f32[512,64]{1,0:T(8,128)S(1)} %get-tuple-element.39.sums_ref, f32[8,16,128]{2,1,0:T(8,128)S(1)} %get-tuple-element.40.weight_sums_ref, f32[32,128]{1,0:T(8,128)S(1)} %add_add_fusion.refs_0_, f32[32,128]{1,0:T(8,128)S(1)} %collective-permute-done.7.refs_1_, ...), custom_call_target="tpu_custom_call" | custom-call | tf_op jit(solution)/shard_map/pallas_call | solution.py:329
  (2 shorter events, 0.0 us)
Async XLA Ops:
  1.6 10.3 %collective-permute-start = (f32[16,1920]{1,0:T(8,128)S(1)}, f32[16,1920]{1,0:T(8,128)S(1)}, u32[]{:S(2)}, u32[]{:S(2)}) collective-permute-start(f32[16,1920]{1,0:T(8,128)S(1)} %get-tuple-element.29), channel_id=1, source_target_pairs={{0,8},{8,0},{16,24},{24,16},{1,9},{9,1},{17,25},{25,17},{2,10},{10... | collective-permute-start | bytes 368648 | tf_op jit(solution)/shard_map/ppermute | solution.py:341
  4.6 6.4 %collective-permute-start.1 = (f32[16,1792]{1,0:T(8,128)S(1)}, f32[16,1792]{1,0:T(8,128)S(1)}, u32[]{:S(2)}, u32[]{:S(2)}) collective-permute-start(f32[16,1792]{1,0:T(8,128)S(1)} %get-tuple-element.30), channel_id=1, source_target_pairs={{0,16},{8,24},{16,0},{24,8},{1,17},{9,25},{17,1},{25,9},{2,18},{10... | collective-permute-start | bytes 344072 | tf_op jit(solution)/shard_map/ppermute | solution.py:341
  6.1 5.7 %collective-permute-start.2 = (f32[16,1792]{1,0:T(8,128)S(1)}, f32[16,1792]{1,0:T(8,128)S(1)}, u32[]{:S(2)}, u32[]{:S(2)}) collective-permute-start(f32[16,1792]{1,0:T(8,128)S(1)} %get-tuple-element.31), channel_id=1, source_target_pairs={{0,24},{8,16},{16,8},{24,0},{1,25},{9,17},{17,9},{25,1},{2,26},{10... | collective-permute-start | bytes 344072 | tf_op jit(solution)/shard_map/ppermute | solution.py:341
  12.5 1.2 %collective-permute-start.5 = (f32[32,128]{1,0:T(8,128)S(1)}, f32[32,128]{1,0:T(8,128)S(1)}, u32[]{:S(2)}, u32[]{:S(2)}) collective-permute-start(f32[32,128]{1,0:T(8,128)S(1)} %get-tuple-element.41), channel_id=1, source_target_pairs={{0,1},{1,0},{2,3},{3,2},{4,5},{5,4},{6,7},{7,6},{8,9},{9,8},{10,11... | collective-permute-start | bytes 49160 | tf_op jit(solution)/shard_map/ppermute | solution.py:341
  12.6 4.9 %collective-permute-start.3 = (bf16[336,128]{1,0:T(8,128)(2,1)S(1)}, bf16[336,128]{1,0:T(8,128)(2,1)S(1)}, u32[]{:S(2)}, u32[]{:S(2)}) collective-permute-start(bf16[336,128]{1,0:T(8,128)(2,1)S(1)} %get-tuple-element.33), channel_id=1, source_target_pairs={{0,1},{1,0},{2,3},{3,2},{4,5},{5,4},{6,7},{7,6},{8,9},{9,8},{10,11... | collective-permute-start | bytes 258056 | tf_op jit(solution)/shard_map/ppermute | solution.py:341
  13.8 5.7 %collective-permute-start.6 = (f32[32,128]{1,0:T(8,128)S(1)}, f32[32,128]{1,0:T(8,128)S(1)}, u32[]{:S(2)}, u32[]{:S(2)}) collective-permute-start(f32[32,128]{1,0:T(8,128)S(1)} %add_add_fusion.1), channel_id=1, source_target_pairs={{0,5},{1,4},{2,7},{3,6},{4,1},{5,0},{6,3},{7,2},{8,13},{9,12},{10,... | collective-permute-start | bytes 49160 | tf_op jit(solution)/shard_map/ppermute | solution.py:341
  16.2 6.5 %collective-permute-start.4 = (bf16[336,128]{1,0:T(8,128)(2,1)S(1)}, bf16[336,128]{1,0:T(8,128)(2,1)S(1)}, u32[]{:S(2)}, u32[]{:S(2)}) collective-permute-start(bf16[336,128]{1,0:T(8,128)(2,1)S(1)} %get-tuple-element.34), channel_id=1, source_target_pairs={{1,2},{3,4},{5,6},{7,0},{2,1},{4,3},{6,5},{0,7},{9,10},{11,12},{13... | collective-permute-start | bytes 258056 | tf_op jit(solution)/shard_map/ppermute | solution.py:433
  19.5 5.1 %collective-permute-start.9 = (f32[32,128]{1,0:T(8,128)S(1)}, f32[32,128]{1,0:T(8,128)S(1)}, u32[]{:S(2)}, u32[]{:S(2)}) collective-permute-start(f32[32,128]{1,0:T(8,128)S(1)} %add_add_fusion.refs_0_), channel_id=1, source_target_pairs={{0,19},{1,18},{2,17},{3,16},{4,23},{5,22},{6,21},{7,20},{8,27},{9,... | collective-permute-start | bytes 49160 | tf_op jit(solution)/shard_map/ppermute | solution.py:355
  20.6 4.0 %collective-permute-start.8 = (f32[32,128]{1,0:T(8,128)S(1)}, f32[32,128]{1,0:T(8,128)S(1)}, u32[]{:S(2)}, u32[]{:S(2)}) collective-permute-start(f32[32,128]{1,0:T(8,128)S(1)} %add_add_fusion.refs_0_), channel_id=1, source_target_pairs={{0,17},{1,16},{2,19},{3,18},{4,21},{5,20},{6,23},{7,22},{8,25},{9,... | collective-permute-start | bytes 49160 | tf_op jit(solution)/shard_map/ppermute | solution.py:355
  21.4 3.2 %collective-permute-start.7 = (f32[32,128]{1,0:T(8,128)S(1)}, f32[32,128]{1,0:T(8,128)S(1)}, u32[]{:S(2)}, u32[]{:S(2)}) collective-permute-start(f32[32,128]{1,0:T(8,128)S(1)} %add_add_fusion.refs_0_), channel_id=1, source_target_pairs={{0,3},{1,2},{2,1},{3,0},{4,7},{5,6},{6,5},{7,4},{8,11},{9,10},{10,... | collective-permute-start | bytes 49160 | tf_op jit(solution)/shard_map/ppermute | solution.py:341
